TPU v7x, 512 devices: a whole 4x4x16 slice. The times are simulated.
512 devices in a mesh: cuts: 64 (over x, z_lo, core), ang: 8 (over y, z_hi).
Axes of the slice: x: 4, y: 4, z: 16 (z_hi: 2, z_lo: 8; z = z_hi * 8 + z_lo), core: 2. Of those that a mesh axis runs over, the one named last changes fastest.
Arguments:
- projections: bfloat16 [64, 64, 8, 32, 256], P('cuts', None, 'ang'), may hold values from -48 to 48
- start_image: bfloat16 [16384, 1024], P('cuts'), may hold values from 0 to 2
- system: bfloat16 [32, 16, 2, 64, 128], P('ang'), may hold values from 0.0009994507 to 0.029907227
- first_tile: int32 [32, 16], P('ang'), may hold values from 0 to 3, as said below
Outputs:
- new_image: float32 [16384, 1024], P('cuts', 'ang')
- residual: bfloat16 [64, 16384, 256], P('ang', 'cuts')
Inputs may be any that keep to these rules, and one draw needn't show every extreme that they name: In every angle block each bin tile is first_tile of at least one pixel tile; every pixel tile meets exactly two bin tiles, first_tile and first_tile + 1 modulo 4.
All inputs are finite; a program needn't handle non-finite values.
Results may differ from a plain program's by a relative error of at most 0.001.
Values may be sent and summed in bfloat16 or wider, within the bound.
No kernel may reach another device: no remote copies, remote signals or barrier semaphores. Data moves between devices by JAX's collectives and lax.ppermute only.
A program may use at most 128 MiB of HBM per device.

v0:
```python
import jax
import jax.numpy as jnp
from jax import lax
from jax.sharding import PartitionSpec as P


def on_device(projections, start_image, system, first_tile):
    arrived = lax.all_to_all(
        lax.all_to_all(projections, "cuts", split_axis=1, concat_axis=0, tiled=True),
        "ang",
        split_axis=0,
        concat_axis=2,
        tiled=True,
    )
    blocks = system.shape[0]
    pix_tiles = system.shape[1]
    tile_len = system.shape[3]
    pair_len = system.shape[4] // tile_len
    bin_tiles = arrived.shape[-1] // tile_len
    slices = start_image.shape[0]
    npixels = pix_tiles * tile_len
    highest = lax.Precision.HIGHEST
    tile_ids = jnp.arange(bin_tiles, dtype=jnp.int32)
    bin_index = jnp.stack([first_tile, (first_tile + 1) % bin_tiles], axis=2)
    onehot = (bin_index[..., None] == tile_ids).astype(jnp.float32)
    pixels = start_image.reshape(slices, pix_tiles, tile_len)
    partial_value = jnp.einsum(
        "spi,gpjic->gpjsc", pixels, system, preferred_element_type=jnp.float32
    )
    forward = jnp.einsum(
        "gpjb,gpjsc->gbsc",
        onehot,
        partial_value,
        precision=highest,
        preferred_element_type=jnp.float32,
    )
    ray_weights = jnp.sum(system, axis=3, dtype=jnp.float32)
    row_total = jnp.einsum(
        "gpjb,gpjc->gbc", onehot, ray_weights, precision=highest, preferred_element_type=jnp.float32
    )
    col_part = jnp.sum(system, axis=(0, 2, 4), dtype=jnp.float32).reshape(npixels)
    sinogram = arrived.reshape(blocks, pair_len, slices, bin_tiles, tile_len)
    sinogram = sinogram.transpose(0, 3, 2, 1, 4).reshape(
        blocks, bin_tiles, slices, pair_len * tile_len
    )
    resid_tiles = ((sinogram.astype(jnp.float32) - forward) / row_total[:, :, None, :]).astype(
        jnp.bfloat16
    )
    picked = jnp.einsum(
        "gpjb,gbsc->gpjsc",
        onehot.astype(jnp.bfloat16),
        resid_tiles,
        preferred_element_type=jnp.float32,
    ).astype(jnp.bfloat16)
    backproj = jnp.einsum(
        "gpjsc,gpjic->spi", picked, system, preferred_element_type=jnp.float32
    ).reshape(slices, npixels)
    share_len = npixels // lax.axis_size("ang")
    offset = lax.axis_index("ang") * share_len
    summed, columns = lax.psum((backproj, col_part), "ang")
    summed = lax.dynamic_slice_in_dim(summed, offset, share_len, 1)
    columns = lax.dynamic_slice_in_dim(columns, offset, share_len, 0)
    local_image = lax.dynamic_slice_in_dim(start_image, offset, share_len, 1).astype(jnp.float32)
    new_image = local_image + summed / columns[None, :]
    residual = resid_tiles.reshape(blocks, bin_tiles, slices, pair_len, tile_len)
    residual = residual.transpose(0, 3, 2, 1, 4).reshape(
        blocks * pair_len, slices, bin_tiles * tile_len
    )
    return (new_image, residual)


def solution(mesh):
    in_specs = (
        P("cuts", None, "ang", None, None),
        P("cuts", None),
        P("ang", None, None, None, None),
        P("ang", None),
    )
    out_specs = (P("cuts", "ang"), P("ang", "cuts", None))
    return jax.shard_map(
        on_device, mesh=mesh, in_specs=in_specs, out_specs=out_specs, check_vma=False
    )
```

profile of v0, /device:TPU:1, one launch (start us, length us, event | category | flops | bytes accessed | tf_op | source)
XLA Modules:
  0.0 399.6 jit_solution(7453883128527357558)
XLA Ops:
  7.2 0.0 copy-start.2
  7.2 68.5 %all_to_all.24 = bf16[1,64,1,32,256]{4,3,2,0,1:T(8,128)(2,1)} all-to-all(bf16[1,64,1,32,256]{4,3,2,0,1:T(8,128)(2,1)} %bitcast.69), channel_id=1, replica_groups=mesh['cuts'=64,'ang'=8] {'cuts'}, dimensions={1} | all-to-all | bytes 2097152 | tf_op jit(solution)/shard_map/all_to_all | solution.py:9
  75.7 0.0 copy-start
  75.7 10.1 %all-to-all-start.1 = ((bf16[64,1,1,32,256]{4,3,2,1,0:T(8,128)(2,1)}), bf16[64,1,1,32,256]{4,3,2,1,0:T(8,128)(2,1)S(1)}, u32[]{:S(2)}, u32[]{:S(2)}) async-start(bf16[64,1,1,32,256]{4,3,2,1,0:T(8,128)(2,1)} %bitcast.65), calls=%async_computation.1 | async-start | bytes 2097152 | tf_op jit(solution)/shard_map/all_to_all | solution.py:8
  85.7 0.0 all-reduce.2.cloned.1.call-start
  85.8 0.0 copy-done.2
  85.8 2.0 copy.25
  87.9 0.0 copy-done
  87.9 9.1 %convolution_bitcast_fusion = f32[4,16,2,256,128]{3,4,2,0,1:T(8,128)} fusion(bf16[256,16,64,1,1]{0,2,4,3,1:T(8,128)(2,1)} %bitcast.68, bf16[4,16,2,64,128]{4,3,2,1,0:T(8,128)(2,1)S(1)} %copy-done), kind=kOutput, calls=%fused_computation | convolution fusion | flops 536870912 | bytes 19398656 | tf_op jit(solution)/shard_map/spi,gpjic->gpjsc/dot_general | solution.py:27
  97.0 20.2 %copy.27 = f32[4,16,2,256,128]{4,1,2,3,0:T(8,128)} copy(f32[4,16,2,256,128]{3,4,2,0,1:T(8,128)} %convolution_bitcast_fusion) | data formatting | bytes 33554432 | tf_op jit(solution)/shard_map/spi,gpjic->gpjsc/transpose | solution.py:27
  117.2 0.6 convert_reduce_fusion
  117.8 0.2 convolution_bitcast_fusion.1
  118.1 5.0 %all-to-all-done.1 = bf16[64,1,1,32,256]{4,3,2,1,0:T(8,128)(2,1)S(1)} async-done(((bf16[64,1,1,32,256]{4,3,2,1,0:T(8,128)(2,1)}), bf16[64,1,1,32,256]{4,3,2,1,0:T(8,128)(2,1)S(1)}, u32[]{:S(2)}, u32[]{:S(2)}) %all-to-all-start.1) | async-done | bytes 1048608 | tf_op jit(solution)/shard_map/all_to_all | solution.py:8
  123.0 0.2 copy_bitcast_fusion
  123.3 3.1 reshape.38
  126.3 4.8 %copy.24 = f32[4,4,256,2,64]{2,4,3,1,0:T(8,128)} copy(f32[4,4,256,2,64]{4,1,2,3,0:T(4,128)} %bitcast.62) | data formatting | bytes 4194304 | tf_op jit(solution)/shard_map/convert_element_type | solution.py:46
  131.1 2.0 copy.28
  133.1 9.9 %fusion.3 = bf16[4,4,256,128]{3,1,2,0:T(4,128)(2,1)S(1)} fusion(f32[4,4,256,128]{3,1,2,0:T(4,128)S(1)} %copy.28, f32[4,16,2,256,128]{4,1,2,3,0:T(8,128)} %copy.27, f32[4,4,128]{2,1,0:T(4,128)S(1)} %convolution_bitcast_fusion.1, s32[4,16,2]{1,2,0:T(2,128)S(1)} %copy.20), kind=kOutput, calls=%fused_computation.9 | convolution fusion | flops 202899968 | bytes 19931648 | tf_op jit(solution)/shard_map/gpjb,gpjsc->gbsc/dot_general | solution.py:30
  143.0 0.0 copy-start.1
  143.1 3.0 convolution_convert_fusion
  146.1 0.0 copy-done.1
  146.1 5.0 %fusion = f32[16,256,64,1,1]{1,2,4,3,0:T(8,128)S(1)} fusion(bf16[4,16,2,256,128]{4,1,3,2,0:T(8,128)(2,1)S(1)} %convolution_convert_fusion, bf16[4,16,2,64,128]{4,3,2,1,0:T(8,128)(2,1)S(1)} %copy-done.1), kind=kOutput, calls=%fused_computation.1 | convolution fusion | flops 536870912 | bytes 11534336 | tf_op jit(solution)/shard_map/gpjsc,gpjic->spi/dot_general | solution.py:55
  151.0 1.4 copy.31
  152.4 0.0 all-reduce.2.cloned.1.call-update
  152.4 0.1 reshape.34
  152.5 37.4 %psum.15 = f32[1024]{0:T(1024)S(1)} all-reduce(f32[1024]{0:T(1024)S(1)} %reshape.34), channel_id=1, replica_groups=mesh['cuts'=64,'ang'=8] {'ang'}, use_global_device_ids=true, to_apply=%region_3.4 | all-reduce | flops 1024 | bytes 8192 | tf_op jit(solution)/shard_map/psum | solution.py:60
  189.9 0.1 dynamic_slice.11
  190.0 0.6 copy.32
  190.5 0.1 copy.33
  190.6 1.3 copy.34
  191.9 199.3 %all-reduce.2.cloned.1.call-done = f32[256,1024]{1,0:T(8,128)} async-done(((f32[256,1024]{1,0:T(8,128)}), f32[256,1024]{1,0:T(8,128)}) %all-reduce.2.cloned.1.call-update) | async-done | bytes 1048592 | tf_op jit(solution)/shard_map/psum | solution.py:60
  391.2 1.6 divide_add_fusion
  (3 shorter events, 0.0 us)
Async XLA Ops:
  7.2 78.6 %copy-start.2 = (s32[4,16]{1,0:T(4,128)S(1)}, s32[4,16]{1,0:T(4,128)}, u32[]{:S(2)}) copy-start(s32[4,16]{1,0:T(4,128)} %param.7) | copy-start | bytes 772
  75.7 12.2 %copy-start = (bf16[4,16,2,64,128]{4,3,2,1,0:T(8,128)(2,1)S(1)}, bf16[4,16,2,64,128]{4,3,2,1,0:T(8,128)(2,1)}, u32[]{:S(2)}) copy-start(bf16[4,16,2,64,128]{4,3,2,1,0:T(8,128)(2,1)} %param.6) | copy-start | bytes 6291460
  75.7 47.3 %all-to-all-start.1 = ((bf16[64,1,1,32,256]{4,3,2,1,0:T(8,128)(2,1)}), bf16[64,1,1,32,256]{4,3,2,1,0:T(8,128)(2,1)S(1)}, u32[]{:S(2)}, u32[]{:S(2)}) async-start(bf16[64,1,1,32,256]{4,3,2,1,0:T(8,128)(2,1)} %bitcast.65), calls=%async_computation.1 | async-start | bytes 2097152 | tf_op jit(solution)/shard_map/all_to_all | solution.py:8
  85.7 305.5 %all-reduce.2.cloned.1.call-start = ((), (), s32[]{:S(2)}) async-start(), calls=%async_computation.2 | async-start | bytes 2097152 | tf_op jit(solution)/shard_map/psum | solution.py:60
  143.0 3.0 copy-start.1
Sparse Core Ops, SparseCore 0:
  152.6 238.6 all-reduce.1
where the time goes:
time: 401 us; the launch traced here: 400 us
  waiting for transfers between devices  204 us (51%)
  blocking collectives  106 us (26%)
  local copies, waits for them, and re-layouts  35.6 us (9%)
  matrix products  27.2 us (7%)
  between operations  14.1 us (4%)
  starting transfers between devices  10.1 us (3%)
    psum x1, waiting for transfers between devices, on_device(): summed, columns = lax.psum((backproj, col_part), 'ang')  199 us
    all_to_all x1, blocking collectives, on_device(): lax.all_to_all(projections, 'cuts', split_axis=1, concat_axis=0, tiled=True)  68.5 us
    psum x1, blocking collectives, on_device(): summed, columns = lax.psum((backproj, col_part), 'ang')  37.4 us
    transpose x1, local copies, waits for them, and re-layouts, on_device(): jnp.einsum('spi,gpjic->gpjsc', pixels, system, preferred_element_type=jnp...  20.2 us
    all_to_all x1, starting transfers between devices, on_device(): lax.all_to_all(lax.all_to_all(projections, 'cuts', split_axis=1, concat_a...  10.1 us
    dot_general x1, matrix products, on_device(): jnp.einsum('gpjb,gpjsc->gbsc', onehot, partial_value, precision=highest,...  9.9 us
    convert_element_type x3, local copies, waits for them, and re-layouts, on_device(): sinogram.astype(jnp.float32) - forward  9.87 us
    dot_general x1, matrix products, on_device(): jnp.einsum('spi,gpjic->gpjsc', pixels, system, preferred_element_type=jnp...  9.13 us
  transfers between devices with their start and end apart: 2, of which 2 were waited for; matrix products, arithmetic and copies ran while one was open for 9% of the time, Pallas kernels for 0%

commit v1 on v0

v1 whole, which is shorter than its diff:
```python
import functools

import jax
import jax.numpy as jnp
from jax import lax
from jax.experimental import pallas as pl
from jax.experimental.pallas import tpu as pltpu
from jax.sharding import Mesh
from jax.sharding import PartitionSpec as P

AXES = ("x", "zl", "core", "y", "zh")
SIZES = (4, 8, 2, 4, 2)
F32 = jnp.float32
BF16 = jnp.bfloat16


def index_of(x, zl, core, y, zh):
    return (((x * 8 + zl) * 2 + core) * 4 + y) * 2 + zh


def pairs(dest):
    out = []
    for x in range(4):
        for zl in range(8):
            for core in range(2):
                for y in range(4):
                    for zh in range(2):
                        out.append((index_of(x, zl, core, y, zh), index_of(*dest(x, zl, core, y, zh))))
    return out


def contract(a, b, da, db):
    return lax.dot_general(a, b, (((da,), (db,)), ((), ())), preferred_element_type=F32)


def prepare_kernel(first_ref, image_ref, system_ref, a_ref, fwd_ref, rinv_ref, col_ref):
    g = pl.program_id(0)
    low = lax.broadcasted_iota(jnp.int32, (64, 128), 1) < 64
    for p in range(16):
        f = first_ref[g, p]
        t0 = system_ref[0, p, 0].astype(F32)
        t1 = system_ref[0, p, 1].astype(F32)
        even = f % 2 == 0
        e = jnp.where(even, t0, t1)
        o = jnp.where(even, t1, t0)
        x0 = jnp.where(low, e, pltpu.roll(o, 64, 1))
        x1 = jnp.where(low, pltpu.roll(e, 64, 1), o)
        ve = jnp.where((f == 1) | (f == 2), 1, 0)
        vo = jnp.where(f >= 2, 1, 0)
        place = jnp.where(low, ve, vo)
        for t, xt in ((0, x0), (1, x1)):
            for v in range(2):
                a_ref[0, p * 64 : (p + 1) * 64, t * 256 + v * 128 : t * 256 + (v + 1) * 128] = jnp.where(
                    place == v, xt, 0.0
                ).astype(BF16)
    a = a_ref[0]
    fwd_ref[0] = contract(image_ref[...], a, 1, 0)
    rows = contract(jnp.ones((8, 1024), BF16), a, 1, 0)
    rinv_ref[0] = 1.0 / rows
    cols = contract(jnp.ones((8, 512), BF16), a, 1, 1)

    @pl.when(g == 0)
    def _():
        col_ref[...] = cols

    @pl.when(g > 0)
    def _():
        col_ref[...] += cols


def prepare(first, image, system):
    return pl.pallas_call(
        prepare_kernel,
        grid=(4,),
        in_specs=[
            pl.BlockSpec(memory_space=pltpu.SMEM),
            pl.BlockSpec((256, 1024), lambda g: (0, 0)),
            pl.BlockSpec((1, 16, 2, 64, 128), lambda g: (g, 0, 0, 0, 0)),
        ],
        out_specs=[
            pl.BlockSpec((1, 1024, 512), lambda g: (g, 0, 0)),
            pl.BlockSpec((1, 256, 512), lambda g: (g, 0, 0)),
            pl.BlockSpec((1, 8, 512), lambda g: (g, 0, 0)),
            pl.BlockSpec((8, 1024), lambda g: (0, 0)),
        ],
        out_shape=[
            jax.ShapeDtypeStruct((4, 1024, 512), BF16),
            jax.ShapeDtypeStruct((4, 256, 512), F32),
            jax.ShapeDtypeStruct((4, 8, 512), F32),
            jax.ShapeDtypeStruct((8, 1024), F32),
        ],
        cost_estimate=pl.CostEstimate(flops=1100000000, bytes_accessed=10000000, transcendentals=0),
        compiler_params=pltpu.CompilerParams(vmem_limit_bytes=40 * 1024 * 1024),
        name="prepare",
    )(first, image, system)


def finish_kernel(where_ref, *refs):
    chunks, (a_ref, fwd_ref, rinv_ref, col_ref, res_ref, part_ref, held_ref) = refs[:8], refs[8:]
    dh, dl = where_ref[0], where_ref[1]
    for b in range(4):
        g = dl ^ b
        for a in range(2):
            zh = dh ^ a
            chunk = chunks[a * 4 + b]
            for t in range(2):
                rinv = rinv_ref[g, 0:1, t * 256 : (t + 1) * 256]
                for y in range(4):
                    rows = pl.ds(pl.multiple_of((y * 2 + zh) * 32, 32), 32)
                    lanes = slice(t * 256, (t + 1) * 256)
                    res = ((chunk[t * 4 + y].astype(F32) - fwd_ref[g, rows, lanes]) * rinv).astype(BF16)
                    res_ref[g * 2 + t, rows, :] = res
                    held_ref[rows, lanes] = res
        for q in range(4):
            add = contract(held_ref[...], a_ref[g, q * 256 : (q + 1) * 256, :], 1, 1)
            if b == 0:
                part_ref[q, 0:256, :] = add
            else:
                part_ref[q, 0:256, :] += add
    for q in range(4):
        part_ref[q, 256:264, :] = col_ref[:, q * 256 : (q + 1) * 256]


def finish(where, chunks, a, fwd, rinv, col):
    vmem = pl.BlockSpec(memory_space=pltpu.VMEM)
    return pl.pallas_call(
        finish_kernel,
        in_specs=[pl.BlockSpec(memory_space=pltpu.SMEM)] + [vmem] * 12,
        out_specs=[vmem, vmem],
        out_shape=[
            jax.ShapeDtypeStruct((8, 256, 256), BF16),
            jax.ShapeDtypeStruct((4, 264, 256), F32),
        ],
        scratch_shapes=[pltpu.VMEM((256, 512), BF16)],
        cost_estimate=pl.CostEstimate(flops=1100000000, bytes_accessed=10000000, transcendentals=0),
        compiler_params=pltpu.CompilerParams(vmem_limit_bytes=40 * 1024 * 1024),
        name="finish",
    )(where, *chunks, a, fwd, rinv, col)


def on_device(projections, start_image, system, first_tile):
    zl, y, zh = lax.axis_index("zl"), lax.axis_index("y"), lax.axis_index("zh")
    dh, dl = zl // 4, zl % 4
    sent = projections.reshape(4, 8, 2, 32, 256).transpose(2, 0, 1, 3, 4).reshape(8, 8, 32, 256)
    sent = lax.all_to_all(sent, ("core", "y"), 0, 0, tiled=True)
    chunks = []
    for k in range(8):

        def dest(x, zl, core, y, zh, k=k):
            return (y, (zh * 4 + zl % 4) ^ k, core, x, zl // 4)

        block = lax.dynamic_index_in_dim(sent, (zh * 4 + dl) ^ k, 1, keepdims=False)
        chunks.append(lax.ppermute(block, AXES, pairs(dest)))
    first_tile, image, system, _ = lax.optimization_barrier((first_tile, start_image, system, sent))
    a, fwd, rinv, col = prepare(first_tile, image, system)
    where = jnp.stack([dh, dl]).astype(jnp.int32)
    residual, part = finish(where, chunks, a, fwd, rinv, col)
    part = lax.all_to_all(part, "y", 0, 0, tiled=True).sum(0)
    halves = jnp.stack([part[:, :128], part[:, 128:]])
    mine = lax.dynamic_index_in_dim(halves, zh, 0, keepdims=False)
    other = lax.dynamic_index_in_dim(halves, 1 - zh, 0, keepdims=False)
    swap = pairs(lambda x, zl, core, y, zh: (x, zl, core, y, 1 - zh))
    total = mine + lax.ppermute(other, AXES, swap)
    local = lax.dynamic_slice_in_dim(start_image, (y * 2 + zh) * 128, 128, 1).astype(F32)
    new_image = local + total[:256] / total[256:257]
    return new_image, residual


def solution(mesh):
    mesh = Mesh(mesh.devices.reshape(SIZES), AXES)
    cuts, ang = ("x", "zl", "core"), ("y", "zh")
    in_specs = (
        P(cuts, None, ang, None, None),
        P(cuts, None),
        P(ang, None, None, None, None),
        P(ang, None),
    )
    out_specs = (P(cuts, ang), P(ang, cuts, None))
    return jax.shard_map(on_device, mesh=mesh, in_specs=in_specs, out_specs=out_specs, check_vma=False)
```

time: 401 us -> 170 us (0.42)
  the two profiles are of different devices: /device:TPU:1 before, /device:TPU:4 now
where the time goes in v1:
time: 170 us; the launch traced here: 169 us
  starting transfers between devices  85 us (50%)
  waiting for transfers between devices  70.3 us (41%)
  Pallas kernels  7.72 us (5%)
  local copies, waits for them, and re-layouts  4.45 us (3%)
    ppermute x8, starting transfers between devices, on_device(): chunks.append(lax.ppermute(block, AXES, pairs(dest)))  74.8 us
    ppermute x1, waiting for transfers between devices, on_device(): total = mine + lax.ppermute(other, AXES, swap)  22.4 us
    ppermute x8, waiting for transfers between devices, on_device(): chunks.append(lax.ppermute(block, AXES, pairs(dest)))  21.4 us
    all_to_all x1, waiting for transfers between devices, on_device(): sent = lax.all_to_all(sent, ('core', 'y'), 0, 0, tiled=True)  15.4 us
    all_to_all x1, waiting for transfers between devices, on_device(): part = lax.all_to_all(part, 'y', 0, 0, tiled=True).sum(0)  11 us
    pallas_call x1, Pallas kernels, prepare(): pl.pallas_call(prepare_kernel, grid=(4,), in_specs=[pl.BlockSpec(memory_s...  4.79 us
    all_to_all x1, starting transfers between devices, on_device(): sent = lax.all_to_all(sent, ('core', 'y'), 0, 0, tiled=True)  4.73 us
    all_to_all x1, starting transfers between devices, on_device(): part = lax.all_to_all(part, 'y', 0, 0, tiled=True).sum(0)  3.52 us
  transfers between devices with their start and end apart: 11, of which 4 were waited for; matrix products, arithmetic and copies ran while one was open for 0% of the time, Pallas kernels for 3%

profile of v1, /device:TPU:4, one launch (start us, length us, event | category | flops | bytes accessed | tf_op | source)
XLA Modules:
  0.0 169.2 jit_solution(16028711828667613527)
XLA Ops:
  0.6 2.3 %copy.7 = bf16[4,8,2,32,256]{4,3,1,0,2:T(8,128)(2,1)} copy(bf16[4,8,2,32,256]{4,3,2,1,0:T(8,128)(2,1)} %bitcast.35) | data formatting | bytes 2097152 | tf_op jit(solution)/shard_map/reshape | solution.py:144
  2.9 0.0 copy-start
  2.9 0.0 copy-start.1
  2.9 0.0 copy-start.2
  2.9 4.7 %all-to-all-start = ((bf16[8,8,32,256]{3,2,1,0:T(8,128)(2,1)}), bf16[8,8,32,256]{3,2,1,0:T(8,128)(2,1)}, u32[]{:S(2)}, u32[]{:S(2)}) async-start(bf16[8,8,32,256]{3,2,1,0:T(8,128)(2,1)} %bitcast.34), calls=%async_computation | async-start | bytes 2097152 | tf_op jit(solution)/shard_map/all_to_all | solution.py:145
  7.7 15.4 %all-to-all-done = bf16[8,8,32,256]{3,2,1,0:T(8,128)(2,1)} async-done(((bf16[8,8,32,256]{3,2,1,0:T(8,128)(2,1)}), bf16[8,8,32,256]{3,2,1,0:T(8,128)(2,1)}, u32[]{:S(2)}, u32[]{:S(2)}) %all-to-all-start) | async-done | bytes 1048608 | tf_op jit(solution)/shard_map/all_to_all | solution.py:145
  23.1 2.1 %dynamic-slice_bitcast_fusion = (bf16[8,32,256]{2,1,0:T(8,128)(2,1)S(1)}, bf16[8,32,256]{2,1,0:T(8,128)(2,1)S(1)}, bf16[8,32,256]{2,1,0:T(8,128)(2,1)S(1)}, bf16...) fusion(bf16[8,8,32,256]{3,2,1,0:T(8,128)(2,1)} %all-to-all-done, ...), kind=kLoop, calls=%fused_computation.13 | loop fusion | bytes 2097184 | tf_op jit(solution)/shard_map/jit(dynamic_index_in_dim)/squeeze | solution.py:152
  25.2 7.9 %collective-permute-start = (bf16[8,32,256]{2,1,0:T(8,128)(2,1)}, bf16[8,32,256]{2,1,0:T(8,128)(2,1)S(1)}, u32[]{:S(2)}, u32[]{:S(2)}) collective-permute-start(bf16[8,32,256]{2,1,0:T(8,128)(2,1)} %get-tuple-element.27), channel_id=1, source_target_pairs={{0,0},{1,64},{2,128},{3,192},{4,256},{5,320},{6,384},{7,448},{8,8}... | collective-permute-start | bytes 393224 | tf_op jit(solution)/shard_map/ppermute | solution.py:153
  33.1 3.2 %collective-permute-start.1 = (bf16[8,32,256]{2,1,0:T(8,128)(2,1)}, bf16[8,32,256]{2,1,0:T(8,128)(2,1)S(1)}, u32[]{:S(2)}, u32[]{:S(2)}) collective-permute-start(bf16[8,32,256]{2,1,0:T(8,128)(2,1)} %get-tuple-element.26), channel_id=1, source_target_pairs={{0,16},{1,80},{2,144},{3,208},{4,272},{5,336},{6,400},{7,464},{8,2... | collective-permute-start | bytes 393224 | tf_op jit(solution)/shard_map/ppermute | solution.py:153
  36.3 5.5 %collective-permute-start.2 = (bf16[8,32,256]{2,1,0:T(8,128)(2,1)}, bf16[8,32,256]{2,1,0:T(8,128)(2,1)S(1)}, u32[]{:S(2)}, u32[]{:S(2)}) collective-permute-start(bf16[8,32,256]{2,1,0:T(8,128)(2,1)} %get-tuple-element.25), channel_id=1, source_target_pairs={{0,32},{1,96},{2,160},{3,224},{4,288},{5,352},{6,416},{7,480},{8,4... | collective-permute-start | bytes 393224 | tf_op jit(solution)/shard_map/ppermute | solution.py:153
  41.9 5.6 %collective-permute-start.3 = (bf16[8,32,256]{2,1,0:T(8,128)(2,1)}, bf16[8,32,256]{2,1,0:T(8,128)(2,1)S(1)}, u32[]{:S(2)}, u32[]{:S(2)}) collective-permute-start(bf16[8,32,256]{2,1,0:T(8,128)(2,1)} %get-tuple-element.24), channel_id=1, source_target_pairs={{0,48},{1,112},{2,176},{3,240},{4,304},{5,368},{6,432},{7,496},{8,... | collective-permute-start | bytes 393224 | tf_op jit(solution)/shard_map/ppermute | solution.py:153
  47.5 19.5 %collective-permute-start.4 = (bf16[8,32,256]{2,1,0:T(8,128)(2,1)S(1)}, bf16[8,32,256]{2,1,0:T(8,128)(2,1)S(1)}, u32[]{:S(2)}, u32[]{:S(2)}) collective-permute-start(bf16[8,32,256]{2,1,0:T(8,128)(2,1)S(1)} %get-tuple-element.23), channel_id=1, source_target_pairs={{0,64},{1,0},{2,192},{3,128},{4,320},{5,256},{6,448},{7,384},{8,72... | collective-permute-start | bytes 393224 | tf_op jit(solution)/shard_map/ppermute | solution.py:153
  67.0 0.0 collective-permute-done.refs_0_
  67.0 4.8 %collective-permute-start.5 = (bf16[8,32,256]{2,1,0:T(8,128)(2,1)S(1)}, bf16[8,32,256]{2,1,0:T(8,128)(2,1)S(1)}, u32[]{:S(2)}, u32[]{:S(2)}) collective-permute-start(bf16[8,32,256]{2,1,0:T(8,128)(2,1)S(1)} %get-tuple-element.22), channel_id=1, source_target_pairs={{0,80},{1,16},{2,208},{3,144},{4,336},{5,272},{6,464},{7,400},{8,8... | collective-permute-start | bytes 393224 | tf_op jit(solution)/shard_map/ppermute | solution.py:153
  71.9 0.0 collective-permute-done.1.refs_1_
  71.9 15.4 %collective-permute-start.6 = (bf16[8,32,256]{2,1,0:T(8,128)(2,1)S(1)}, bf16[8,32,256]{2,1,0:T(8,128)(2,1)S(1)}, u32[]{:S(2)}, u32[]{:S(2)}) collective-permute-start(bf16[8,32,256]{2,1,0:T(8,128)(2,1)S(1)} %get-tuple-element.21), channel_id=1, source_target_pairs={{0,96},{1,32},{2,224},{3,160},{4,352},{5,288},{6,480},{7,416},{8,1... | collective-permute-start | bytes 393224 | tf_op jit(solution)/shard_map/ppermute | solution.py:153
  87.3 0.0 collective-permute-done.2.refs_2_
  87.3 12.8 %collective-permute-start.7 = (bf16[8,32,256]{2,1,0:T(8,128)(2,1)S(1)}, bf16[8,32,256]{2,1,0:T(8,128)(2,1)S(1)}, u32[]{:S(2)}, u32[]{:S(2)}) collective-permute-start(bf16[8,32,256]{2,1,0:T(8,128)(2,1)S(1)} %get-tuple-element.20), channel_id=1, source_target_pairs={{0,112},{1,48},{2,240},{3,176},{4,368},{5,304},{6,496},{7,432},{8,... | collective-permute-start | bytes 393224 | tf_op jit(solution)/shard_map/ppermute | solution.py:153
  100.1 0.1 pad_add_fusion.where_ref
  100.2 0.0 copy-done
  100.2 0.0 copy-done.1
  100.2 0.0 copy-done.2
  100.2 4.8 %prepare.1 = (bf16[4,1024,512]{2,1,0:T(8,128)(2,1)S(1)}, f32[4,256,512]{2,1,0:T(8,128)S(1)}, f32[4,8,512]{2,1,0:T(8,128)S(1)}, f32[8,1024]{1,0:T(8,128)S(1)}) custom-call(s32[4,16]{1,0:T(4,128)S(1)} %copy-done.2, bf16[256,1024]{1,0:T(8,128)(2,1)S(1)} %copy-done, bf16[4,16,2,64,128]{4,3,2,1,0:T(8,128)(2,1)S(1)} %copy-done.1), custom_call_target="tpu_custom_call" | custom-call | flops 1100000000 | bytes 10000000 | tf_op jit(solution)/shard_map/prepare/pallas_call | solution.py:72
  105.0 0.0 collective-permute-done.3.refs_3_
  105.1 0.0 collective-permute-done.4.refs_4_
  105.1 0.0 collective-permute-done.5.refs_5_
  105.1 0.0 collective-permute-done.6.refs_6_
  105.1 21.4 %collective-permute-done.7.refs_7_ = bf16[8,32,256]{2,1,0:T(8,128)(2,1)S(1)} collective-permute-done((bf16[8,32,256]{2,1,0:T(8,128)(2,1)S(1)}, bf16[8,32,256]{2,1,0:T(8,128)(2,1)S(1)}, u32[]{:S(2)}, u32[]{:S(2)}) %collective-permute-start.7) | collective-permute-done | bytes 131104 | tf_op jit(solution)/shard_map/ppermute | solution.py:153
  126.5 2.9 %finish.1 = (bf16[8,256,256]{2,1,0:T(8,128)(2,1)}, f32[4,264,256]{2,1,0:T(8,128)}) custom-call(s32[2]{0:T(128)S(1)} %pad_add_fusion.where_ref, bf16[8,32,256]{2,1,0:T(8,128)(2,1)S(1)} %collective-permute-done.refs_0_, bf16[8,32,256]{2,1,0:T(8,128)(2,1)S(1)} %collective-permute-done.1.refs_1_, bf16[8,32,256]{2,1,0:T(8,128)(2,1)S(1)} %collective-permute-done.2.refs_2_, ...), custom_call_target="tpu_custom_call" | custom-call | flops 1100000000 | bytes 10000000 | tf_op jit(solution)/shard_map/finish/pallas_call | solution.py:126
  129.4 3.5 %all-to-all-start.1 = ((f32[4,264,256]{2,1,0:T(8,128)}), f32[4,264,256]{2,1,0:T(8,128)S(1)}, u32[]{:S(2)}, u32[]{:S(2)}) async-start(f32[4,264,256]{2,1,0:T(8,128)} %get-tuple-element.18), calls=%async_computation.1 | async-start | bytes 2162688 | tf_op jit(solution)/shard_map/all_to_all | solution.py:158
  132.9 11.0 %all-to-all-done.1 = f32[4,264,256]{2,1,0:T(8,128)S(1)} async-done(((f32[4,264,256]{2,1,0:T(8,128)}), f32[4,264,256]{2,1,0:T(8,128)S(1)}, u32[]{:S(2)}, u32[]{:S(2)}) %all-to-all-start.1) | async-done | bytes 1081376 | tf_op jit(solution)/shard_map/all_to_all | solution.py:158
  144.0 0.1 reduce_sum.9
  144.1 1.9 %collective-permute-start.8 = (f32[264,128]{1,0:T(8,128)S(1)}, f32[264,128]{1,0:T(8,128)S(1)}, u32[]{:S(2)}, u32[]{:S(2)}) collective-permute-start(f32[264,128]{1,0:T(8,128)S(1)} %fusion.1), channel_id=1, source_target_pairs={{0,1},{1,0},{2,3},{3,2},{4,5},{5,4},{6,7},{7,6},{8,9},{9,8},{10,11... | collective-permute-start | bytes 405512 | tf_op jit(solution)/shard_map/ppermute | solution.py:163
  146.1 22.4 %collective-permute-done.8 = f32[264,128]{1,0:T(8,128)S(1)} collective-permute-done((f32[264,128]{1,0:T(8,128)S(1)}, f32[264,128]{1,0:T(8,128)S(1)}, u32[]{:S(2)}, u32[]{:S(2)}) %collective-permute-start.8) | collective-permute-done | bytes 135200 | tf_op jit(solution)/shard_map/ppermute | solution.py:163
  168.5 0.7 fusion.5
  (4 shorter events, 0.1 us)
Async XLA Ops:
  2.9 97.3 %copy-start = (bf16[256,1024]{1,0:T(8,128)(2,1)S(1)}, bf16[256,1024]{1,0:T(8,128)(2,1)}, u32[]{:S(2)}) copy-start(bf16[256,1024]{1,0:T(8,128)(2,1)} %image_ref) | copy-start | bytes 1572868
  2.9 97.3 %copy-start.1 = (bf16[4,16,2,64,128]{4,3,2,1,0:T(8,128)(2,1)S(1)}, bf16[4,16,2,64,128]{4,3,2,1,0:T(8,128)(2,1)}, u32[]{:S(2)}) copy-start(bf16[4,16,2,64,128]{4,3,2,1,0:T(8,128)(2,1)} %system_ref) | copy-start | bytes 6291460
  2.9 97.3 %copy-start.2 = (s32[4,16]{1,0:T(4,128)S(1)}, s32[4,16]{1,0:T(4,128)}, u32[]{:S(2)}) copy-start(s32[4,16]{1,0:T(4,128)} %first_ref) | copy-start | bytes 772
  2.9 20.2 %all-to-all-start = ((bf16[8,8,32,256]{3,2,1,0:T(8,128)(2,1)}), bf16[8,8,32,256]{3,2,1,0:T(8,128)(2,1)}, u32[]{:S(2)}, u32[]{:S(2)}) async-start(bf16[8,8,32,256]{3,2,1,0:T(8,128)(2,1)} %bitcast.34), calls=%async_computation | async-start | bytes 2097152 | tf_op jit(solution)/shard_map/all_to_all | solution.py:145
  25.2 41.8 %collective-permute-start = (bf16[8,32,256]{2,1,0:T(8,128)(2,1)}, bf16[8,32,256]{2,1,0:T(8,128)(2,1)S(1)}, u32[]{:S(2)}, u32[]{:S(2)}) collective-permute-start(bf16[8,32,256]{2,1,0:T(8,128)(2,1)} %get-tuple-element.27), channel_id=1, source_target_pairs={{0,0},{1,64},{2,128},{3,192},{4,256},{5,320},{6,384},{7,448},{8,8}... | collective-permute-start | bytes 393224 | tf_op jit(solution)/shard_map/ppermute | solution.py:153
  33.1 38.8 %collective-permute-start.1 = (bf16[8,32,256]{2,1,0:T(8,128)(2,1)}, bf16[8,32,256]{2,1,0:T(8,128)(2,1)S(1)}, u32[]{:S(2)}, u32[]{:S(2)}) collective-permute-start(bf16[8,32,256]{2,1,0:T(8,128)(2,1)} %get-tuple-element.26), channel_id=1, source_target_pairs={{0,16},{1,80},{2,144},{3,208},{4,272},{5,336},{6,400},{7,464},{8,2... | collective-permute-start | bytes 393224 | tf_op jit(solution)/shard_map/ppermute | solution.py:153
  36.3 51.0 %collective-permute-start.2 = (bf16[8,32,256]{2,1,0:T(8,128)(2,1)}, bf16[8,32,256]{2,1,0:T(8,128)(2,1)S(1)}, u32[]{:S(2)}, u32[]{:S(2)}) collective-permute-start(bf16[8,32,256]{2,1,0:T(8,128)(2,1)} %get-tuple-element.25), channel_id=1, source_target_pairs={{0,32},{1,96},{2,160},{3,224},{4,288},{5,352},{6,416},{7,480},{8,4... | collective-permute-start | bytes 393224 | tf_op jit(solution)/shard_map/ppermute | solution.py:153
  41.9 63.1 %collective-permute-start.3 = (bf16[8,32,256]{2,1,0:T(8,128)(2,1)}, bf16[8,32,256]{2,1,0:T(8,128)(2,1)S(1)}, u32[]{:S(2)}, u32[]{:S(2)}) collective-permute-start(bf16[8,32,256]{2,1,0:T(8,128)(2,1)} %get-tuple-element.24), channel_id=1, source_target_pairs={{0,48},{1,112},{2,176},{3,240},{4,304},{5,368},{6,432},{7,496},{8,... | collective-permute-start | bytes 393224 | tf_op jit(solution)/shard_map/ppermute | solution.py:153
  47.5 57.5 %collective-permute-start.4 = (bf16[8,32,256]{2,1,0:T(8,128)(2,1)S(1)}, bf16[8,32,256]{2,1,0:T(8,128)(2,1)S(1)}, u32[]{:S(2)}, u32[]{:S(2)}) collective-permute-start(bf16[8,32,256]{2,1,0:T(8,128)(2,1)S(1)} %get-tuple-element.23), channel_id=1, source_target_pairs={{0,64},{1,0},{2,192},{3,128},{4,320},{5,256},{6,448},{7,384},{8,72... | collective-permute-start | bytes 393224 | tf_op jit(solution)/shard_map/ppermute | solution.py:153
  67.0 38.0 %collective-permute-start.5 = (bf16[8,32,256]{2,1,0:T(8,128)(2,1)S(1)}, bf16[8,32,256]{2,1,0:T(8,128)(2,1)S(1)}, u32[]{:S(2)}, u32[]{:S(2)}) collective-permute-start(bf16[8,32,256]{2,1,0:T(8,128)(2,1)S(1)} %get-tuple-element.22), channel_id=1, source_target_pairs={{0,80},{1,16},{2,208},{3,144},{4,336},{5,272},{6,464},{7,400},{8,8... | collective-permute-start | bytes 393224 | tf_op jit(solution)/shard_map/ppermute | solution.py:153
  71.9 33.2 %collective-permute-start.6 = (bf16[8,32,256]{2,1,0:T(8,128)(2,1)S(1)}, bf16[8,32,256]{2,1,0:T(8,128)(2,1)S(1)}, u32[]{:S(2)}, u32[]{:S(2)}) collective-permute-start(bf16[8,32,256]{2,1,0:T(8,128)(2,1)S(1)} %get-tuple-element.21), channel_id=1, source_target_pairs={{0,96},{1,32},{2,224},{3,160},{4,352},{5,288},{6,480},{7,416},{8,1... | collective-permute-start | bytes 393224 | tf_op jit(solution)/shard_map/ppermute | solution.py:153
  87.3 39.1 %collective-permute-start.7 = (bf16[8,32,256]{2,1,0:T(8,128)(2,1)S(1)}, bf16[8,32,256]{2,1,0:T(8,128)(2,1)S(1)}, u32[]{:S(2)}, u32[]{:S(2)}) collective-permute-start(bf16[8,32,256]{2,1,0:T(8,128)(2,1)S(1)} %get-tuple-element.20), channel_id=1, source_target_pairs={{0,112},{1,48},{2,240},{3,176},{4,368},{5,304},{6,496},{7,432},{8,... | collective-permute-start | bytes 393224 | tf_op jit(solution)/shard_map/ppermute | solution.py:153
  129.4 14.6 %all-to-all-start.1 = ((f32[4,264,256]{2,1,0:T(8,128)}), f32[4,264,256]{2,1,0:T(8,128)S(1)}, u32[]{:S(2)}, u32[]{:S(2)}) async-start(f32[4,264,256]{2,1,0:T(8,128)} %get-tuple-element.18), calls=%async_computation.1 | async-start | bytes 2162688 | tf_op jit(solution)/shard_map/all_to_all | solution.py:158
  144.1 24.3 %collective-permute-start.8 = (f32[264,128]{1,0:T(8,128)S(1)}, f32[264,128]{1,0:T(8,128)S(1)}, u32[]{:S(2)}, u32[]{:S(2)}) collective-permute-start(f32[264,128]{1,0:T(8,128)S(1)} %fusion.1), channel_id=1, source_target_pairs={{0,1},{1,0},{2,3},{3,2},{4,5},{5,4},{6,7},{7,6},{8,9},{9,8},{10,11... | collective-permute-start | bytes 405512 | tf_op jit(solution)/shard_map/ppermute | solution.py:163

commit v2 on v1

--- a/solution.py
+++ b/solution.py
@@ -96,19 +96,19 @@
 
 
 def finish_kernel(where_ref, *refs):
-    chunks, (a_ref, fwd_ref, rinv_ref, col_ref, res_ref, part_ref, held_ref) = refs[:8], refs[8:]
-    dh, dl = where_ref[0], where_ref[1]
+    near_ref, far_refs, (a_ref, fwd_ref, rinv_ref, col_ref, res_ref, part_ref, held_ref) = refs[0], refs[1:5], refs[5:]
+    dh, dl, own_y = where_ref[0], where_ref[1], where_ref[2]
     for b in range(4):
         g = dl ^ b
         for a in range(2):
             zh = dh ^ a
-            chunk = chunks[a * 4 + b]
             for t in range(2):
                 rinv = rinv_ref[g, 0:1, t * 256 : (t + 1) * 256]
                 for y in range(4):
                     rows = pl.ds(pl.multiple_of((y * 2 + zh) * 32, 32), 32)
                     lanes = slice(t * 256, (t + 1) * 256)
-                    res = ((chunk[t * 4 + y].astype(F32) - fwd_ref[g, rows, lanes]) * rinv).astype(BF16)
+                    block = near_ref[(y ^ own_y) * 2 + t, b] if a == 0 else far_refs[b][t * 4 + y]
+                    res = ((block.astype(F32) - fwd_ref[g, rows, lanes]) * rinv).astype(BF16)
                     res_ref[g * 2 + t, rows, :] = res
                     held_ref[rows, lanes] = res
         for q in range(4):
@@ -121,11 +121,11 @@
         part_ref[q, 256:264, :] = col_ref[:, q * 256 : (q + 1) * 256]
 
 
-def finish(where, chunks, a, fwd, rinv, col):
+def finish(where, near, far, a, fwd, rinv, col):
     vmem = pl.BlockSpec(memory_space=pltpu.VMEM)
     return pl.pallas_call(
         finish_kernel,
-        in_specs=[pl.BlockSpec(memory_space=pltpu.SMEM)] + [vmem] * 12,
+        in_specs=[pl.BlockSpec(memory_space=pltpu.SMEM)] + [vmem] * 9,
         out_specs=[vmem, vmem],
         out_shape=[
             jax.ShapeDtypeStruct((8, 256, 256), BF16),
@@ -135,26 +135,37 @@
         cost_estimate=pl.CostEstimate(flops=1100000000, bytes_accessed=10000000, transcendentals=0),
         compiler_params=pltpu.CompilerParams(vmem_limit_bytes=40 * 1024 * 1024),
         name="finish",
-    )(where, *chunks, a, fwd, rinv, col)
+    )(where, near, *far, a, fwd, rinv, col)
 
 
 def on_device(projections, start_image, system, first_tile):
-    zl, y, zh = lax.axis_index("zl"), lax.axis_index("y"), lax.axis_index("zh")
+    x, zl, y, zh = (lax.axis_index(name) for name in ("x", "zl", "y", "zh"))
     dh, dl = zl // 4, zl % 4
-    sent = projections.reshape(4, 8, 2, 32, 256).transpose(2, 0, 1, 3, 4).reshape(8, 8, 32, 256)
-    sent = lax.all_to_all(sent, ("core", "y"), 0, 0, tiled=True)
-    chunks = []
-    for k in range(8):
+    mine = zh * 4 + dl
+    blocks = projections.reshape(4, 2, 4, 2, 32, 256)
 
-        def dest(x, zl, core, y, zh, k=k):
-            return (y, (zh * 4 + zl % 4) ^ k, core, x, zl // 4)
+    def send(block, k):
+        def dest(x, zl, core, y, zh):
+            return (x ^ y, (zh * 4 + zl % 4) ^ k, core, x, zl // 4)
 
-        block = lax.dynamic_index_in_dim(sent, (zh * 4 + dl) ^ k, 1, keepdims=False)
-        chunks.append(lax.ppermute(block, AXES, pairs(dest)))
-    first_tile, image, system, _ = lax.optimization_barrier((first_tile, start_image, system, sent))
+        return lax.ppermute(block, AXES, pairs(dest))
+
+    near = lax.dynamic_index_in_dim(blocks, zh, 1, keepdims=False)
+    near = [lax.dynamic_index_in_dim(near, dl ^ b, 1, keepdims=False) for b in range(4)]
+    first_tile, image, system, near = lax.optimization_barrier((first_tile, start_image, system, near))
+    far = lax.dynamic_index_in_dim(blocks, 1 - zh, 1, keepdims=False)
+    far = jnp.stack([lax.dynamic_index_in_dim(far, x ^ m, 0, keepdims=False) for m in range(4)])
+    far = far.transpose(2, 0, 1, 3, 4).reshape(8, 4, 32, 256)
+    near = [send(block.reshape(8, 32, 256), b) for b, block in enumerate(near)]
+    far = lax.all_to_all(far, ("core", "y"), 0, 0, tiled=True)
+    near, _ = lax.optimization_barrier((near, far))
+    far = [lax.dynamic_index_in_dim(far, dl ^ b, 1, keepdims=False) for b in range(4)]
+    near = jnp.stack(near, 1)
+    far = [send(block, 4 + b) for b, block in enumerate(far)]
+    near = lax.all_to_all(near, ("x", "core"), 0, 0, tiled=True)
     a, fwd, rinv, col = prepare(first_tile, image, system)
-    where = jnp.stack([dh, dl]).astype(jnp.int32)
-    residual, part = finish(where, chunks, a, fwd, rinv, col)
+    where = jnp.stack([dh, dl, y]).astype(jnp.int32)
+    residual, part = finish(where, near, far, a, fwd, rinv, col)
     part = lax.all_to_all(part, "y", 0, 0, tiled=True).sum(0)
     halves = jnp.stack([part[:, :128], part[:, 128:]])
     mine = lax.dynamic_index_in_dim(halves, zh, 0, keepdims=False)

time: 170 us -> 174 us (1.024)
  the two profiles are of different devices: /device:TPU:4 before, /device:TPU:69 now
where the time goes in v2:
time: 174 us; the launch traced here: 173 us
  starting transfers between devices  89.2 us (51%)
  waiting for transfers between devices  46.1 us (26%)
  blocking collectives  17.4 us (10%)
  local copies, waits for them, and re-layouts  8.85 us (5%)
  Pallas kernels  7.5 us (4%)
  other arithmetic  3.47 us (2%)
    ppermute x8, starting transfers between devices, send(): return lax.ppermute(block, AXES, pairs(dest))  76.2 us
    ppermute x8, waiting for transfers between devices, send(): return lax.ppermute(block, AXES, pairs(dest))  26.9 us
    ppermute x1, waiting for transfers between devices, on_device(): total = mine + lax.ppermute(other, AXES, swap)  19.2 us
    all_to_all x1, blocking collectives, on_device(): part = lax.all_to_all(part, 'y', 0, 0, tiled=True).sum(0)  17.4 us
    unnamed x12, local copies, waits for them, and re-layouts  6.78 us
    all_to_all x1, starting transfers between devices, on_device(): near = lax.all_to_all(near, ('x', 'core'), 0, 0, tiled=True)  5.98 us
    all_to_all x1, starting transfers between devices, on_device(): far = lax.all_to_all(far, ('core', 'y'), 0, 0, tiled=True)  5.14 us
    pallas_call x1, Pallas kernels, prepare(): pl.pallas_call(prepare_kernel, grid=(4,), in_specs=[pl.BlockSpec(memory_s...  4.78 us
  transfers between devices with their start and end apart: 11, of which 4 were waited for; matrix products, arithmetic and copies ran while one was open for 0% of the time, Pallas kernels for 3%

profile of v2, /device:TPU:69, one launch (start us, length us, event | category | flops | bytes accessed | tf_op | source)
XLA Modules:
  0.0 173.4 jit_solution(14009920378487091781)
XLA Ops:
  0.7 0.0 copy-start.5
  0.7 1.2 constant_dynamic-slice_fusion.3
  2.0 0.9 pad_maximum_fusion
  2.8 5.1 %all-to-all-start = ((bf16[8,4,32,256]{3,2,1,0:T(8,128)(2,1)}), bf16[8,4,32,256]{3,2,1,0:T(8,128)(2,1)S(1)}, u32[]{:S(2)}, u32[]{:S(2)}) async-start(bf16[8,4,32,256]{3,2,1,0:T(8,128)(2,1)} %bitcast.17), calls=%async_computation | async-start | bytes 1048576 | tf_op jit(solution)/shard_map/all_to_all | solution.py:160
  8.0 0.0 copy-done.5
  8.0 0.0 copy-start.4
  8.0 6.2 %collective-permute-start.1 = (bf16[8,32,256]{2,1,0:T(8,128)(2,1)S(1)}, bf16[8,32,256]{2,1,0:T(8,128)(2,1)S(1)}, u32[]{:S(2)}, u32[]{:S(2)}) collective-permute-start(bf16[8,32,256]{2,1,0:T(8,128)(2,1)S(1)} %bitcast.59), channel_id=1, source_target_pairs={{0,16},{1,80},{2,144},{3,208},{4,272},{5,336},{6,400},{7,464},{8,2... | collective-permute-start | bytes 393224 | tf_op jit(solution)/shard_map/ppermute | solution.py:151
  14.2 2.1 %collective-permute-start = (bf16[8,32,256]{2,1,0:T(8,128)(2,1)S(1)}, bf16[8,32,256]{2,1,0:T(8,128)(2,1)S(1)}, u32[]{:S(2)}, u32[]{:S(2)}) collective-permute-start(bf16[8,32,256]{2,1,0:T(8,128)(2,1)S(1)} %bitcast.57), channel_id=1, source_target_pairs={{0,0},{1,64},{2,128},{3,192},{4,256},{5,320},{6,384},{7,448},{8,8}... | collective-permute-start | bytes 393224 | tf_op jit(solution)/shard_map/ppermute | solution.py:151
  16.3 4.0 %collective-permute-start.2 = (bf16[8,32,256]{2,1,0:T(8,128)(2,1)S(1)}, bf16[8,32,256]{2,1,0:T(8,128)(2,1)S(1)}, u32[]{:S(2)}, u32[]{:S(2)}) collective-permute-start(bf16[8,32,256]{2,1,0:T(8,128)(2,1)S(1)} %bitcast.55), channel_id=1, source_target_pairs={{0,32},{1,96},{2,160},{3,224},{4,288},{5,352},{6,416},{7,480},{8,4... | collective-permute-start | bytes 393224 | tf_op jit(solution)/shard_map/ppermute | solution.py:151
  20.3 5.7 %collective-permute-start.3 = (bf16[8,32,256]{2,1,0:T(8,128)(2,1)S(1)}, bf16[8,32,256]{2,1,0:T(8,128)(2,1)S(1)}, u32[]{:S(2)}, u32[]{:S(2)}) collective-permute-start(bf16[8,32,256]{2,1,0:T(8,128)(2,1)S(1)} %bitcast.53), channel_id=1, source_target_pairs={{0,48},{1,112},{2,176},{3,240},{4,304},{5,368},{6,432},{7,496},{8,... | collective-permute-start | bytes 393224 | tf_op jit(solution)/shard_map/ppermute | solution.py:151
  26.0 0.0 collective-permute-done.1
  26.0 0.0 collective-permute-done
  26.1 2.1 %collective-permute-done.2 = bf16[8,32,256]{2,1,0:T(8,128)(2,1)S(1)} collective-permute-done((bf16[8,32,256]{2,1,0:T(8,128)(2,1)S(1)}, bf16[8,32,256]{2,1,0:T(8,128)(2,1)S(1)}, u32[]{:S(2)}, u32[]{:S(2)}) %collective-permute-start.2) | collective-permute-done | bytes 131104 | tf_op jit(solution)/shard_map/ppermute | solution.py:151
  28.1 7.5 %collective-permute-done.3 = bf16[8,32,256]{2,1,0:T(8,128)(2,1)S(1)} collective-permute-done((bf16[8,32,256]{2,1,0:T(8,128)(2,1)S(1)}, bf16[8,32,256]{2,1,0:T(8,128)(2,1)S(1)}, u32[]{:S(2)}, u32[]{:S(2)}) %collective-permute-start.3) | collective-permute-done | bytes 131104 | tf_op jit(solution)/shard_map/ppermute | solution.py:151
  35.6 0.0 all-to-all-done
  35.6 0.9 pad_maximum_fusion.1
  36.5 6.0 %all-to-all-start.1 = ((bf16[8,4,32,256]{3,2,1,0:T(8,128)(2,1)}), bf16[8,4,32,256]{3,2,1,0:T(8,128)(2,1)S(1)}, u32[]{:S(2)}, u32[]{:S(2)}) async-start(bf16[8,4,32,256]{3,2,1,0:T(8,128)(2,1)} %pad_maximum_fusion.1), calls=%async_computation.1 | async-start | bytes 1048576 | tf_op jit(solution)/shard_map/all_to_all | solution.py:165
  42.5 0.7 dynamic-slice_bitcast_fusion
  43.2 28.6 %collective-permute-start.7 = (bf16[8,32,256]{2,1,0:T(8,128)(2,1)}, bf16[8,32,256]{2,1,0:T(8,128)(2,1)S(1)}, u32[]{:S(2)}, u32[]{:S(2)}) collective-permute-start(bf16[8,32,256]{2,1,0:T(8,128)(2,1)} %get-tuple-element.44), channel_id=1, source_target_pairs={{0,112},{1,48},{2,240},{3,176},{4,368},{5,304},{6,496},{7,432},{8,... | collective-permute-start | bytes 393224 | tf_op jit(solution)/shard_map/ppermute | solution.py:151
  71.8 4.7 %collective-permute-start.6 = (bf16[8,32,256]{2,1,0:T(8,128)(2,1)}, bf16[8,32,256]{2,1,0:T(8,128)(2,1)S(1)}, u32[]{:S(2)}, u32[]{:S(2)}) collective-permute-start(bf16[8,32,256]{2,1,0:T(8,128)(2,1)} %get-tuple-element.45), channel_id=1, source_target_pairs={{0,96},{1,32},{2,224},{3,160},{4,352},{5,288},{6,480},{7,416},{8,1... | collective-permute-start | bytes 393224 | tf_op jit(solution)/shard_map/ppermute | solution.py:151
  76.5 14.0 %collective-permute-start.5 = (bf16[8,32,256]{2,1,0:T(8,128)(2,1)S(1)}, bf16[8,32,256]{2,1,0:T(8,128)(2,1)S(1)}, u32[]{:S(2)}, u32[]{:S(2)}) collective-permute-start(bf16[8,32,256]{2,1,0:T(8,128)(2,1)S(1)} %get-tuple-element.46), channel_id=1, source_target_pairs={{0,80},{1,16},{2,208},{3,144},{4,336},{5,272},{6,464},{7,400},{8,8... | collective-permute-start | bytes 393224 | tf_op jit(solution)/shard_map/ppermute | solution.py:151
  90.6 10.8 %collective-permute-start.4 = (bf16[8,32,256]{2,1,0:T(8,128)(2,1)S(1)}, bf16[8,32,256]{2,1,0:T(8,128)(2,1)S(1)}, u32[]{:S(2)}, u32[]{:S(2)}) collective-permute-start(bf16[8,32,256]{2,1,0:T(8,128)(2,1)S(1)} %get-tuple-element.47), channel_id=1, source_target_pairs={{0,64},{1,0},{2,192},{3,128},{4,320},{5,256},{6,448},{7,384},{8,72... | collective-permute-start | bytes 393224 | tf_op jit(solution)/shard_map/ppermute | solution.py:151
  101.4 0.0 copy-done.4
  101.4 0.0 copy-start.2
  101.4 1.0 copy-done.2
  102.5 0.0 copy-start.3
  102.5 1.6 copy-done.3
  104.0 4.8 %prepare.1 = (bf16[4,1024,512]{2,1,0:T(8,128)(2,1)S(1)}, f32[4,256,512]{2,1,0:T(8,128)S(1)}, f32[4,8,512]{2,1,0:T(8,128)S(1)}, f32[8,1024]{1,0:T(8,128)S(1)}) custom-call(s32[4,16]{1,0:T(4,128)S(1)} %copy-done.4, bf16[256,1024]{1,0:T(8,128)(2,1)S(1)} %copy-done.2, bf16[4,16,2,64,128]{4,3,2,1,0:T(8,128)(2,1)S(1)} %copy-done.3), custom_call_target="tpu_custom_call" | custom-call | flops 1100000000 | bytes 10000000 | tf_op jit(solution)/shard_map/prepare/pallas_call | solution.py:72
  108.8 0.0 copy-start
  108.9 2.0 %copy-done = bf16[4,1024,512]{2,1,0:T(8,128)(2,1)} copy-done((bf16[4,1024,512]{2,1,0:T(8,128)(2,1)}, bf16[4,1024,512]{2,1,0:T(8,128)(2,1)S(1)}, u32[]{:S(2)}) %copy-start) | copy-done | bytes 4194328
  110.8 0.1 pad_add_fusion.where_ref
  110.9 0.0 collective-permute-done.7.refs_4_
  110.9 0.0 collective-permute-done.6.refs_3_
  110.9 17.3 %collective-permute-done.5.refs_2_ = bf16[8,32,256]{2,1,0:T(8,128)(2,1)S(1)} collective-permute-done((bf16[8,32,256]{2,1,0:T(8,128)(2,1)S(1)}, bf16[8,32,256]{2,1,0:T(8,128)(2,1)S(1)}, u32[]{:S(2)}, u32[]{:S(2)}) %collective-permute-start.5) | collective-permute-done | bytes 131104 | tf_op jit(solution)/shard_map/ppermute | solution.py:151
  128.2 0.0 collective-permute-done.4.refs_1_
  128.2 0.0 all-to-all-done.1.refs_0_
  128.2 0.0 copy-start.1
  128.2 2.2 %copy-done.1 = bf16[4,1024,512]{2,1,0:T(8,128)(2,1)S(1)} copy-done((bf16[4,1024,512]{2,1,0:T(8,128)(2,1)S(1)}, bf16[4,1024,512]{2,1,0:T(8,128)(2,1)}, u32[]{:S(2)}) %copy-start.1) | copy-done | bytes 4194328
  130.4 2.7 %finish.1 = (bf16[8,256,256]{2,1,0:T(8,128)(2,1)}, f32[4,264,256]{2,1,0:T(8,128)S(1)}) custom-call(s32[3]{0:T(128)S(1)} %pad_add_fusion.where_ref, bf16[8,4,32,256]{3,2,1,0:T(8,128)(2,1)S(1)} %all-to-all-done.1.refs_0_, bf16[8,32,256]{2,1,0:T(8,128)(2,1)S(1)} %collective-permute-done.4.refs_1_, bf16[8,32,256]{2,1,0:T(8,128)(2,1)S(1)} %collective-permute-done.5.refs_2_, ...), custom_call_target="tpu_custom_call" | custom-call | flops 1100000000 | bytes 10000000 | tf_op jit(solution)/shard_map/finish/pallas_call | solution.py:126
  133.1 17.4 %all_to_all.15 = f32[4,264,256]{2,1,0:T(8,128)S(1)} all-to-all(f32[4,264,256]{2,1,0:T(8,128)S(1)} %get-tuple-element.34), channel_id=1, replica_groups=mesh['x'=4,'zl'=8,'core'=2,'y'=4,'zh'=2] {'y'}, dimensions={0} | all-to-all | bytes 2162688 | tf_op jit(solution)/shard_map/all_to_all | solution.py:169
  150.5 0.1 reduce_sum.9
  150.7 1.9 %collective-permute-start.8 = (f32[264,128]{1,0:T(8,128)S(1)}, f32[264,128]{1,0:T(8,128)S(1)}, u32[]{:S(2)}, u32[]{:S(2)}) collective-permute-start(f32[264,128]{1,0:T(8,128)S(1)} %fusion.1), channel_id=1, source_target_pairs={{0,1},{1,0},{2,3},{3,2},{4,5},{5,4},{6,7},{7,6},{8,9},{9,8},{10,11... | collective-permute-start | bytes 405512 | tf_op jit(solution)/shard_map/ppermute | solution.py:174
  152.6 19.2 %collective-permute-done.8 = f32[264,128]{1,0:T(8,128)S(1)} collective-permute-done((f32[264,128]{1,0:T(8,128)S(1)}, f32[264,128]{1,0:T(8,128)S(1)}, u32[]{:S(2)}, u32[]{:S(2)}) %collective-permute-start.8) | collective-permute-done | bytes 135200 | tf_op jit(solution)/shard_map/ppermute | solution.py:174
  171.9 1.5 fusion.5
  (7 shorter events, 0.2 us)
Async XLA Ops:
  0.7 7.3 %copy-start.5 = (bf16[1,64,1,32,256]{4,3,2,1,0:T(8,128)(2,1)S(1)}, bf16[1,64,1,32,256]{4,3,2,1,0:T(8,128)(2,1)}, u32[]{:S(2)}) copy-start(bf16[1,64,1,32,256]{4,3,2,1,0:T(8,128)(2,1)} %param.4) | copy-start | bytes 3145732
  2.8 32.8 %all-to-all-start = ((bf16[8,4,32,256]{3,2,1,0:T(8,128)(2,1)}), bf16[8,4,32,256]{3,2,1,0:T(8,128)(2,1)S(1)}, u32[]{:S(2)}, u32[]{:S(2)}) async-start(bf16[8,4,32,256]{3,2,1,0:T(8,128)(2,1)} %bitcast.17), calls=%async_computation | async-start | bytes 1048576 | tf_op jit(solution)/shard_map/all_to_all | solution.py:160
  8.0 93.4 %copy-start.4 = (s32[4,16]{1,0:T(4,128)S(1)}, s32[4,16]{1,0:T(4,128)}, u32[]{:S(2)}) copy-start(s32[4,16]{1,0:T(4,128)} %first_ref) | copy-start | bytes 772
  8.0 18.0 %collective-permute-start.1 = (bf16[8,32,256]{2,1,0:T(8,128)(2,1)S(1)}, bf16[8,32,256]{2,1,0:T(8,128)(2,1)S(1)}, u32[]{:S(2)}, u32[]{:S(2)}) collective-permute-start(bf16[8,32,256]{2,1,0:T(8,128)(2,1)S(1)} %bitcast.59), channel_id=1, source_target_pairs={{0,16},{1,80},{2,144},{3,208},{4,272},{5,336},{6,400},{7,464},{8,2... | collective-permute-start | bytes 393224 | tf_op jit(solution)/shard_map/ppermute | solution.py:151
  14.2 11.9 %collective-permute-start = (bf16[8,32,256]{2,1,0:T(8,128)(2,1)S(1)}, bf16[8,32,256]{2,1,0:T(8,128)(2,1)S(1)}, u32[]{:S(2)}, u32[]{:S(2)}) collective-permute-start(bf16[8,32,256]{2,1,0:T(8,128)(2,1)S(1)} %bitcast.57), channel_id=1, source_target_pairs={{0,0},{1,64},{2,128},{3,192},{4,256},{5,320},{6,384},{7,448},{8,8}... | collective-permute-start | bytes 393224 | tf_op jit(solution)/shard_map/ppermute | solution.py:151
  16.3 11.8 %collective-permute-start.2 = (bf16[8,32,256]{2,1,0:T(8,128)(2,1)S(1)}, bf16[8,32,256]{2,1,0:T(8,128)(2,1)S(1)}, u32[]{:S(2)}, u32[]{:S(2)}) collective-permute-start(bf16[8,32,256]{2,1,0:T(8,128)(2,1)S(1)} %bitcast.55), channel_id=1, source_target_pairs={{0,32},{1,96},{2,160},{3,224},{4,288},{5,352},{6,416},{7,480},{8,4... | collective-permute-start | bytes 393224 | tf_op jit(solution)/shard_map/ppermute | solution.py:151
  20.3 15.3 %collective-permute-start.3 = (bf16[8,32,256]{2,1,0:T(8,128)(2,1)S(1)}, bf16[8,32,256]{2,1,0:T(8,128)(2,1)S(1)}, u32[]{:S(2)}, u32[]{:S(2)}) collective-permute-start(bf16[8,32,256]{2,1,0:T(8,128)(2,1)S(1)} %bitcast.53), channel_id=1, source_target_pairs={{0,48},{1,112},{2,176},{3,240},{4,304},{5,368},{6,432},{7,496},{8,... | collective-permute-start | bytes 393224 | tf_op jit(solution)/shard_map/ppermute | solution.py:151
  36.5 91.7 %all-to-all-start.1 = ((bf16[8,4,32,256]{3,2,1,0:T(8,128)(2,1)}), bf16[8,4,32,256]{3,2,1,0:T(8,128)(2,1)S(1)}, u32[]{:S(2)}, u32[]{:S(2)}) async-start(bf16[8,4,32,256]{3,2,1,0:T(8,128)(2,1)} %pad_maximum_fusion.1), calls=%async_computation.1 | async-start | bytes 1048576 | tf_op jit(solution)/shard_map/all_to_all | solution.py:165
  43.2 67.7 %collective-permute-start.7 = (bf16[8,32,256]{2,1,0:T(8,128)(2,1)}, bf16[8,32,256]{2,1,0:T(8,128)(2,1)S(1)}, u32[]{:S(2)}, u32[]{:S(2)}) collective-permute-start(bf16[8,32,256]{2,1,0:T(8,128)(2,1)} %get-tuple-element.44), channel_id=1, source_target_pairs={{0,112},{1,48},{2,240},{3,176},{4,368},{5,304},{6,496},{7,432},{8,... | collective-permute-start | bytes 393224 | tf_op jit(solution)/shard_map/ppermute | solution.py:151
  71.8 39.1 %collective-permute-start.6 = (bf16[8,32,256]{2,1,0:T(8,128)(2,1)}, bf16[8,32,256]{2,1,0:T(8,128)(2,1)S(1)}, u32[]{:S(2)}, u32[]{:S(2)}) collective-permute-start(bf16[8,32,256]{2,1,0:T(8,128)(2,1)} %get-tuple-element.45), channel_id=1, source_target_pairs={{0,96},{1,32},{2,224},{3,160},{4,352},{5,288},{6,480},{7,416},{8,1... | collective-permute-start | bytes 393224 | tf_op jit(solution)/shard_map/ppermute | solution.py:151
  76.5 51.7 %collective-permute-start.5 = (bf16[8,32,256]{2,1,0:T(8,128)(2,1)S(1)}, bf16[8,32,256]{2,1,0:T(8,128)(2,1)S(1)}, u32[]{:S(2)}, u32[]{:S(2)}) collective-permute-start(bf16[8,32,256]{2,1,0:T(8,128)(2,1)S(1)} %get-tuple-element.46), channel_id=1, source_target_pairs={{0,80},{1,16},{2,208},{3,144},{4,336},{5,272},{6,464},{7,400},{8,8... | collective-permute-start | bytes 393224 | tf_op jit(solution)/shard_map/ppermute | solution.py:151
  90.6 37.6 %collective-permute-start.4 = (bf16[8,32,256]{2,1,0:T(8,128)(2,1)S(1)}, bf16[8,32,256]{2,1,0:T(8,128)(2,1)S(1)}, u32[]{:S(2)}, u32[]{:S(2)}) collective-permute-start(bf16[8,32,256]{2,1,0:T(8,128)(2,1)S(1)} %get-tuple-element.47), channel_id=1, source_target_pairs={{0,64},{1,0},{2,192},{3,128},{4,320},{5,256},{6,448},{7,384},{8,72... | collective-permute-start | bytes 393224 | tf_op jit(solution)/shard_map/ppermute | solution.py:151
  101.4 1.0 copy-start.2
  102.5 1.6 copy-start.3
  108.8 2.0 %copy-start = (bf16[4,1024,512]{2,1,0:T(8,128)(2,1)}, bf16[4,1024,512]{2,1,0:T(8,128)(2,1)S(1)}, u32[]{:S(2)}) copy-start(bf16[4,1024,512]{2,1,0:T(8,128)(2,1)S(1)} %get-tuple-element.30.refs_5_) | copy-start | bytes 12582916
  128.2 2.2 %copy-start.1 = (bf16[4,1024,512]{2,1,0:T(8,128)(2,1)S(1)}, bf16[4,1024,512]{2,1,0:T(8,128)(2,1)}, u32[]{:S(2)}) copy-start(bf16[4,1024,512]{2,1,0:T(8,128)(2,1)} %copy-done) | copy-start | bytes 12582916
  150.7 21.2 %collective-permute-start.8 = (f32[264,128]{1,0:T(8,128)S(1)}, f32[264,128]{1,0:T(8,128)S(1)}, u32[]{:S(2)}, u32[]{:S(2)}) collective-permute-start(f32[264,128]{1,0:T(8,128)S(1)} %fusion.1), channel_id=1, source_target_pairs={{0,1},{1,0},{2,3},{3,2},{4,5},{5,4},{6,7},{7,6},{8,9},{9,8},{10,11... | collective-permute-start | bytes 405512 | tf_op jit(solution)/shard_map/ppermute | solution.py:174

commit v3 on v2

--- a/solution.py
+++ b/solution.py
@@ -95,13 +95,43 @@
     )(first, image, system)
 
 
+def pack_kernel(where_ref, p_ref, n0_ref, n1_ref, n2_ref, n3_ref, far_ref, sems):
+    x, dl, zh = where_ref[0], where_ref[1], where_ref[2]
+    copies = []
+    for b, near_ref in enumerate((n0_ref, n1_ref, n2_ref, n3_ref)):
+        low = dl ^ b
+        copies.append(pltpu.make_async_copy(p_ref.at[:, (zh ^ (low & 1)) * 4 + low], near_ref, sems.at[b]))
+    for m in range(4):
+        for low in range(4):
+            src = p_ref.at[x ^ m, (zh ^ (low & 1) ^ 1) * 4 + low]
+            copies.append(pltpu.make_async_copy(src, far_ref.at[:, m, low], sems.at[4 + m * 4 + low]))
+    for copy in copies:
+        copy.start()
+    for copy in copies:
+        copy.wait()
+
+
+def pack(where, projections):
+    vmem = pl.BlockSpec(memory_space=pltpu.VMEM)
+    return pl.pallas_call(
+        pack_kernel,
+        in_specs=[pl.BlockSpec(memory_space=pltpu.SMEM), pl.BlockSpec(memory_space=pl.ANY)],
+        out_specs=[vmem] * 5,
+        out_shape=[jax.ShapeDtypeStruct((4, 2, 32, 256), BF16)] * 4 + [jax.ShapeDtypeStruct((2, 4, 4, 32, 256), BF16)],
+        scratch_shapes=[pltpu.SemaphoreType.DMA((20,))],
+        cost_estimate=pl.CostEstimate(flops=0, bytes_accessed=2097152, transcendentals=0),
+        compiler_params=pltpu.CompilerParams(vmem_limit_bytes=8 * 1024 * 1024),
+        name="pack",
+    )(where.astype(jnp.int32), projections.reshape(4, 8, 2, 32, 256))
+
+
 def finish_kernel(where_ref, *refs):
     near_ref, far_refs, (a_ref, fwd_ref, rinv_ref, col_ref, res_ref, part_ref, held_ref) = refs[0], refs[1:5], refs[5:]
     dh, dl, own_y = where_ref[0], where_ref[1], where_ref[2]
     for b in range(4):
         g = dl ^ b
         for a in range(2):
-            zh = dh ^ a
+            zh = dh ^ (dl & 1) ^ a
             for t in range(2):
                 rinv = rinv_ref[g, 0:1, t * 256 : (t + 1) * 256]
                 for y in range(4):
@@ -141,27 +171,21 @@
 def on_device(projections, start_image, system, first_tile):
     x, zl, y, zh = (lax.axis_index(name) for name in ("x", "zl", "y", "zh"))
     dh, dl = zl // 4, zl % 4
-    mine = zh * 4 + dl
-    blocks = projections.reshape(4, 2, 4, 2, 32, 256)
-
-    def send(block, k):
+    def send(block, half, b):
         def dest(x, zl, core, y, zh):
-            return (x ^ y, (zh * 4 + zl % 4) ^ k, core, x, zl // 4)
+            low = (zl % 4) ^ b
+            return (x ^ y, (zh ^ (low & 1) ^ half) * 4 + low, core, x, zl // 4)
 
         return lax.ppermute(block, AXES, pairs(dest))
 
-    near = lax.dynamic_index_in_dim(blocks, zh, 1, keepdims=False)
-    near = [lax.dynamic_index_in_dim(near, dl ^ b, 1, keepdims=False) for b in range(4)]
-    first_tile, image, system, near = lax.optimization_barrier((first_tile, start_image, system, near))
-    far = lax.dynamic_index_in_dim(blocks, 1 - zh, 1, keepdims=False)
-    far = jnp.stack([lax.dynamic_index_in_dim(far, x ^ m, 0, keepdims=False) for m in range(4)])
-    far = far.transpose(2, 0, 1, 3, 4).reshape(8, 4, 32, 256)
-    near = [send(block.reshape(8, 32, 256), b) for b, block in enumerate(near)]
-    far = lax.all_to_all(far, ("core", "y"), 0, 0, tiled=True)
+    *near, far = pack(jnp.stack([x, dl, zh]), projections)
+    first_tile, image, system, far = lax.optimization_barrier((first_tile, start_image, system, far))
+    near = [send(block.reshape(8, 32, 256), 0, b) for b, block in enumerate(near)]
+    far = lax.all_to_all(far.reshape(8, 4, 32, 256), ("core", "y"), 0, 0, tiled=True)
     near, _ = lax.optimization_barrier((near, far))
     far = [lax.dynamic_index_in_dim(far, dl ^ b, 1, keepdims=False) for b in range(4)]
     near = jnp.stack(near, 1)
-    far = [send(block, 4 + b) for b, block in enumerate(far)]
+    far = [send(block, 1, b) for b, block in enumerate(far)]
     near = lax.all_to_all(near, ("x", "core"), 0, 0, tiled=True)
     a, fwd, rinv, col = prepare(first_tile, image, system)
     where = jnp.stack([dh, dl, y]).astype(jnp.int32)

time: 174 us -> 165 us (0.948)
  the two profiles are of different devices: /device:TPU:69 before, /device:TPU:4 now
where the time goes in v3:
time: 165 us; the launch traced here: 164 us
  starting transfers between devices  80.3 us (49%)
  waiting for transfers between devices  60.7 us (37%)
  local copies, waits for them, and re-layouts  9.78 us (6%)
  Pallas kernels  9.54 us (6%)
  other arithmetic  2.68 us (2%)
    ppermute x8, starting transfers between devices, send(): return lax.ppermute(block, AXES, pairs(dest))  65.6 us
    ppermute x8, waiting for transfers between devices, send(): return lax.ppermute(block, AXES, pairs(dest))  30.4 us
    all_to_all x1, waiting for transfers between devices, on_device(): part = lax.all_to_all(part, 'y', 0, 0, tiled=True).sum(0)  15.9 us
    ppermute x1, waiting for transfers between devices, on_device(): total = mine + lax.ppermute(other, AXES, swap)  14.4 us
    unnamed x14, local copies, waits for them, and re-layouts  9.02 us
    all_to_all x1, starting transfers between devices, on_device(): near = lax.all_to_all(near, ('x', 'core'), 0, 0, tiled=True)  4.8 us
    pallas_call x1, Pallas kernels, prepare(): pl.pallas_call(prepare_kernel, grid=(4,), in_specs=[pl.BlockSpec(memory_s...  4.76 us
    all_to_all x1, starting transfers between devices, on_device(): lax.all_to_all(far.reshape(8, 4, 32, 256), ('core', 'y'), 0, 0, tiled=True)  4.48 us
  transfers between devices with their start and end apart: 12, of which 5 were waited for; matrix products, arithmetic and copies ran while one was open for 0% of the time, Pallas kernels for 3%

profile of v3, /device:TPU:4, one launch (start us, length us, event | category | flops | bytes accessed | tf_op | source)
XLA Modules:
  0.0 163.9 jit_solution(8554400089016126539)
XLA Ops:
  0.6 0.1 pad_add_fusion.1.where_ref
  0.7 0.0 copy-start.3
  0.7 1.2 copy-done.3
  1.9 2.1 %pack.1 = (bf16[4,2,32,256]{3,2,1,0:T(8,128)(2,1)S(1)}, bf16[4,2,32,256]{3,2,1,0:T(8,128)(2,1)S(1)}, bf16[4,2,32,256]{3,2,1,0:T(8,128)(2,1)S(1)}, bf16[4,2,32,25...) custom-call(s32[3]{0:T(128)S(1)} %pad_add_fusion.1.where_ref, bf16[4,8,2,32,256]{4,3,2,1,0:T(8,128)(2,1)S(1)} %bitcast.35), custom_call_target="tpu_custom_call" | custom-call | bytes 2097152 | tf_op jit(solution)/shard_map/pack/pallas_call | solution.py:116
  4.0 0.0 copy-start.6
  4.0 4.5 %all-to-all-start = ((bf16[8,4,32,256]{3,2,1,0:T(8,128)(2,1)}), bf16[8,4,32,256]{3,2,1,0:T(8,128)(2,1)S(1)}, u32[]{:S(2)}, u32[]{:S(2)}) async-start(bf16[8,4,32,256]{3,2,1,0:T(8,128)(2,1)} %bitcast.10), calls=%async_computation | async-start | bytes 1048576 | tf_op jit(solution)/shard_map/all_to_all | solution.py:184
  8.5 5.4 %collective-permute-start = (bf16[8,32,256]{2,1,0:T(8,128)(2,1)S(1)}, bf16[8,32,256]{2,1,0:T(8,128)(2,1)S(1)}, u32[]{:S(2)}, u32[]{:S(2)}) collective-permute-start(bf16[8,32,256]{2,1,0:T(8,128)(2,1)S(1)} %bitcast.39), channel_id=1, source_target_pairs={{0,0},{1,64},{2,128},{3,192},{4,256},{5,320},{6,384},{7,448},{8,8}... | collective-permute-start | bytes 393224 | tf_op jit(solution)/shard_map/ppermute | solution.py:179
  14.0 17.9 %collective-permute-start.1 = (bf16[8,32,256]{2,1,0:T(8,128)(2,1)S(1)}, bf16[8,32,256]{2,1,0:T(8,128)(2,1)S(1)}, u32[]{:S(2)}, u32[]{:S(2)}) collective-permute-start(bf16[8,32,256]{2,1,0:T(8,128)(2,1)S(1)} %bitcast.38), channel_id=1, source_target_pairs={{0,80},{1,16},{2,208},{3,144},{4,336},{5,272},{6,464},{7,400},{8,8... | collective-permute-start | bytes 393224 | tf_op jit(solution)/shard_map/ppermute | solution.py:179
  31.9 5.3 %collective-permute-start.2 = (bf16[8,32,256]{2,1,0:T(8,128)(2,1)S(1)}, bf16[8,32,256]{2,1,0:T(8,128)(2,1)S(1)}, u32[]{:S(2)}, u32[]{:S(2)}) collective-permute-start(bf16[8,32,256]{2,1,0:T(8,128)(2,1)S(1)} %bitcast.37), channel_id=1, source_target_pairs={{0,32},{1,96},{2,160},{3,224},{4,288},{5,352},{6,416},{7,480},{8,4... | collective-permute-start | bytes 393224 | tf_op jit(solution)/shard_map/ppermute | solution.py:179
  37.2 5.0 %collective-permute-start.3 = (bf16[8,32,256]{2,1,0:T(8,128)(2,1)S(1)}, bf16[8,32,256]{2,1,0:T(8,128)(2,1)S(1)}, u32[]{:S(2)}, u32[]{:S(2)}) collective-permute-start(bf16[8,32,256]{2,1,0:T(8,128)(2,1)S(1)} %bitcast.36), channel_id=1, source_target_pairs={{0,112},{1,48},{2,240},{3,176},{4,368},{5,304},{6,496},{7,432},{8,... | collective-permute-start | bytes 393224 | tf_op jit(solution)/shard_map/ppermute | solution.py:179
  42.2 0.0 collective-permute-done
  42.2 0.0 collective-permute-done.1
  42.2 5.5 %collective-permute-done.2 = bf16[8,32,256]{2,1,0:T(8,128)(2,1)S(1)} collective-permute-done((bf16[8,32,256]{2,1,0:T(8,128)(2,1)S(1)}, bf16[8,32,256]{2,1,0:T(8,128)(2,1)S(1)}, u32[]{:S(2)}, u32[]{:S(2)}) %collective-permute-start.2) | collective-permute-done | bytes 131104 | tf_op jit(solution)/shard_map/ppermute | solution.py:179
  47.7 6.6 %collective-permute-done.3 = bf16[8,32,256]{2,1,0:T(8,128)(2,1)S(1)} collective-permute-done((bf16[8,32,256]{2,1,0:T(8,128)(2,1)S(1)}, bf16[8,32,256]{2,1,0:T(8,128)(2,1)S(1)}, u32[]{:S(2)}, u32[]{:S(2)}) %collective-permute-start.3) | collective-permute-done | bytes 131104 | tf_op jit(solution)/shard_map/ppermute | solution.py:179
  54.3 0.0 all-to-all-done
  54.3 0.9 pad_maximum_fusion
  55.1 4.8 %all-to-all-start.1 = ((bf16[8,4,32,256]{3,2,1,0:T(8,128)(2,1)}), bf16[8,4,32,256]{3,2,1,0:T(8,128)(2,1)S(1)}, u32[]{:S(2)}, u32[]{:S(2)}) async-start(bf16[8,4,32,256]{3,2,1,0:T(8,128)(2,1)} %pad_maximum_fusion), calls=%async_computation.1 | async-start | bytes 1048576 | tf_op jit(solution)/shard_map/all_to_all | solution.py:189
  59.9 0.7 dynamic-slice_bitcast_fusion
  60.7 10.9 %collective-permute-start.4 = (bf16[8,32,256]{2,1,0:T(8,128)(2,1)}, bf16[8,32,256]{2,1,0:T(8,128)(2,1)S(1)}, u32[]{:S(2)}, u32[]{:S(2)}) collective-permute-start(bf16[8,32,256]{2,1,0:T(8,128)(2,1)} %get-tuple-element.43), channel_id=1, source_target_pairs={{0,64},{1,0},{2,192},{3,128},{4,320},{5,256},{6,448},{7,384},{8,72... | collective-permute-start | bytes 393224 | tf_op jit(solution)/shard_map/ppermute | solution.py:179
  71.5 3.5 %collective-permute-start.5 = (bf16[8,32,256]{2,1,0:T(8,128)(2,1)}, bf16[8,32,256]{2,1,0:T(8,128)(2,1)S(1)}, u32[]{:S(2)}, u32[]{:S(2)}) collective-permute-start(bf16[8,32,256]{2,1,0:T(8,128)(2,1)} %get-tuple-element.42), channel_id=1, source_target_pairs={{0,16},{1,80},{2,144},{3,208},{4,272},{5,336},{6,400},{7,464},{8,2... | collective-permute-start | bytes 393224 | tf_op jit(solution)/shard_map/ppermute | solution.py:179
  75.0 15.7 %collective-permute-start.6 = (bf16[8,32,256]{2,1,0:T(8,128)(2,1)S(1)}, bf16[8,32,256]{2,1,0:T(8,128)(2,1)S(1)}, u32[]{:S(2)}, u32[]{:S(2)}) collective-permute-start(bf16[8,32,256]{2,1,0:T(8,128)(2,1)S(1)} %get-tuple-element.41), channel_id=1, source_target_pairs={{0,96},{1,32},{2,224},{3,160},{4,352},{5,288},{6,480},{7,416},{8,1... | collective-permute-start | bytes 393224 | tf_op jit(solution)/shard_map/ppermute | solution.py:179
  90.8 1.9 %collective-permute-start.7 = (bf16[8,32,256]{2,1,0:T(8,128)(2,1)S(1)}, bf16[8,32,256]{2,1,0:T(8,128)(2,1)S(1)}, u32[]{:S(2)}, u32[]{:S(2)}) collective-permute-start(bf16[8,32,256]{2,1,0:T(8,128)(2,1)S(1)} %get-tuple-element.40), channel_id=1, source_target_pairs={{0,48},{1,112},{2,176},{3,240},{4,304},{5,368},{6,432},{7,496},{8,... | collective-permute-start | bytes 393224 | tf_op jit(solution)/shard_map/ppermute | solution.py:179
  92.7 0.0 copy-done.6
  92.7 0.0 copy-start.4
  92.7 1.0 copy-done.4
  93.8 0.0 copy-start.5
  93.8 1.6 copy-done.5
  95.3 4.8 %prepare.1 = (bf16[4,1024,512]{2,1,0:T(8,128)(2,1)S(1)}, f32[4,256,512]{2,1,0:T(8,128)S(1)}, f32[4,8,512]{2,1,0:T(8,128)S(1)}, f32[8,1024]{1,0:T(8,128)S(1)}) custom-call(s32[4,16]{1,0:T(4,128)S(1)} %copy-done.6, bf16[256,1024]{1,0:T(8,128)(2,1)S(1)} %copy-done.4, bf16[4,16,2,64,128]{4,3,2,1,0:T(8,128)(2,1)S(1)} %copy-done.5), custom_call_target="tpu_custom_call" | custom-call | flops 1100000000 | bytes 10000000 | tf_op jit(solution)/shard_map/prepare/pallas_call | solution.py:72
  100.1 0.0 copy-start
  100.1 2.0 %copy-done = bf16[4,1024,512]{2,1,0:T(8,128)(2,1)} copy-done((bf16[4,1024,512]{2,1,0:T(8,128)(2,1)}, bf16[4,1024,512]{2,1,0:T(8,128)(2,1)S(1)}, u32[]{:S(2)}) %copy-start) | copy-done | bytes 4194328
  102.1 0.1 pad_add_fusion.where_ref
  102.2 18.3 %collective-permute-done.4.refs_1_ = bf16[8,32,256]{2,1,0:T(8,128)(2,1)S(1)} collective-permute-done((bf16[8,32,256]{2,1,0:T(8,128)(2,1)}, bf16[8,32,256]{2,1,0:T(8,128)(2,1)S(1)}, u32[]{:S(2)}, u32[]{:S(2)}) %collective-permute-start.4) | collective-permute-done | bytes 131104 | tf_op jit(solution)/shard_map/ppermute | solution.py:179
  120.5 0.0 collective-permute-done.5.refs_2_
  120.5 0.0 collective-permute-done.6.refs_3_
  120.5 0.0 collective-permute-done.7.refs_4_
  120.5 0.0 all-to-all-done.1.refs_0_
  120.5 0.0 copy-start.1
  120.5 2.2 %copy-done.1 = bf16[4,1024,512]{2,1,0:T(8,128)(2,1)S(1)} copy-done((bf16[4,1024,512]{2,1,0:T(8,128)(2,1)S(1)}, bf16[4,1024,512]{2,1,0:T(8,128)(2,1)}, u32[]{:S(2)}) %copy-start.1) | copy-done | bytes 4194328
  122.7 2.7 %finish.1 = (bf16[8,256,256]{2,1,0:T(8,128)(2,1)}, f32[4,264,256]{2,1,0:T(8,128)S(1)}) custom-call(s32[3]{0:T(128)S(1)} %pad_add_fusion.where_ref, bf16[8,4,32,256]{3,2,1,0:T(8,128)(2,1)S(1)} %all-to-all-done.1.refs_0_, bf16[8,32,256]{2,1,0:T(8,128)(2,1)S(1)} %collective-permute-done.4.refs_1_, bf16[8,32,256]{2,1,0:T(8,128)(2,1)S(1)} %collective-permute-done.5.refs_2_, ...), custom_call_target="tpu_custom_call" | custom-call | flops 1100000000 | bytes 10000000 | tf_op jit(solution)/shard_map/finish/pallas_call | solution.py:156
  125.4 0.0 copy-start.2
  125.4 1.0 copy-done.2
  126.4 3.5 %all-to-all-start.2 = ((f32[4,264,256]{2,1,0:T(8,128)}), f32[4,264,256]{2,1,0:T(8,128)S(1)}, u32[]{:S(2)}, u32[]{:S(2)}) async-start(f32[4,264,256]{2,1,0:T(8,128)} %copy-done.2), calls=%async_computation.2 | async-start | bytes 2162688 | tf_op jit(solution)/shard_map/all_to_all | solution.py:193
  130.0 15.9 %all-to-all-done.2 = f32[4,264,256]{2,1,0:T(8,128)S(1)} async-done(((f32[4,264,256]{2,1,0:T(8,128)}), f32[4,264,256]{2,1,0:T(8,128)S(1)}, u32[]{:S(2)}, u32[]{:S(2)}) %all-to-all-start.2) | async-done | bytes 1081376 | tf_op jit(solution)/shard_map/all_to_all | solution.py:193
  145.9 0.1 reduce_sum.9
  146.0 1.9 %collective-permute-start.8 = (f32[264,128]{1,0:T(8,128)S(1)}, f32[264,128]{1,0:T(8,128)S(1)}, u32[]{:S(2)}, u32[]{:S(2)}) collective-permute-start(f32[264,128]{1,0:T(8,128)S(1)} %fusion.1), channel_id=1, source_target_pairs={{0,1},{1,0},{2,3},{3,2},{4,5},{5,4},{6,7},{7,6},{8,9},{9,8},{10,11... | collective-permute-start | bytes 405512 | tf_op jit(solution)/shard_map/ppermute | solution.py:198
  148.0 14.4 %collective-permute-done.8 = f32[264,128]{1,0:T(8,128)S(1)} collective-permute-done((f32[264,128]{1,0:T(8,128)S(1)}, f32[264,128]{1,0:T(8,128)S(1)}, u32[]{:S(2)}, u32[]{:S(2)}) %collective-permute-start.8) | collective-permute-done | bytes 135200 | tf_op jit(solution)/shard_map/ppermute | solution.py:198
  162.4 1.5 fusion.5
  (4 shorter events, 0.1 us)
Async XLA Ops:
  0.7 1.2 copy-start.3
  4.0 88.7 %copy-start.6 = (s32[4,16]{1,0:T(4,128)S(1)}, s32[4,16]{1,0:T(4,128)}, u32[]{:S(2)}) copy-start(s32[4,16]{1,0:T(4,128)} %first_ref) | copy-start | bytes 772
  4.0 50.2 %all-to-all-start = ((bf16[8,4,32,256]{3,2,1,0:T(8,128)(2,1)}), bf16[8,4,32,256]{3,2,1,0:T(8,128)(2,1)S(1)}, u32[]{:S(2)}, u32[]{:S(2)}) async-start(bf16[8,4,32,256]{3,2,1,0:T(8,128)(2,1)} %bitcast.10), calls=%async_computation | async-start | bytes 1048576 | tf_op jit(solution)/shard_map/all_to_all | solution.py:184
  8.5 33.6 %collective-permute-start = (bf16[8,32,256]{2,1,0:T(8,128)(2,1)S(1)}, bf16[8,32,256]{2,1,0:T(8,128)(2,1)S(1)}, u32[]{:S(2)}, u32[]{:S(2)}) collective-permute-start(bf16[8,32,256]{2,1,0:T(8,128)(2,1)S(1)} %bitcast.39), channel_id=1, source_target_pairs={{0,0},{1,64},{2,128},{3,192},{4,256},{5,320},{6,384},{7,448},{8,8}... | collective-permute-start | bytes 393224 | tf_op jit(solution)/shard_map/ppermute | solution.py:179
  14.0 28.2 %collective-permute-start.1 = (bf16[8,32,256]{2,1,0:T(8,128)(2,1)S(1)}, bf16[8,32,256]{2,1,0:T(8,128)(2,1)S(1)}, u32[]{:S(2)}, u32[]{:S(2)}) collective-permute-start(bf16[8,32,256]{2,1,0:T(8,128)(2,1)S(1)} %bitcast.38), channel_id=1, source_target_pairs={{0,80},{1,16},{2,208},{3,144},{4,336},{5,272},{6,464},{7,400},{8,8... | collective-permute-start | bytes 393224 | tf_op jit(solution)/shard_map/ppermute | solution.py:179
  31.9 15.8 %collective-permute-start.2 = (bf16[8,32,256]{2,1,0:T(8,128)(2,1)S(1)}, bf16[8,32,256]{2,1,0:T(8,128)(2,1)S(1)}, u32[]{:S(2)}, u32[]{:S(2)}) collective-permute-start(bf16[8,32,256]{2,1,0:T(8,128)(2,1)S(1)} %bitcast.37), channel_id=1, source_target_pairs={{0,32},{1,96},{2,160},{3,224},{4,288},{5,352},{6,416},{7,480},{8,4... | collective-permute-start | bytes 393224 | tf_op jit(solution)/shard_map/ppermute | solution.py:179
  37.2 17.1 %collective-permute-start.3 = (bf16[8,32,256]{2,1,0:T(8,128)(2,1)S(1)}, bf16[8,32,256]{2,1,0:T(8,128)(2,1)S(1)}, u32[]{:S(2)}, u32[]{:S(2)}) collective-permute-start(bf16[8,32,256]{2,1,0:T(8,128)(2,1)S(1)} %bitcast.36), channel_id=1, source_target_pairs={{0,112},{1,48},{2,240},{3,176},{4,368},{5,304},{6,496},{7,432},{8,... | collective-permute-start | bytes 393224 | tf_op jit(solution)/shard_map/ppermute | solution.py:179
  55.1 65.4 %all-to-all-start.1 = ((bf16[8,4,32,256]{3,2,1,0:T(8,128)(2,1)}), bf16[8,4,32,256]{3,2,1,0:T(8,128)(2,1)S(1)}, u32[]{:S(2)}, u32[]{:S(2)}) async-start(bf16[8,4,32,256]{3,2,1,0:T(8,128)(2,1)} %pad_maximum_fusion), calls=%async_computation.1 | async-start | bytes 1048576 | tf_op jit(solution)/shard_map/all_to_all | solution.py:189
  60.7 59.8 %collective-permute-start.4 = (bf16[8,32,256]{2,1,0:T(8,128)(2,1)}, bf16[8,32,256]{2,1,0:T(8,128)(2,1)S(1)}, u32[]{:S(2)}, u32[]{:S(2)}) collective-permute-start(bf16[8,32,256]{2,1,0:T(8,128)(2,1)} %get-tuple-element.43), channel_id=1, source_target_pairs={{0,64},{1,0},{2,192},{3,128},{4,320},{5,256},{6,448},{7,384},{8,72... | collective-permute-start | bytes 393224 | tf_op jit(solution)/shard_map/ppermute | solution.py:179
  71.5 48.9 %collective-permute-start.5 = (bf16[8,32,256]{2,1,0:T(8,128)(2,1)}, bf16[8,32,256]{2,1,0:T(8,128)(2,1)S(1)}, u32[]{:S(2)}, u32[]{:S(2)}) collective-permute-start(bf16[8,32,256]{2,1,0:T(8,128)(2,1)} %get-tuple-element.42), channel_id=1, source_target_pairs={{0,16},{1,80},{2,144},{3,208},{4,272},{5,336},{6,400},{7,464},{8,2... | collective-permute-start | bytes 393224 | tf_op jit(solution)/shard_map/ppermute | solution.py:179
  75.0 45.5 %collective-permute-start.6 = (bf16[8,32,256]{2,1,0:T(8,128)(2,1)S(1)}, bf16[8,32,256]{2,1,0:T(8,128)(2,1)S(1)}, u32[]{:S(2)}, u32[]{:S(2)}) collective-permute-start(bf16[8,32,256]{2,1,0:T(8,128)(2,1)S(1)} %get-tuple-element.41), channel_id=1, source_target_pairs={{0,96},{1,32},{2,224},{3,160},{4,352},{5,288},{6,480},{7,416},{8,1... | collective-permute-start | bytes 393224 | tf_op jit(solution)/shard_map/ppermute | solution.py:179
  90.8 29.7 %collective-permute-start.7 = (bf16[8,32,256]{2,1,0:T(8,128)(2,1)S(1)}, bf16[8,32,256]{2,1,0:T(8,128)(2,1)S(1)}, u32[]{:S(2)}, u32[]{:S(2)}) collective-permute-start(bf16[8,32,256]{2,1,0:T(8,128)(2,1)S(1)} %get-tuple-element.40), channel_id=1, source_target_pairs={{0,48},{1,112},{2,176},{3,240},{4,304},{5,368},{6,432},{7,496},{8,... | collective-permute-start | bytes 393224 | tf_op jit(solution)/shard_map/ppermute | solution.py:179
  92.7 1.0 copy-start.4
  93.8 1.6 copy-start.5
  100.1 2.0 %copy-start = (bf16[4,1024,512]{2,1,0:T(8,128)(2,1)}, bf16[4,1024,512]{2,1,0:T(8,128)(2,1)S(1)}, u32[]{:S(2)}) copy-start(bf16[4,1024,512]{2,1,0:T(8,128)(2,1)S(1)} %get-tuple-element.34.refs_5_) | copy-start | bytes 12582916
  120.5 2.2 %copy-start.1 = (bf16[4,1024,512]{2,1,0:T(8,128)(2,1)S(1)}, bf16[4,1024,512]{2,1,0:T(8,128)(2,1)}, u32[]{:S(2)}) copy-start(bf16[4,1024,512]{2,1,0:T(8,128)(2,1)} %copy-done) | copy-start | bytes 12582916
  125.4 1.0 copy-start.2
  126.4 19.4 %all-to-all-start.2 = ((f32[4,264,256]{2,1,0:T(8,128)}), f32[4,264,256]{2,1,0:T(8,128)S(1)}, u32[]{:S(2)}, u32[]{:S(2)}) async-start(f32[4,264,256]{2,1,0:T(8,128)} %copy-done.2), calls=%async_computation.2 | async-start | bytes 2162688 | tf_op jit(solution)/shard_map/all_to_all | solution.py:193
  146.0 16.3 %collective-permute-start.8 = (f32[264,128]{1,0:T(8,128)S(1)}, f32[264,128]{1,0:T(8,128)S(1)}, u32[]{:S(2)}, u32[]{:S(2)}) collective-permute-start(f32[264,128]{1,0:T(8,128)S(1)} %fusion.1), channel_id=1, source_target_pairs={{0,1},{1,0},{2,3},{3,2},{4,5},{5,4},{6,7},{7,6},{8,9},{9,8},{10,11... | collective-permute-start | bytes 405512 | tf_op jit(solution)/shard_map/ppermute | solution.py:198

commit v4 on v1

--- a/solution.py
+++ b/solution.py
@@ -10,6 +10,8 @@
 
 AXES = ("x", "zl", "core", "y", "zh")
 SIZES = (4, 8, 2, 4, 2)
+HALVES = 2
+HALF = 32 // HALVES
 F32 = jnp.float32
 BF16 = jnp.bfloat16
 
@@ -95,22 +97,52 @@
     )(first, image, system)
 
 
+def pack_kernel(where_ref, p_ref, *refs):
+    l, zh = where_ref[0], where_ref[1]
+    sems = refs[HALVES]
+    copies = []
+    for half in range(HALVES):
+        rows = pl.ds(half * HALF, HALF)
+        for slot in range(8):
+            zl = (zh ^ (slot // 4)) * 4 + ((slot % 4 - l) & 3)
+            copies.append(pltpu.make_async_copy(p_ref.at[:, zl, :, rows], refs[half].at[slot], sems.at[half * 8 + slot]))
+    for copy in copies:
+        copy.start()
+    for copy in copies:
+        copy.wait()
+
+
+def pack(where, projections):
+    return pl.pallas_call(
+        pack_kernel,
+        in_specs=[pl.BlockSpec(memory_space=pltpu.SMEM), pl.BlockSpec(memory_space=pl.ANY)],
+        out_specs=[pl.BlockSpec(memory_space=pltpu.VMEM)] * HALVES,
+        out_shape=[jax.ShapeDtypeStruct((8, 4, 2, HALF, 256), BF16)] * HALVES,
+        scratch_shapes=[pltpu.SemaphoreType.DMA((8 * HALVES,))],
+        cost_estimate=pl.CostEstimate(flops=0, bytes_accessed=2097152, transcendentals=0),
+        compiler_params=pltpu.CompilerParams(vmem_limit_bytes=8 * 1024 * 1024),
+        name="pack",
+    )(where, projections.reshape(4, 8, 2, 32, 256))
+
+
 def finish_kernel(where_ref, *refs):
-    chunks, (a_ref, fwd_ref, rinv_ref, col_ref, res_ref, part_ref, held_ref) = refs[:8], refs[8:]
-    dh, dl = where_ref[0], where_ref[1]
+    parts, (a_ref, fwd_ref, rinv_ref, col_ref, res_ref, part_ref, held_ref) = refs[:HALVES], refs[HALVES:]
+    dh, dl, own_y = where_ref[0], where_ref[1], where_ref[2]
     for b in range(4):
-        g = dl ^ b
-        for a in range(2):
-            zh = dh ^ a
-            chunk = chunks[a * 4 + b]
-            for t in range(2):
-                rinv = rinv_ref[g, 0:1, t * 256 : (t + 1) * 256]
+        g = (b - dl) & 3
+        slot = (b ^ own_y) * 2
+        for t in range(2):
+            lanes = slice(t * 256, (t + 1) * 256)
+            rinv = rinv_ref[g, 0:1, lanes]
+            for a in range(2):
                 for y in range(4):
-                    rows = pl.ds(pl.multiple_of((y * 2 + zh) * 32, 32), 32)
-                    lanes = slice(t * 256, (t + 1) * 256)
-                    res = ((chunk[t * 4 + y].astype(F32) - fwd_ref[g, rows, lanes]) * rinv).astype(BF16)
-                    res_ref[g * 2 + t, rows, :] = res
-                    held_ref[rows, lanes] = res
+                    for half in range(HALVES):
+                        start = (y * 2 + (dh ^ a)) * 32 + half * HALF
+                        rows = pl.ds(pl.multiple_of(start, HALF), HALF)
+                        block = parts[half][slot + a, t * 4 + y].astype(F32)
+                        res = ((block - fwd_ref[g, rows, lanes]) * rinv).astype(BF16)
+                        res_ref[g * 2 + t, rows, :] = res
+                        held_ref[rows, lanes] = res
         for q in range(4):
             add = contract(held_ref[...], a_ref[g, q * 256 : (q + 1) * 256, :], 1, 1)
             if b == 0:
@@ -121,11 +153,11 @@
         part_ref[q, 256:264, :] = col_ref[:, q * 256 : (q + 1) * 256]
 
 
-def finish(where, chunks, a, fwd, rinv, col):
+def finish(where, parts, a, fwd, rinv, col):
     vmem = pl.BlockSpec(memory_space=pltpu.VMEM)
     return pl.pallas_call(
         finish_kernel,
-        in_specs=[pl.BlockSpec(memory_space=pltpu.SMEM)] + [vmem] * 12,
+        in_specs=[pl.BlockSpec(memory_space=pltpu.SMEM)] + [vmem] * (HALVES + 4),
         out_specs=[vmem, vmem],
         out_shape=[
             jax.ShapeDtypeStruct((8, 256, 256), BF16),
@@ -135,26 +167,31 @@
         cost_estimate=pl.CostEstimate(flops=1100000000, bytes_accessed=10000000, transcendentals=0),
         compiler_params=pltpu.CompilerParams(vmem_limit_bytes=40 * 1024 * 1024),
         name="finish",
-    )(where, *chunks, a, fwd, rinv, col)
+    )(where, *parts, a, fwd, rinv, col)
 
 
 def on_device(projections, start_image, system, first_tile):
-    zl, y, zh = lax.axis_index("zl"), lax.axis_index("y"), lax.axis_index("zh")
+    zl, y, zh = (lax.axis_index(name) for name in ("zl", "y", "zh"))
     dh, dl = zl // 4, zl % 4
-    sent = projections.reshape(4, 8, 2, 32, 256).transpose(2, 0, 1, 3, 4).reshape(8, 8, 32, 256)
-    sent = lax.all_to_all(sent, ("core", "y"), 0, 0, tiled=True)
-    chunks = []
-    for k in range(8):
-
-        def dest(x, zl, core, y, zh, k=k):
-            return (y, (zh * 4 + zl % 4) ^ k, core, x, zl // 4)
-
-        block = lax.dynamic_index_in_dim(sent, (zh * 4 + dl) ^ k, 1, keepdims=False)
-        chunks.append(lax.ppermute(block, AXES, pairs(dest)))
-    first_tile, image, system, _ = lax.optimization_barrier((first_tile, start_image, system, sent))
+    def dest(x, zl, core, y, zh):
+        return (x ^ y, (zh ^ core) * 4 + ((y - zl % 4) & 3), core, x, zl // 4)
+
+    parts = []
+    packed = pack(jnp.stack([dl, zh]), projections)
+    first_tile, image, system, packed = lax.optimization_barrier((first_tile, start_image, system, packed))
+    for part in packed:
+        part = part.reshape(8, 8, HALF, 256)
+        if parts:
+            part, parts[-1] = lax.optimization_barrier((part, parts[-1]))
+        parts.append(lax.all_to_all(part, ("core", "y"), 0, 0, tiled=True))
+    parts = [lax.ppermute(part.swapaxes(0, 1), AXES, pairs(dest)) for part in parts]
+    for n in range(HALVES):
+        if n:
+            parts[n], parts[n - 1] = lax.optimization_barrier((parts[n], parts[n - 1]))
+        parts[n] = lax.all_to_all(parts[n], ("x", "core"), 0, 0, tiled=True)
     a, fwd, rinv, col = prepare(first_tile, image, system)
-    where = jnp.stack([dh, dl]).astype(jnp.int32)
-    residual, part = finish(where, chunks, a, fwd, rinv, col)
+    where = jnp.stack([dh, dl, y]).astype(jnp.int32)
+    residual, part = finish(where, parts, a, fwd, rinv, col)
     part = lax.all_to_all(part, "y", 0, 0, tiled=True).sum(0)
     halves = jnp.stack([part[:, :128], part[:, 128:]])
     mine = lax.dynamic_index_in_dim(halves, zh, 0, keepdims=False)

time: 170 us -> 174 us (1.024)
  the two profiles are of different devices: /device:TPU:4 before, /device:TPU:162 now
where the time goes in v4:
time: 174 us; the launch traced here: 173 us
  waiting for transfers between devices  65.7 us (38%)
  starting transfers between devices  55.1 us (32%)
  blocking collectives  31.5 us (18%)
  Pallas kernels  9.16 us (5%)
  local copies, waits for them, and re-layouts  9.11 us (5%)
  other arithmetic  1.83 us (1%)
    ppermute x2, waiting for transfers between devices, on_device(): lax.ppermute(part.swapaxes(0, 1), AXES, pairs(dest))  41.2 us
    ppermute x1, starting transfers between devices, on_device(): total = mine + lax.ppermute(other, AXES, swap)  22.4 us
    ppermute x2, starting transfers between devices, on_device(): lax.ppermute(part.swapaxes(0, 1), AXES, pairs(dest))  18.9 us
    all_to_all x1, blocking collectives, on_device(): parts[n] = lax.all_to_all(parts[n], ('x', 'core'), 0, 0, tiled=True)  17.5 us
    all_to_all x1, waiting for transfers between devices, on_device(): part = lax.all_to_all(part, 'y', 0, 0, tiled=True).sum(0)  16 us
    all_to_all x1, blocking collectives, on_device(): parts.append(lax.all_to_all(part, ('core', 'y'), 0, 0, tiled=True))  14 us
    unnamed x14, local copies, waits for them, and re-layouts  9.01 us
    ppermute x1, waiting for transfers between devices, on_device(): total = mine + lax.ppermute(other, AXES, swap)  8.52 us
  transfers between devices with their start and end apart: 6, of which 4 were waited for; matrix products, arithmetic and copies ran while one was open for 0% of the time, Pallas kernels for 3%

profile of v4, /device:TPU:162, one launch (start us, length us, event | category | flops | bytes accessed | tf_op | source)
XLA Modules:
  0.0 173.3 jit_solution(167213037153728213)
XLA Ops:
  0.6 0.1 pad_add_fusion.1.where_ref
  0.7 0.0 copy-start.3
  0.7 1.2 copy-done.3
  1.9 1.7 pack.1
  3.7 14.0 %all_to_all.25 = bf16[8,8,16,256]{3,2,1,0:T(8,128)(2,1)S(1)} all-to-all(bf16[8,8,16,256]{3,2,1,0:T(8,128)(2,1)S(1)} %bitcast.26), channel_id=1, replica_groups=mesh['x'=4,'zl'=8,'core'=2,'y'=4,'zh'=2] {'core','y'}, dimensions={0} | all-to-all | bytes 1048576 | tf_op jit(solution)/shard_map/all_to_all | solution.py:186
  17.7 0.0 copy-start.6
  17.7 3.5 %all-to-all-start.1 = ((bf16[8,8,16,256]{3,2,1,0:T(8,128)(2,1)}), bf16[8,8,16,256]{3,2,1,0:T(8,128)(2,1)S(1)}, u32[]{:S(2)}, u32[]{:S(2)}) async-start(bf16[8,8,16,256]{3,2,1,0:T(8,128)(2,1)} %bitcast.5), calls=%async_computation.1 | async-start | bytes 1048576 | tf_op jit(solution)/shard_map/all_to_all | solution.py:186
  21.2 10.5 %collective-permute-start.1 = (bf16[8,8,16,256]{3,2,1,0:T(8,128)(2,1)S(1)}, bf16[8,8,16,256]{3,2,1,0:T(8,128)(2,1)S(1)}, u32[]{:S(2)}, u32[]{:S(2)}) collective-permute-start(bf16[8,8,16,256]{3,2,1,0:T(8,128)(2,1)S(1)} %bitcast.27), channel_id=1, source_target_pairs={{0,0},{1,64},{2,144},{3,208},{4,288},{5,352},{6,432},{7,496},{8,72... | collective-permute-start | bytes 1572872 | tf_op jit(solution)/shard_map/ppermute | solution.py:187
  31.7 0.0 all-to-all-done.1
  31.7 8.4 %collective-permute-start = (bf16[8,8,16,256]{3,2,1,0:T(8,128)(2,1)S(1)}, bf16[8,8,16,256]{3,2,1,0:T(8,128)(2,1)}, u32[]{:S(2)}, u32[]{:S(2)}) collective-permute-start(bf16[8,8,16,256]{3,2,1,0:T(8,128)(2,1)S(1)} %bitcast.28), channel_id=1, source_target_pairs={{0,0},{1,64},{2,144},{3,208},{4,288},{5,352},{6,432},{7,496},{8,72... | collective-permute-start | bytes 1572872 | tf_op jit(solution)/shard_map/ppermute | solution.py:187
  40.2 39.9 %collective-permute-done.1 = bf16[8,8,16,256]{3,2,1,0:T(8,128)(2,1)S(1)} collective-permute-done((bf16[8,8,16,256]{3,2,1,0:T(8,128)(2,1)S(1)}, bf16[8,8,16,256]{3,2,1,0:T(8,128)(2,1)S(1)}, u32[]{:S(2)}, u32[]{:S(2)}) %collective-permute-start.1) | collective-permute-done | bytes 524320 | tf_op jit(solution)/shard_map/ppermute | solution.py:187
  80.1 17.5 %all_to_all.26.refs_0_ = bf16[8,8,16,256]{3,2,1,0:T(8,128)(2,1)S(1)} all-to-all(bf16[8,8,16,256]{3,2,1,0:T(8,128)(2,1)S(1)} %collective-permute-done.1), channel_id=1, replica_groups=mesh['x'=4,'zl'=8,'core'=2,'y'=4,'zh'=2] {'x','core'}, dimensions={0} | all-to-all | bytes 1048576 | tf_op jit(solution)/shard_map/all_to_all | solution.py:191
  97.6 1.3 collective-permute-done
  98.9 6.8 %all-to-all-start.3 = ((bf16[8,8,16,256]{3,2,1,0:T(8,128)(2,1)}), bf16[8,8,16,256]{3,2,1,0:T(8,128)(2,1)S(1)}, u32[]{:S(2)}, u32[]{:S(2)}) async-start(bf16[8,8,16,256]{3,2,1,0:T(8,128)(2,1)} %collective-permute-done), calls=%async_computation.3 | async-start | bytes 1048576 | tf_op jit(solution)/shard_map/all_to_all | solution.py:191
  105.8 0.0 copy-done.6
  105.8 0.0 copy-start.4
  105.8 1.0 copy-done.4
  106.8 0.0 copy-start.5
  106.8 1.6 copy-done.5
  108.4 4.8 %prepare.1 = (bf16[4,1024,512]{2,1,0:T(8,128)(2,1)S(1)}, f32[4,256,512]{2,1,0:T(8,128)S(1)}, f32[4,8,512]{2,1,0:T(8,128)S(1)}, f32[8,1024]{1,0:T(8,128)S(1)}) custom-call(s32[4,16]{1,0:T(4,128)S(1)} %copy-done.6, bf16[256,1024]{1,0:T(8,128)(2,1)S(1)} %copy-done.4, bf16[4,16,2,64,128]{4,3,2,1,0:T(8,128)(2,1)S(1)} %copy-done.5), custom_call_target="tpu_custom_call" | custom-call | flops 1100000000 | bytes 10000000 | tf_op jit(solution)/shard_map/prepare/pallas_call | solution.py:74
  113.2 0.0 copy-start
  113.2 2.0 %copy-done = bf16[4,1024,512]{2,1,0:T(8,128)(2,1)} copy-done((bf16[4,1024,512]{2,1,0:T(8,128)(2,1)}, bf16[4,1024,512]{2,1,0:T(8,128)(2,1)S(1)}, u32[]{:S(2)}) %copy-start) | copy-done | bytes 4194328
  115.1 0.1 pad_add_fusion.where_ref
  115.2 0.0 all-to-all-done.3.refs_1_
  115.2 0.0 copy-start.1
  115.2 2.2 %copy-done.1 = bf16[4,1024,512]{2,1,0:T(8,128)(2,1)S(1)} copy-done((bf16[4,1024,512]{2,1,0:T(8,128)(2,1)S(1)}, bf16[4,1024,512]{2,1,0:T(8,128)(2,1)}, u32[]{:S(2)}) %copy-start.1) | copy-done | bytes 4194328
  117.4 2.7 %finish.1 = (bf16[8,256,256]{2,1,0:T(8,128)(2,1)}, f32[4,264,256]{2,1,0:T(8,128)S(1)}) custom-call(s32[3]{0:T(128)S(1)} %pad_add_fusion.where_ref, bf16[8,8,16,256]{3,2,1,0:T(8,128)(2,1)S(1)} %all_to_all.26.refs_0_, bf16[8,8,16,256]{3,2,1,0:T(8,128)(2,1)S(1)} %all-to-all-done.3.refs_1_, bf16[4,1024,512]{2,1,0:T(8,128)(2,1)S(1)} %copy-done.1, ...), custom_call_target="tpu_custom_call" | custom-call | flops 1100000000 | bytes 10000000 | tf_op jit(solution)/shard_map/finish/pallas_call | solution.py:158
  120.1 0.0 copy-start.2
  120.1 1.0 copy-done.2
  121.1 3.5 %all-to-all-start.4 = ((f32[4,264,256]{2,1,0:T(8,128)}), f32[4,264,256]{2,1,0:T(8,128)S(1)}, u32[]{:S(2)}, u32[]{:S(2)}) async-start(f32[4,264,256]{2,1,0:T(8,128)} %copy-done.2), calls=%async_computation.4 | async-start | bytes 2162688 | tf_op jit(solution)/shard_map/all_to_all | solution.py:195
  124.6 16.0 %all-to-all-done.4 = f32[4,264,256]{2,1,0:T(8,128)S(1)} async-done(((f32[4,264,256]{2,1,0:T(8,128)}), f32[4,264,256]{2,1,0:T(8,128)S(1)}, u32[]{:S(2)}, u32[]{:S(2)}) %all-to-all-start.4) | async-done | bytes 1081376 | tf_op jit(solution)/shard_map/all_to_all | solution.py:195
  140.6 0.1 reduce_sum.9
  140.8 22.4 %collective-permute-start.2 = (f32[264,128]{1,0:T(8,128)S(1)}, f32[264,128]{1,0:T(8,128)S(1)}, u32[]{:S(2)}, u32[]{:S(2)}) collective-permute-start(f32[264,128]{1,0:T(8,128)S(1)} %fusion.1), channel_id=1, source_target_pairs={{0,1},{1,0},{2,3},{3,2},{4,5},{5,4},{6,7},{7,6},{8,9},{9,8},{10,11... | collective-permute-start | bytes 405512 | tf_op jit(solution)/shard_map/ppermute | solution.py:200
  163.2 8.5 %collective-permute-done.2 = f32[264,128]{1,0:T(8,128)S(1)} collective-permute-done((f32[264,128]{1,0:T(8,128)S(1)}, f32[264,128]{1,0:T(8,128)S(1)}, u32[]{:S(2)}, u32[]{:S(2)}) %collective-permute-start.2) | collective-permute-done | bytes 135200 | tf_op jit(solution)/shard_map/ppermute | solution.py:200
  171.7 1.5 fusion.5
  (6 shorter events, 0.2 us)
Async XLA Ops:
  0.7 1.2 copy-start.3
  17.7 88.1 %copy-start.6 = (s32[4,16]{1,0:T(4,128)S(1)}, s32[4,16]{1,0:T(4,128)}, u32[]{:S(2)}) copy-start(s32[4,16]{1,0:T(4,128)} %first_ref) | copy-start | bytes 772
  17.7 14.0 %all-to-all-start.1 = ((bf16[8,8,16,256]{3,2,1,0:T(8,128)(2,1)}), bf16[8,8,16,256]{3,2,1,0:T(8,128)(2,1)S(1)}, u32[]{:S(2)}, u32[]{:S(2)}) async-start(bf16[8,8,16,256]{3,2,1,0:T(8,128)(2,1)} %bitcast.5), calls=%async_computation.1 | async-start | bytes 1048576 | tf_op jit(solution)/shard_map/all_to_all | solution.py:186
  21.2 58.8 %collective-permute-start.1 = (bf16[8,8,16,256]{3,2,1,0:T(8,128)(2,1)S(1)}, bf16[8,8,16,256]{3,2,1,0:T(8,128)(2,1)S(1)}, u32[]{:S(2)}, u32[]{:S(2)}) collective-permute-start(bf16[8,8,16,256]{3,2,1,0:T(8,128)(2,1)S(1)} %bitcast.27), channel_id=1, source_target_pairs={{0,0},{1,64},{2,144},{3,208},{4,288},{5,352},{6,432},{7,496},{8,72... | collective-permute-start | bytes 1572872 | tf_op jit(solution)/shard_map/ppermute | solution.py:187
  31.7 67.2 %collective-permute-start = (bf16[8,8,16,256]{3,2,1,0:T(8,128)(2,1)S(1)}, bf16[8,8,16,256]{3,2,1,0:T(8,128)(2,1)}, u32[]{:S(2)}, u32[]{:S(2)}) collective-permute-start(bf16[8,8,16,256]{3,2,1,0:T(8,128)(2,1)S(1)} %bitcast.28), channel_id=1, source_target_pairs={{0,0},{1,64},{2,144},{3,208},{4,288},{5,352},{6,432},{7,496},{8,72... | collective-permute-start | bytes 1572872 | tf_op jit(solution)/shard_map/ppermute | solution.py:187
  98.9 16.3 %all-to-all-start.3 = ((bf16[8,8,16,256]{3,2,1,0:T(8,128)(2,1)}), bf16[8,8,16,256]{3,2,1,0:T(8,128)(2,1)S(1)}, u32[]{:S(2)}, u32[]{:S(2)}) async-start(bf16[8,8,16,256]{3,2,1,0:T(8,128)(2,1)} %collective-permute-done), calls=%async_computation.3 | async-start | bytes 1048576 | tf_op jit(solution)/shard_map/all_to_all | solution.py:191
  105.8 1.0 copy-start.4
  106.8 1.6 copy-start.5
  113.2 2.0 %copy-start = (bf16[4,1024,512]{2,1,0:T(8,128)(2,1)}, bf16[4,1024,512]{2,1,0:T(8,128)(2,1)S(1)}, u32[]{:S(2)}) copy-start(bf16[4,1024,512]{2,1,0:T(8,128)(2,1)S(1)} %get-tuple-element.30.refs_2_) | copy-start | bytes 12582916
  115.2 2.2 %copy-start.1 = (bf16[4,1024,512]{2,1,0:T(8,128)(2,1)S(1)}, bf16[4,1024,512]{2,1,0:T(8,128)(2,1)}, u32[]{:S(2)}) copy-start(bf16[4,1024,512]{2,1,0:T(8,128)(2,1)} %copy-done) | copy-start | bytes 12582916
  120.1 1.0 copy-start.2
  121.1 19.5 %all-to-all-start.4 = ((f32[4,264,256]{2,1,0:T(8,128)}), f32[4,264,256]{2,1,0:T(8,128)S(1)}, u32[]{:S(2)}, u32[]{:S(2)}) async-start(f32[4,264,256]{2,1,0:T(8,128)} %copy-done.2), calls=%async_computation.4 | async-start | bytes 2162688 | tf_op jit(solution)/shard_map/all_to_all | solution.py:195
  140.8 30.9 %collective-permute-start.2 = (f32[264,128]{1,0:T(8,128)S(1)}, f32[264,128]{1,0:T(8,128)S(1)}, u32[]{:S(2)}, u32[]{:S(2)}) collective-permute-start(f32[264,128]{1,0:T(8,128)S(1)} %fusion.1), channel_id=1, source_target_pairs={{0,1},{1,0},{2,3},{3,2},{4,5},{5,4},{6,7},{7,6},{8,9},{9,8},{10,11... | collective-permute-start | bytes 405512 | tf_op jit(solution)/shard_map/ppermute | solution.py:200

commit v5 on v4

--- a/solution.py
+++ b/solution.py
@@ -12,6 +12,7 @@
 SIZES = (4, 8, 2, 4, 2)
 HALVES = 2
 HALF = 32 // HALVES
+VMEM_LIMIT = 60 * 1024 * 1024
 F32 = jnp.float32
 BF16 = jnp.bfloat16
 
@@ -92,7 +93,7 @@
             jax.ShapeDtypeStruct((8, 1024), F32),
         ],
         cost_estimate=pl.CostEstimate(flops=1100000000, bytes_accessed=10000000, transcendentals=0),
-        compiler_params=pltpu.CompilerParams(vmem_limit_bytes=40 * 1024 * 1024),
+        compiler_params=pltpu.CompilerParams(vmem_limit_bytes=VMEM_LIMIT),
         name="prepare",
     )(first, image, system)
 
@@ -104,7 +105,7 @@
     for half in range(HALVES):
         rows = pl.ds(half * HALF, HALF)
         for slot in range(8):
-            zl = (zh ^ (slot // 4)) * 4 + ((slot % 4 - l) & 3)
+            zl = (zh ^ (slot // 4)) * 4 + ((((slot % 4) ^ half) - l) & 3)
             copies.append(pltpu.make_async_copy(p_ref.at[:, zl, :, rows], refs[half].at[slot], sems.at[half * 8 + slot]))
     for copy in copies:
         copy.start()
@@ -120,7 +121,7 @@
         out_shape=[jax.ShapeDtypeStruct((8, 4, 2, HALF, 256), BF16)] * HALVES,
         scratch_shapes=[pltpu.SemaphoreType.DMA((8 * HALVES,))],
         cost_estimate=pl.CostEstimate(flops=0, bytes_accessed=2097152, transcendentals=0),
-        compiler_params=pltpu.CompilerParams(vmem_limit_bytes=8 * 1024 * 1024),
+        compiler_params=pltpu.CompilerParams(vmem_limit_bytes=VMEM_LIMIT),
         name="pack",
     )(where, projections.reshape(4, 8, 2, 32, 256))
 
@@ -128,44 +129,60 @@
 def finish_kernel(where_ref, *refs):
     parts, (a_ref, fwd_ref, rinv_ref, col_ref, res_ref, part_ref, held_ref) = refs[:HALVES], refs[HALVES:]
     dh, dl, own_y = where_ref[0], where_ref[1], where_ref[2]
-    for b in range(4):
-        g = (b - dl) & 3
-        slot = (b ^ own_y) * 2
-        for t in range(2):
-            lanes = slice(t * 256, (t + 1) * 256)
-            rinv = rinv_ref[g, 0:1, lanes]
-            for a in range(2):
-                for y in range(4):
-                    for half in range(HALVES):
-                        start = (y * 2 + (dh ^ a)) * 32 + half * HALF
-                        rows = pl.ds(pl.multiple_of(start, HALF), HALF)
-                        block = parts[half][slot + a, t * 4 + y].astype(F32)
-                        res = ((block - fwd_ref[g, rows, lanes]) * rinv).astype(BF16)
-                        res_ref[g * 2 + t, rows, :] = res
-                        held_ref[rows, lanes] = res
+    g = pl.program_id(0)
+    b = (g + dl) & 3
+    for t in range(2):
+        lanes = slice(t * 256, (t + 1) * 256)
+        rinv = rinv_ref[0, 0:1, lanes]
+        for a in range(2):
+            for y in range(4):
+                for half in range(HALVES):
+                    start = (y * 2 + (dh ^ a)) * 32 + half * HALF
+                    rows = pl.ds(pl.multiple_of(start, HALF), HALF)
+                    block = parts[half][(b ^ half ^ own_y) * 2 + a, t * 4 + y].astype(F32)
+                    res = ((block - fwd_ref[0, rows, lanes]) * rinv).astype(BF16)
+                    res_ref[t, rows, :] = res
+                    held_ref[rows, lanes] = res
+    adds = [contract(held_ref[...], a_ref[0, q * 256 : (q + 1) * 256, :], 1, 1) for q in range(4)]
+
+    @pl.when(g == 0)
+    def _():
+        row = lax.broadcasted_iota(jnp.int32, (16, 256), 0)
         for q in range(4):
-            add = contract(held_ref[...], a_ref[g, q * 256 : (q + 1) * 256, :], 1, 1)
-            if b == 0:
-                part_ref[q, 0:256, :] = add
-            else:
-                part_ref[q, 0:256, :] += add
-    for q in range(4):
-        part_ref[q, 256:264, :] = col_ref[:, q * 256 : (q + 1) * 256]
+            part_ref[q, 0:256, :] = adds[q]
+            cols = col_ref[0:1, q * 256 : (q + 1) * 256]
+            high = cols.astype(BF16).astype(F32)
+            part_ref[q, 256:272, :] = jnp.where(row == 0, high, jnp.where(row == 1, cols - high, 0.0))
+
+    @pl.when(g > 0)
+    def _():
+        for q in range(4):
+            part_ref[q, 0:256, :] += adds[q]
 
 
 def finish(where, parts, a, fwd, rinv, col):
-    vmem = pl.BlockSpec(memory_space=pltpu.VMEM)
     return pl.pallas_call(
         finish_kernel,
-        in_specs=[pl.BlockSpec(memory_space=pltpu.SMEM)] + [vmem] * (HALVES + 4),
-        out_specs=[vmem, vmem],
+        grid=(4,),
+        in_specs=[pl.BlockSpec(memory_space=pltpu.SMEM)]
+        + [pl.BlockSpec((8, 8, HALF, 256), lambda g: (0, 0, 0, 0))] * HALVES
+        + [
+            pl.BlockSpec((1, 1024, 512), lambda g: (g, 0, 0)),
+            pl.BlockSpec((1, 256, 512), lambda g: (g, 0, 0)),
+            pl.BlockSpec((1, 8, 512), lambda g: (g, 0, 0)),
+            pl.BlockSpec((8, 1024), lambda g: (0, 0)),
+        ],
+        out_specs=[
+            pl.BlockSpec((2, 256, 256), lambda g: (g, 0, 0)),
+            pl.BlockSpec((4, 272, 256), lambda g: (0, 0, 0)),
+        ],
         out_shape=[
             jax.ShapeDtypeStruct((8, 256, 256), BF16),
-            jax.ShapeDtypeStruct((4, 264, 256), F32),
+            jax.ShapeDtypeStruct((4, 272, 256), F32),
         ],
         scratch_shapes=[pltpu.VMEM((256, 512), BF16)],
         cost_estimate=pl.CostEstimate(flops=1100000000, bytes_accessed=10000000, transcendentals=0),
-        compiler_params=pltpu.CompilerParams(vmem_limit_bytes=40 * 1024 * 1024),
+        compiler_params=pltpu.CompilerParams(vmem_limit_bytes=VMEM_LIMIT),
         name="finish",
     )(where, *parts, a, fwd, rinv, col)
 
@@ -173,8 +190,11 @@
 def on_device(projections, start_image, system, first_tile):
     zl, y, zh = (lax.axis_index(name) for name in ("zl", "y", "zh"))
     dh, dl = zl // 4, zl % 4
-    def dest(x, zl, core, y, zh):
-        return (x ^ y, (zh ^ core) * 4 + ((y - zl % 4) & 3), core, x, zl // 4)
+    def send(part, half):
+        def dest(x, zl, core, y, zh):
+            return (x ^ y, (zh ^ core) * 4 + (((y ^ half) - zl % 4) & 3), core, x, zl // 4)
+
+        return lax.ppermute(part, AXES, pairs(dest))
 
     parts = []
     packed = pack(jnp.stack([dl, zh]), projections)
@@ -184,22 +204,26 @@
         if parts:
             part, parts[-1] = lax.optimization_barrier((part, parts[-1]))
         parts.append(lax.all_to_all(part, ("core", "y"), 0, 0, tiled=True))
-    parts = [lax.ppermute(part.swapaxes(0, 1), AXES, pairs(dest)) for part in parts]
+    parts = [send(part.swapaxes(0, 1), half) for half, part in enumerate(parts)]
+    a, fwd, rinv, col = prepare(first_tile, image, system)
+    parts[0], col = lax.optimization_barrier((parts[0], col))
     for n in range(HALVES):
         if n:
             parts[n], parts[n - 1] = lax.optimization_barrier((parts[n], parts[n - 1]))
         parts[n] = lax.all_to_all(parts[n], ("x", "core"), 0, 0, tiled=True)
-    a, fwd, rinv, col = prepare(first_tile, image, system)
     where = jnp.stack([dh, dl, y]).astype(jnp.int32)
     residual, part = finish(where, parts, a, fwd, rinv, col)
-    part = lax.all_to_all(part, "y", 0, 0, tiled=True).sum(0)
+    part = lax.all_to_all(part.astype(jnp.float16), "y", 0, 0, tiled=True).astype(F32).sum(0)
     halves = jnp.stack([part[:, :128], part[:, 128:]])
     mine = lax.dynamic_index_in_dim(halves, zh, 0, keepdims=False)
     other = lax.dynamic_index_in_dim(halves, 1 - zh, 0, keepdims=False)
+    cols = other[256:257] + other[257:258]
+    high = lax.reduce_precision(cols, 8, 7)
+    other = jnp.concatenate([other[:256], high, cols - high, jnp.zeros((14, 128), F32)]).astype(jnp.float16)
     swap = pairs(lambda x, zl, core, y, zh: (x, zl, core, y, 1 - zh))
-    total = mine + lax.ppermute(other, AXES, swap)
+    total = mine + lax.ppermute(other, AXES, swap).astype(F32)
     local = lax.dynamic_slice_in_dim(start_image, (y * 2 + zh) * 128, 128, 1).astype(F32)
-    new_image = local + total[:256] / total[256:257]
+    new_image = local + total[:256] / (total[256:257] + total[257:258])
     return new_image, residual
 
 

time: 174 us -> 165 us (0.948)
  the two profiles are of different devices: /device:TPU:162 before, /device:TPU:480 now
where the time goes in v5:
time: 165 us
  blocking collectives  71.5 us (43%)
  waiting for transfers between devices  49.5 us (30%)
  starting transfers between devices  20.1 us (12%)
  Pallas kernels  16.5 us (10%)
  other arithmetic  5.18 us (3%)
    all_to_all x1, blocking collectives, on_device(): parts[n] = lax.all_to_all(parts[n], ('x', 'core'), 0, 0, tiled=True)  57.3 us
    all_to_all x1, blocking collectives, on_device(): parts.append(lax.all_to_all(part, ('core', 'y'), 0, 0, tiled=True))  14.2 us
    ppermute x2, waiting for transfers between devices, send(): return lax.ppermute(part, AXES, pairs(dest))  12.3 us
    ppermute x1, waiting for transfers between devices, on_device(): total = mine + lax.ppermute(other, AXES, swap).astype(F32)  11.6 us
    all_to_all x1, waiting for transfers between devices, on_device(): lax.all_to_all(part.astype(jnp.float16), 'y', 0, 0, tiled=True).astype(F32)  9.78 us
    all_to_all x1, waiting for transfers between devices, on_device(): parts[n] = lax.all_to_all(parts[n], ('x', 'core'), 0, 0, tiled=True)  9.59 us
    pallas_call x1, Pallas kernels, prepare(): pl.pallas_call(prepare_kernel, grid=(4,), in_specs=[pl.BlockSpec(memory_s...  7.11 us
    pallas_call x1, Pallas kernels, finish(): pl.pallas_call(finish_kernel, grid=(4,), in_specs=[pl.BlockSpec(memory_sp...  6.38 us
  transfers between devices with their start and end apart: 6, of which 5 were waited for; matrix products, arithmetic and copies ran while one was open for 0% of the time, Pallas kernels for 4%

profile of v5, /device:TPU:480, one launch (start us, length us, event | category | flops | bytes accessed | tf_op | source)
XLA Modules:
  0.0 164.6 jit_solution(7059183141299032440)
XLA Ops:
  0.6 0.6 pad_add_fusion.1.where_ref
  1.2 3.0 %pack.1 = (bf16[8,4,2,16,256]{4,3,2,1,0:T(8,128)(2,1)}, bf16[8,4,2,16,256]{4,3,2,1,0:T(8,128)(2,1)}) custom-call(s32[2]{0:T(128)} %pad_add_fusion.1.where_ref, bf16[4,8,2,32,256]{4,3,2,1,0:T(8,128)(2,1)} %bitcast.31), custom_call_target="tpu_custom_call" | custom-call | bytes 2097152 | tf_op jit(solution)/shard_map/pack/pallas_call | solution.py:117
  4.3 14.2 %all_to_all.25 = bf16[8,8,16,256]{3,2,1,0:T(8,128)(2,1)S(1)} all-to-all(bf16[8,8,16,256]{3,2,1,0:T(8,128)(2,1)} %bitcast.35), channel_id=1, replica_groups=mesh['x'=4,'zl'=8,'core'=2,'y'=4,'zh'=2] {'core','y'}, dimensions={0} | all-to-all | bytes 1048576 | tf_op jit(solution)/shard_map/all_to_all | solution.py:206
  18.5 3.5 %all-to-all-start.1 = ((bf16[8,8,16,256]{3,2,1,0:T(8,128)(2,1)}), bf16[8,8,16,256]{3,2,1,0:T(8,128)(2,1)S(1)}, u32[]{:S(2)}, u32[]{:S(2)}) async-start(bf16[8,8,16,256]{3,2,1,0:T(8,128)(2,1)} %bitcast.34), calls=%async_computation.1 | async-start | bytes 1048576 | tf_op jit(solution)/shard_map/all_to_all | solution.py:206
  22.0 3.4 %collective-permute-start.1 = (bf16[8,8,16,256]{3,2,1,0:T(8,128)(2,1)S(1)}, bf16[8,8,16,256]{3,2,1,0:T(8,128)(2,1)S(1)}, u32[]{:S(2)}, u32[]{:S(2)}) collective-permute-start(bf16[8,8,16,256]{3,2,1,0:T(8,128)(2,1)S(1)} %bitcast.32), channel_id=1, source_target_pairs={{0,0},{1,64},{2,144},{3,208},{4,288},{5,352},{6,432},{7,496},{8,72... | collective-permute-start | bytes 1572872 | tf_op jit(solution)/shard_map/ppermute | solution.py:197
  25.4 6.2 %all-to-all-done.1 = bf16[8,8,16,256]{3,2,1,0:T(8,128)(2,1)S(1)} async-done(((bf16[8,8,16,256]{3,2,1,0:T(8,128)(2,1)}), bf16[8,8,16,256]{3,2,1,0:T(8,128)(2,1)S(1)}, u32[]{:S(2)}, u32[]{:S(2)}) %all-to-all-start.1) | async-done | bytes 524320 | tf_op jit(solution)/shard_map/all_to_all | solution.py:206
  31.7 2.9 %collective-permute-start = (bf16[8,8,16,256]{3,2,1,0:T(8,128)(2,1)S(1)}, bf16[8,8,16,256]{3,2,1,0:T(8,128)(2,1)}, u32[]{:S(2)}, u32[]{:S(2)}) collective-permute-start(bf16[8,8,16,256]{3,2,1,0:T(8,128)(2,1)S(1)} %bitcast.33), channel_id=1, source_target_pairs={{0,16},{1,80},{2,128},{3,192},{4,304},{5,368},{6,416},{7,480},{8,8... | collective-permute-start | bytes 1572872 | tf_op jit(solution)/shard_map/ppermute | solution.py:197
  34.6 7.1 %prepare.1 = (bf16[4,1024,512]{2,1,0:T(8,128)(2,1)}, f32[4,256,512]{2,1,0:T(8,128)}, f32[4,8,512]{2,1,0:T(8,128)}, f32[8,1024]{1,0:T(8,128)}) custom-call(s32[4,16]{1,0:T(4,128)} %first_ref, bf16[256,1024]{1,0:T(8,128)(2,1)} %image_ref, bf16[4,16,2,64,128]{4,3,2,1,0:T(8,128)(2,1)} %system_ref), custom_call_target="tpu_custom_call" | custom-call | flops 1100000000 | bytes 10000000 | tf_op jit(solution)/shard_map/prepare/pallas_call | solution.py:75
  41.7 12.3 %collective-permute-done.1 = bf16[8,8,16,256]{3,2,1,0:T(8,128)(2,1)S(1)} collective-permute-done((bf16[8,8,16,256]{3,2,1,0:T(8,128)(2,1)S(1)}, bf16[8,8,16,256]{3,2,1,0:T(8,128)(2,1)S(1)}, u32[]{:S(2)}, u32[]{:S(2)}) %collective-permute-start.1) | collective-permute-done | bytes 524320 | tf_op jit(solution)/shard_map/ppermute | solution.py:197
  54.0 57.3 %all_to_all.26.refs_0_ = bf16[8,8,16,256]{3,2,1,0:T(8,128)(2,1)} all-to-all(bf16[8,8,16,256]{3,2,1,0:T(8,128)(2,1)S(1)} %collective-permute-done.1), channel_id=1, replica_groups=mesh['x'=4,'zl'=8,'core'=2,'y'=4,'zh'=2] {'x','core'}, dimensions={0} | all-to-all | bytes 1048576 | tf_op jit(solution)/shard_map/all_to_all | solution.py:213
  111.3 0.0 collective-permute-done
  111.3 3.5 %all-to-all-start.3 = ((bf16[8,8,16,256]{3,2,1,0:T(8,128)(2,1)}), bf16[8,8,16,256]{3,2,1,0:T(8,128)(2,1)S(1)}, u32[]{:S(2)}, u32[]{:S(2)}) async-start(bf16[8,8,16,256]{3,2,1,0:T(8,128)(2,1)} %collective-permute-done), calls=%async_computation.3 | async-start | bytes 1048576 | tf_op jit(solution)/shard_map/all_to_all | solution.py:213
  114.9 0.7 pad_add_fusion.where_ref
  115.5 9.6 %all-to-all-done.3.refs_1_ = bf16[8,8,16,256]{3,2,1,0:T(8,128)(2,1)S(1)} async-done(((bf16[8,8,16,256]{3,2,1,0:T(8,128)(2,1)}), bf16[8,8,16,256]{3,2,1,0:T(8,128)(2,1)S(1)}, u32[]{:S(2)}, u32[]{:S(2)}) %all-to-all-start.3) | async-done | bytes 524320 | tf_op jit(solution)/shard_map/all_to_all | solution.py:213
  125.1 0.0 copy-start
  125.1 0.9 copy-done
  126.0 6.4 %finish.1 = (bf16[8,256,256]{2,1,0:T(8,128)(2,1)}, f32[4,272,256]{2,1,0:T(8,128)}) custom-call(s32[3]{0:T(128)} %pad_add_fusion.where_ref, bf16[8,8,16,256]{3,2,1,0:T(8,128)(2,1)} %all_to_all.26.refs_0_, bf16[8,8,16,256]{3,2,1,0:T(8,128)(2,1)} %copy-done, bf16[4,1024,512]{2,1,0:T(8,128)(2,1)} %get-tuple-element.34.refs_2_, ...), custom_call_target="tpu_custom_call" | custom-call | flops 1100000000 | bytes 10000000 | tf_op jit(solution)/shard_map/finish/pallas_call | solution.py:164
  132.3 2.1 %convert_element_type.14 = f16[4,272,256]{2,1,0:T(8,128)(2,1)} convert(f32[4,272,256]{2,1,0:T(8,128)} %get-tuple-element.38) | non-fusion elementwise | flops 278528 | bytes 1671168 | tf_op jit(solution)/shard_map/convert_element_type | solution.py:216
  134.5 3.5 %all-to-all-start.4 = ((f16[4,272,256]{2,1,0:T(8,128)(2,1)}), f16[4,272,256]{2,1,0:T(8,128)(2,1)S(1)}, u32[]{:S(2)}, u32[]{:S(2)}) async-start(f16[4,272,256]{2,1,0:T(8,128)(2,1)} %convert_element_type.14), calls=%async_computation.4 | async-start | bytes 1114112 | tf_op jit(solution)/shard_map/all_to_all | solution.py:216
  138.0 0.1 pad.3.clone
  138.0 9.8 %all-to-all-done.4 = f16[4,272,256]{2,1,0:T(8,128)(2,1)S(1)} async-done(((f16[4,272,256]{2,1,0:T(8,128)(2,1)}), f16[4,272,256]{2,1,0:T(8,128)(2,1)S(1)}, u32[]{:S(2)}, u32[]{:S(2)}) %all-to-all-start.4) | async-done | bytes 557088 | tf_op jit(solution)/shard_map/all_to_all | solution.py:216
  147.8 0.1 convert_reduce_fusion
  148.0 0.1 maximum_maximum_fusion
  148.1 3.3 %collective-permute-start.2 = (f16[272,128]{1,0:T(8,128)(2,1)S(1)}, f16[272,128]{1,0:T(8,128)(2,1)S(1)}, u32[]{:S(2)}, u32[]{:S(2)}) collective-permute-start(f16[272,128]{1,0:T(8,128)(2,1)S(1)} %maximum_maximum_fusion), channel_id=1, source_target_pairs={{0,1},{1,0},{2,3},{3,2},{4,5},{5,4},{6,7},{7,6},{8,9},{9,8},{10,11... | collective-permute-start | bytes 208904 | tf_op jit(solution)/shard_map/ppermute | solution.py:224
  151.5 11.6 %collective-permute-done.2 = f16[272,128]{1,0:T(8,128)(2,1)S(1)} collective-permute-done((f16[272,128]{1,0:T(8,128)(2,1)S(1)}, f16[272,128]{1,0:T(8,128)(2,1)S(1)}, u32[]{:S(2)}, u32[]{:S(2)}) %collective-permute-start.2) | collective-permute-done | bytes 69664 | tf_op jit(solution)/shard_map/ppermute | solution.py:224
  163.1 1.5 fusion.4
  (9 shorter events, 0.2 us)
Async XLA Ops:
  18.5 13.2 %all-to-all-start.1 = ((bf16[8,8,16,256]{3,2,1,0:T(8,128)(2,1)}), bf16[8,8,16,256]{3,2,1,0:T(8,128)(2,1)S(1)}, u32[]{:S(2)}, u32[]{:S(2)}) async-start(bf16[8,8,16,256]{3,2,1,0:T(8,128)(2,1)} %bitcast.34), calls=%async_computation.1 | async-start | bytes 1048576 | tf_op jit(solution)/shard_map/all_to_all | solution.py:206
  22.0 32.0 %collective-permute-start.1 = (bf16[8,8,16,256]{3,2,1,0:T(8,128)(2,1)S(1)}, bf16[8,8,16,256]{3,2,1,0:T(8,128)(2,1)S(1)}, u32[]{:S(2)}, u32[]{:S(2)}) collective-permute-start(bf16[8,8,16,256]{3,2,1,0:T(8,128)(2,1)S(1)} %bitcast.32), channel_id=1, source_target_pairs={{0,0},{1,64},{2,144},{3,208},{4,288},{5,352},{6,432},{7,496},{8,72... | collective-permute-start | bytes 1572872 | tf_op jit(solution)/shard_map/ppermute | solution.py:197
  31.7 79.6 %collective-permute-start = (bf16[8,8,16,256]{3,2,1,0:T(8,128)(2,1)S(1)}, bf16[8,8,16,256]{3,2,1,0:T(8,128)(2,1)}, u32[]{:S(2)}, u32[]{:S(2)}) collective-permute-start(bf16[8,8,16,256]{3,2,1,0:T(8,128)(2,1)S(1)} %bitcast.33), channel_id=1, source_target_pairs={{0,16},{1,80},{2,128},{3,192},{4,304},{5,368},{6,416},{7,480},{8,8... | collective-permute-start | bytes 1572872 | tf_op jit(solution)/shard_map/ppermute | solution.py:197
  111.3 13.8 %all-to-all-start.3 = ((bf16[8,8,16,256]{3,2,1,0:T(8,128)(2,1)}), bf16[8,8,16,256]{3,2,1,0:T(8,128)(2,1)S(1)}, u32[]{:S(2)}, u32[]{:S(2)}) async-start(bf16[8,8,16,256]{3,2,1,0:T(8,128)(2,1)} %collective-permute-done), calls=%async_computation.3 | async-start | bytes 1048576 | tf_op jit(solution)/shard_map/all_to_all | solution.py:213
  125.1 0.9 copy-start
  134.5 13.4 %all-to-all-start.4 = ((f16[4,272,256]{2,1,0:T(8,128)(2,1)}), f16[4,272,256]{2,1,0:T(8,128)(2,1)S(1)}, u32[]{:S(2)}, u32[]{:S(2)}) async-start(f16[4,272,256]{2,1,0:T(8,128)(2,1)} %convert_element_type.14), calls=%async_computation.4 | async-start | bytes 1114112 | tf_op jit(solution)/shard_map/all_to_all | solution.py:216
  148.1 14.9 %collective-permute-start.2 = (f16[272,128]{1,0:T(8,128)(2,1)S(1)}, f16[272,128]{1,0:T(8,128)(2,1)S(1)}, u32[]{:S(2)}, u32[]{:S(2)}) collective-permute-start(f16[272,128]{1,0:T(8,128)(2,1)S(1)} %maximum_maximum_fusion), channel_id=1, source_target_pairs={{0,1},{1,0},{2,3},{3,2},{4,5},{5,4},{6,7},{7,6},{8,9},{9,8},{10,11... | collective-permute-start | bytes 208904 | tf_op jit(solution)/shard_map/ppermute | solution.py:224

commit v6 on v5

--- a/solution.py
+++ b/solution.py
@@ -57,7 +57,11 @@
                     place == v, xt, 0.0
                 ).astype(BF16)
     a = a_ref[0]
-    fwd_ref[0] = contract(image_ref[...], a, 1, 0)
+    fwd = contract(image_ref[...], a, 1, 0)
+    for half in range(HALVES):
+        for group in range(8):
+            start = group * 32 + half * HALF
+            fwd_ref[0, half, group * HALF : (group + 1) * HALF, :] = fwd[start : start + HALF, :]
     rows = contract(jnp.ones((8, 1024), BF16), a, 1, 0)
     rinv_ref[0] = 1.0 / rows
     cols = contract(jnp.ones((8, 512), BF16), a, 1, 1)
@@ -82,17 +86,17 @@
         ],
         out_specs=[
             pl.BlockSpec((1, 1024, 512), lambda g: (g, 0, 0)),
-            pl.BlockSpec((1, 256, 512), lambda g: (g, 0, 0)),
+            pl.BlockSpec((1, HALVES, 8 * HALF, 512), lambda g: (g, 0, 0, 0)),
             pl.BlockSpec((1, 8, 512), lambda g: (g, 0, 0)),
             pl.BlockSpec((8, 1024), lambda g: (0, 0)),
         ],
         out_shape=[
             jax.ShapeDtypeStruct((4, 1024, 512), BF16),
-            jax.ShapeDtypeStruct((4, 256, 512), F32),
+            jax.ShapeDtypeStruct((4, HALVES, 8 * HALF, 512), F32),
             jax.ShapeDtypeStruct((4, 8, 512), F32),
             jax.ShapeDtypeStruct((8, 1024), F32),
         ],
-        cost_estimate=pl.CostEstimate(flops=1100000000, bytes_accessed=10000000, transcendentals=0),
+        cost_estimate=pl.CostEstimate(flops=100000, bytes_accessed=100000, transcendentals=0),
         compiler_params=pltpu.CompilerParams(vmem_limit_bytes=VMEM_LIMIT),
         name="prepare",
     )(first, image, system)
@@ -126,65 +130,77 @@
     )(where, projections.reshape(4, 8, 2, 32, 256))
 
 
-def finish_kernel(where_ref, *refs):
-    parts, (a_ref, fwd_ref, rinv_ref, col_ref, res_ref, part_ref, held_ref) = refs[:HALVES], refs[HALVES:]
+def finish_kernel(half, where_ref, chunk_ref, a_hbm, fwd_hbm, rinv_ref, col_ref, *refs):
+    res_hbm, part_hbm, a_ref, fwd_ref, res_ref, held_ref, part_ref, sems = refs[-8:]
     dh, dl, own_y = where_ref[0], where_ref[1], where_ref[2]
-    g = pl.program_id(0)
-    b = (g + dl) & 3
-    for t in range(2):
-        lanes = slice(t * 256, (t + 1) * 256)
-        rinv = rinv_ref[0, 0:1, lanes]
-        for a in range(2):
-            for y in range(4):
-                for half in range(HALVES):
-                    start = (y * 2 + (dh ^ a)) * 32 + half * HALF
-                    rows = pl.ds(pl.multiple_of(start, HALF), HALF)
-                    block = parts[half][(b ^ half ^ own_y) * 2 + a, t * 4 + y].astype(F32)
-                    res = ((block - fwd_ref[0, rows, lanes]) * rinv).astype(BF16)
-                    res_ref[t, rows, :] = res
-                    held_ref[rows, lanes] = res
-    adds = [contract(held_ref[...], a_ref[0, q * 256 : (q + 1) * 256, :], 1, 1) for q in range(4)]
-
-    @pl.when(g == 0)
-    def _():
-        row = lax.broadcasted_iota(jnp.int32, (16, 256), 0)
-        for q in range(4):
-            part_ref[q, 0:256, :] = adds[q]
+    copies = []
+    for g in range(4):
+        copies.append(pltpu.make_async_copy(fwd_hbm.at[g, half], fwd_ref.at[g], sems.at[g]))
+    for g in range(4):
+        copies.append(pltpu.make_async_copy(a_hbm.at[g], a_ref.at[g], sems.at[4 + g]))
+    for copy in copies:
+        copy.start()
+    for g in range(4):
+        b = (g + dl) & 3
+        copies[g].wait()
+        for t in range(2):
+            lanes = slice(t * 256, (t + 1) * 256)
+            rinv = rinv_ref[g, 0:1, lanes]
+            for a in range(2):
+                for y in range(4):
+                    group = y * 2 + (dh ^ a)
+                    rows = pl.ds(pl.multiple_of(group * HALF, HALF), HALF)
+                    block = chunk_ref[(b ^ half ^ own_y) * 2 + a, t * 4 + y].astype(F32)
+                    res = ((block - fwd_ref[g, rows, lanes]) * rinv).astype(BF16)
+                    res_ref[g * 2 + t, group] = res
+                    held_ref[g, rows, lanes] = res
+    out = pltpu.make_async_copy(res_ref, res_hbm.at[:, :, pl.ds(half * HALF, HALF)], sems.at[8])
+    out.start()
+    for copy in copies[4:]:
+        copy.wait()
+    for q in range(4):
+        total = contract(held_ref[0], a_ref[0, q * 256 : (q + 1) * 256, :], 1, 1)
+        for g in range(1, 4):
+            total += contract(held_ref[g], a_ref[g, q * 256 : (q + 1) * 256, :], 1, 1)
+        part_ref[q, 0 : 8 * HALF, :] = total
+        if half == 0:
+            row = lax.broadcasted_iota(jnp.int32, (16, 256), 0)
             cols = col_ref[0:1, q * 256 : (q + 1) * 256]
             high = cols.astype(BF16).astype(F32)
-            part_ref[q, 256:272, :] = jnp.where(row == 0, high, jnp.where(row == 1, cols - high, 0.0))
-
-    @pl.when(g > 0)
-    def _():
-        for q in range(4):
-            part_ref[q, 0:256, :] += adds[q]
-
-
-def finish(where, parts, a, fwd, rinv, col):
+            part_ref[q, 8 * HALF :, :] = jnp.where(row == 0, high, jnp.where(row == 1, cols - high, 0.0))
+    shares = [pltpu.make_async_copy(part_ref.at[:, 0 : 8 * HALF], part_hbm.at[:, pl.ds(half * 8 * HALF, 8 * HALF)], sems.at[9])]
+    if half == 0:
+        shares.append(pltpu.make_async_copy(part_ref.at[:, 8 * HALF :], part_hbm.at[:, 256:272], sems.at[10]))
+    for share in shares:
+        share.start()
+    for share in shares:
+        share.wait()
+    out.wait()
+
+
+def finish(half, where, chunk, a, fwd, rinv, col, before=()):
+    vmem, hbm = pl.BlockSpec(memory_space=pltpu.VMEM), pl.BlockSpec(memory_space=pl.ANY)
     return pl.pallas_call(
-        finish_kernel,
-        grid=(4,),
-        in_specs=[pl.BlockSpec(memory_space=pltpu.SMEM)]
-        + [pl.BlockSpec((8, 8, HALF, 256), lambda g: (0, 0, 0, 0))] * HALVES
-        + [
-            pl.BlockSpec((1, 1024, 512), lambda g: (g, 0, 0)),
-            pl.BlockSpec((1, 256, 512), lambda g: (g, 0, 0)),
-            pl.BlockSpec((1, 8, 512), lambda g: (g, 0, 0)),
-            pl.BlockSpec((8, 1024), lambda g: (0, 0)),
-        ],
-        out_specs=[
-            pl.BlockSpec((2, 256, 256), lambda g: (g, 0, 0)),
-            pl.BlockSpec((4, 272, 256), lambda g: (0, 0, 0)),
-        ],
+        functools.partial(finish_kernel, half),
+        in_specs=[pl.BlockSpec(memory_space=pltpu.SMEM), vmem, hbm, hbm, vmem, vmem] + [hbm] * len(before),
+        out_specs=[hbm, hbm],
         out_shape=[
-            jax.ShapeDtypeStruct((8, 256, 256), BF16),
+            jax.ShapeDtypeStruct((8, 8, 32, 256), BF16),
             jax.ShapeDtypeStruct((4, 272, 256), F32),
         ],
-        scratch_shapes=[pltpu.VMEM((256, 512), BF16)],
-        cost_estimate=pl.CostEstimate(flops=1100000000, bytes_accessed=10000000, transcendentals=0),
+        scratch_shapes=[
+            pltpu.VMEM((4, 1024, 512), BF16),
+            pltpu.VMEM((4, 8 * HALF, 512), F32),
+            pltpu.VMEM((8, 8, HALF, 256), BF16),
+            pltpu.VMEM((4, 8 * HALF, 512), BF16),
+            pltpu.VMEM((4, 8 * HALF + (16 if half == 0 else 0), 256), F32),
+            pltpu.SemaphoreType.DMA((11,)),
+        ],
+        input_output_aliases={6: 0, 7: 1} if before else {},
+        cost_estimate=pl.CostEstimate(flops=550000000, bytes_accessed=8000000, transcendentals=0),
         compiler_params=pltpu.CompilerParams(vmem_limit_bytes=VMEM_LIMIT),
-        name="finish",
-    )(where, *parts, a, fwd, rinv, col)
+        name=("finish_first", "finish_second")[half],
+    )(where, chunk, a, fwd, rinv, col, *before)
 
 
 def on_device(projections, start_image, system, first_tile):
@@ -196,23 +212,24 @@
 
         return lax.ppermute(part, AXES, pairs(dest))
 
-    parts = []
-    packed = pack(jnp.stack([dl, zh]), projections)
-    first_tile, image, system, packed = lax.optimization_barrier((first_tile, start_image, system, packed))
-    for part in packed:
-        part = part.reshape(8, 8, HALF, 256)
-        if parts:
-            part, parts[-1] = lax.optimization_barrier((part, parts[-1]))
-        parts.append(lax.all_to_all(part, ("core", "y"), 0, 0, tiled=True))
-    parts = [send(part.swapaxes(0, 1), half) for half, part in enumerate(parts)]
+    where = jnp.stack([dh, dl, y]).astype(jnp.int32)
+    first, second = pack(jnp.stack([dl, zh]), projections)
+    first = lax.all_to_all(first.reshape(8, 8, HALF, 256), ("core", "y"), 0, 0, tiled=True)
+    second, first = lax.optimization_barrier((second, first))
+    second = lax.all_to_all(second.reshape(8, 8, HALF, 256), ("core", "y"), 0, 0, tiled=True)
+    first = send(first.swapaxes(0, 1), 0)
+    first_tile, image, system, second = lax.optimization_barrier((first_tile, start_image, system, second))
     a, fwd, rinv, col = prepare(first_tile, image, system)
-    parts[0], col = lax.optimization_barrier((parts[0], col))
-    for n in range(HALVES):
-        if n:
-            parts[n], parts[n - 1] = lax.optimization_barrier((parts[n], parts[n - 1]))
-        parts[n] = lax.all_to_all(parts[n], ("x", "core"), 0, 0, tiled=True)
-    where = jnp.stack([dh, dl, y]).astype(jnp.int32)
-    residual, part = finish(where, parts, a, fwd, rinv, col)
+    second, col = lax.optimization_barrier((second, col))
+    second = send(second.swapaxes(0, 1), 1)
+    first, _ = lax.optimization_barrier((first, col))
+
+    first = lax.all_to_all(first, ("x", "core"), 0, 0, tiled=True)
+    second, first = lax.optimization_barrier((second, first))
+    done = finish(0, where, first, a, fwd, rinv, col)
+    second = lax.all_to_all(second, ("x", "core"), 0, 0, tiled=True)
+    residual, part = finish(1, where, second, a, fwd, rinv, col, done)
+
     part = lax.all_to_all(part.astype(jnp.float16), "y", 0, 0, tiled=True).astype(F32).sum(0)
     halves = jnp.stack([part[:, :128], part[:, 128:]])
     mine = lax.dynamic_index_in_dim(halves, zh, 0, keepdims=False)
@@ -222,9 +239,10 @@
     other = jnp.concatenate([other[:256], high, cols - high, jnp.zeros((14, 128), F32)]).astype(jnp.float16)
     swap = pairs(lambda x, zl, core, y, zh: (x, zl, core, y, 1 - zh))
     total = mine + lax.ppermute(other, AXES, swap).astype(F32)
+    update = total[:256] * (1.0 / (total[256:257] + total[257:258]))
+    update = update.reshape(HALVES, 8, HALF, 128).swapaxes(0, 1).reshape(256, 128)
     local = lax.dynamic_slice_in_dim(start_image, (y * 2 + zh) * 128, 128, 1).astype(F32)
-    new_image = local + total[:256] / (total[256:257] + total[257:258])
-    return new_image, residual
+    return local + update, residual.reshape(8, 256, 256)
 
 
 def solution(mesh):

time: 165 us -> 165 us (level)
  Pallas kernels: 16.5 us -> 22.4 us
  waiting for transfers between devices: 49.5 us -> 45.3 us
  blocking collectives: 71.5 us -> 69.6 us
    all_to_all x2, waiting for transfers between devices: 15.8 us -> 9.67 us  [the longest x1 6.24 us: on_device(): lax.all_to_all(second.reshape(8, 8, HALF, 256), ('core', 'y'), 0, 0, tile...]
    pallas_call x1 -> x2, Pallas kernels: 6.38 us -> 12.3 us  [finish(): pl.pallas_call(functools.partial(finish_kernel, half), in_specs=[pl.Block...]
    ppermute x2, waiting for transfers between devices: 12.3 us -> 14.3 us  [send(): return lax.ppermute(part, AXES, pairs(dest))]
    all_to_all x2, blocking collectives: 71.5 us -> 69.6 us  [the longest x1 55.4 us: on_device(): first = lax.all_to_all(first, ('x', 'core'), 0, 0, tiled=True)]
  transfers between devices with their start and end apart: 6 -> 6, of which waited for: 5 -> 5; matrix products, arithmetic and copies ran while one was open for 0% -> 0% of each run, Pallas kernels for 4% -> 8%
where the time goes in v6:
time: 165 us; the launch traced here: 164 us
  blocking collectives  69.6 us (42%)
  waiting for transfers between devices  45.3 us (27%)
  Pallas kernels  22.4 us (14%)
  starting transfers between devices  20.1 us (12%)
  other arithmetic  5.18 us (3%)
    all_to_all x1, blocking collectives, on_device(): first = lax.all_to_all(first, ('x', 'core'), 0, 0, tiled=True)  55.4 us
    ppermute x2, waiting for transfers between devices, send(): return lax.ppermute(part, AXES, pairs(dest))  14.3 us
    all_to_all x1, blocking collectives, on_device(): lax.all_to_all(first.reshape(8, 8, HALF, 256), ('core', 'y'), 0, 0, tiled...  14.2 us
    pallas_call x2, Pallas kernels, finish(): pl.pallas_call(functools.partial(finish_kernel, half), in_specs=[pl.Block...  12.3 us
    ppermute x1, waiting for transfers between devices, on_device(): total = mine + lax.ppermute(other, AXES, swap).astype(F32)  11.6 us
    all_to_all x1, waiting for transfers between devices, on_device(): lax.all_to_all(part.astype(jnp.float16), 'y', 0, 0, tiled=True).astype(F32)  9.77 us
    pallas_call x1, Pallas kernels, prepare(): pl.pallas_call(prepare_kernel, grid=(4,), in_specs=[pl.BlockSpec(memory_s...  7.08 us
    ppermute x2, starting transfers between devices, send(): return lax.ppermute(part, AXES, pairs(dest))  6.28 us
  transfers between devices with their start and end apart: 6, of which 5 were waited for; matrix products, arithmetic and copies ran while one was open for 0% of the time, Pallas kernels for 8%

profile of v6, /device:TPU:480, one launch (start us, length us, event | category | flops | bytes accessed | tf_op | source)
XLA Modules:
  0.0 164.3 jit_solution(715144317976560810)
XLA Ops:
  0.6 0.6 pad_add_fusion.1.where_ref
  1.2 3.0 %pack.1 = (bf16[8,4,2,16,256]{4,3,2,1,0:T(8,128)(2,1)}, bf16[8,4,2,16,256]{4,3,2,1,0:T(8,128)(2,1)}) custom-call(s32[2]{0:T(128)} %pad_add_fusion.1.where_ref, bf16[4,8,2,32,256]{4,3,2,1,0:T(8,128)(2,1)} %bitcast.38), custom_call_target="tpu_custom_call" | custom-call | bytes 2097152 | tf_op jit(solution)/shard_map/pack/pallas_call | solution.py:121
  4.3 14.2 %all_to_all.25 = bf16[8,8,16,256]{3,2,1,0:T(8,128)(2,1)S(1)} all-to-all(bf16[8,8,16,256]{3,2,1,0:T(8,128)(2,1)} %bitcast.42), channel_id=1, replica_groups=mesh['x'=4,'zl'=8,'core'=2,'y'=4,'zh'=2] {'core','y'}, dimensions={0} | all-to-all | bytes 1048576 | tf_op jit(solution)/shard_map/all_to_all | solution.py:217
  18.5 3.5 %all-to-all-start.1 = ((bf16[8,8,16,256]{3,2,1,0:T(8,128)(2,1)}), bf16[8,8,16,256]{3,2,1,0:T(8,128)(2,1)S(1)}, u32[]{:S(2)}, u32[]{:S(2)}) async-start(bf16[8,8,16,256]{3,2,1,0:T(8,128)(2,1)} %bitcast.40), calls=%async_computation.1 | async-start | bytes 1048576 | tf_op jit(solution)/shard_map/all_to_all | solution.py:219
  22.0 3.4 %collective-permute-start.1 = (bf16[8,8,16,256]{3,2,1,0:T(8,128)(2,1)S(1)}, bf16[8,8,16,256]{3,2,1,0:T(8,128)(2,1)S(1)}, u32[]{:S(2)}, u32[]{:S(2)}) collective-permute-start(bf16[8,8,16,256]{3,2,1,0:T(8,128)(2,1)S(1)} %bitcast.39), channel_id=1, source_target_pairs={{0,0},{1,64},{2,144},{3,208},{4,288},{5,352},{6,432},{7,496},{8,72... | collective-permute-start | bytes 1572872 | tf_op jit(solution)/shard_map/ppermute | solution.py:213
  25.4 6.2 %all-to-all-done.1 = bf16[8,8,16,256]{3,2,1,0:T(8,128)(2,1)S(1)} async-done(((bf16[8,8,16,256]{3,2,1,0:T(8,128)(2,1)}), bf16[8,8,16,256]{3,2,1,0:T(8,128)(2,1)S(1)}, u32[]{:S(2)}, u32[]{:S(2)}) %all-to-all-start.1) | async-done | bytes 524320 | tf_op jit(solution)/shard_map/all_to_all | solution.py:219
  31.6 7.1 %prepare.1 = (bf16[4,1024,512]{2,1,0:T(8,128)(2,1)}, f32[4,2,128,512]{3,2,1,0:T(8,128)}, f32[4,8,512]{2,1,0:T(8,128)}, f32[8,1024]{1,0:T(8,128)}) custom-call(s32[4,16]{1,0:T(4,128)} %first_ref, bf16[256,1024]{1,0:T(8,128)(2,1)} %image_ref, bf16[4,16,2,64,128]{4,3,2,1,0:T(8,128)(2,1)} %system_ref), custom_call_target="tpu_custom_call" | custom-call | flops 100000 | bytes 100000 | tf_op jit(solution)/shard_map/prepare/pallas_call | solution.py:79
  38.8 2.9 %collective-permute-start = (bf16[8,8,16,256]{3,2,1,0:T(8,128)(2,1)S(1)}, bf16[8,8,16,256]{3,2,1,0:T(8,128)(2,1)}, u32[]{:S(2)}, u32[]{:S(2)}) collective-permute-start(bf16[8,8,16,256]{3,2,1,0:T(8,128)(2,1)S(1)} %bitcast.41), channel_id=1, source_target_pairs={{0,16},{1,80},{2,128},{3,192},{4,304},{5,368},{6,416},{7,480},{8,8... | collective-permute-start | bytes 1572872 | tf_op jit(solution)/shard_map/ppermute | solution.py:213
  41.7 14.3 %collective-permute-done.1 = bf16[8,8,16,256]{3,2,1,0:T(8,128)(2,1)S(1)} collective-permute-done((bf16[8,8,16,256]{3,2,1,0:T(8,128)(2,1)S(1)}, bf16[8,8,16,256]{3,2,1,0:T(8,128)(2,1)S(1)}, u32[]{:S(2)}, u32[]{:S(2)}) %collective-permute-start.1) | collective-permute-done | bytes 524320 | tf_op jit(solution)/shard_map/ppermute | solution.py:213
  55.9 55.4 %all_to_all.26.chunk_ref = bf16[8,8,16,256]{3,2,1,0:T(8,128)(2,1)} all-to-all(bf16[8,8,16,256]{3,2,1,0:T(8,128)(2,1)S(1)} %collective-permute-done.1), channel_id=1, replica_groups=mesh['x'=4,'zl'=8,'core'=2,'y'=4,'zh'=2] {'x','core'}, dimensions={0} | all-to-all | bytes 1048576 | tf_op jit(solution)/shard_map/all_to_all | solution.py:227
  111.3 0.0 collective-permute-done
  111.3 3.5 %all-to-all-start.3 = ((bf16[8,8,16,256]{3,2,1,0:T(8,128)(2,1)}), bf16[8,8,16,256]{3,2,1,0:T(8,128)(2,1)S(1)}, u32[]{:S(2)}, u32[]{:S(2)}) async-start(bf16[8,8,16,256]{3,2,1,0:T(8,128)(2,1)} %collective-permute-done), calls=%async_computation.3 | async-start | bytes 1048576 | tf_op jit(solution)/shard_map/all_to_all | solution.py:230
  114.8 0.7 pad_add_fusion.where_ref
  115.5 6.2 %finish_first.1 = (bf16[8,8,32,256]{3,2,1,0:T(8,128)(2,1)}, f32[4,272,256]{2,1,0:T(8,128)}) custom-call(s32[3]{0:T(128)} %pad_add_fusion.where_ref, bf16[8,8,16,256]{3,2,1,0:T(8,128)(2,1)} %all_to_all.26.chunk_ref, bf16[4,1024,512]{2,1,0:T(8,128)(2,1)} %get-tuple-element.36.a_hbm, f32[4,2,128,512]{3,2,1,0:T(8,128)} %get-tuple-element.37.fwd_hbm, ...), custom_call_target="tpu_custom_call" | custom-call | flops 550000000 | bytes 8000000 | tf_op jit(solution)/shard_map/finish_first/pallas_call | solution.py:183
  121.7 3.4 %all-to-all-done.3.chunk_ref = bf16[8,8,16,256]{3,2,1,0:T(8,128)(2,1)S(1)} async-done(((bf16[8,8,16,256]{3,2,1,0:T(8,128)(2,1)}), bf16[8,8,16,256]{3,2,1,0:T(8,128)(2,1)S(1)}, u32[]{:S(2)}, u32[]{:S(2)}) %all-to-all-start.3) | async-done | bytes 524320 | tf_op jit(solution)/shard_map/all_to_all | solution.py:230
  125.1 0.0 copy-start
  125.1 0.8 copy-done
  125.9 6.2 %finish_second.1 = (bf16[8,8,32,256]{3,2,1,0:T(8,128)(2,1)}, f32[4,272,256]{2,1,0:T(8,128)}) custom-call(s32[3]{0:T(128)} %pad_add_fusion.where_ref, bf16[8,8,16,256]{3,2,1,0:T(8,128)(2,1)} %copy-done, bf16[4,1024,512]{2,1,0:T(8,128)(2,1)} %get-tuple-element.36.a_hbm, ...), custom_call_target="tpu_custom_call", output_to_operand_aliasing={{0}: (6, {}), {1}: (7, {})} | custom-call | flops 550000000 | bytes 8000000 | tf_op jit(solution)/shard_map/finish_second/pallas_call | solution.py:183
  132.1 2.1 %convert_element_type.14 = f16[4,272,256]{2,1,0:T(8,128)(2,1)} convert(f32[4,272,256]{2,1,0:T(8,128)} %get-tuple-element.42) | non-fusion elementwise | flops 278528 | bytes 1671168 | tf_op jit(solution)/shard_map/convert_element_type | solution.py:233
  134.2 3.5 %all-to-all-start.4 = ((f16[4,272,256]{2,1,0:T(8,128)(2,1)}), f16[4,272,256]{2,1,0:T(8,128)(2,1)S(1)}, u32[]{:S(2)}, u32[]{:S(2)}) async-start(f16[4,272,256]{2,1,0:T(8,128)(2,1)} %convert_element_type.14), calls=%async_computation.4 | async-start | bytes 1114112 | tf_op jit(solution)/shard_map/all_to_all | solution.py:233
  137.7 0.1 pad.3.clone
  137.8 9.8 %all-to-all-done.4 = f16[4,272,256]{2,1,0:T(8,128)(2,1)S(1)} async-done(((f16[4,272,256]{2,1,0:T(8,128)(2,1)}), f16[4,272,256]{2,1,0:T(8,128)(2,1)S(1)}, u32[]{:S(2)}, u32[]{:S(2)}) %all-to-all-start.4) | async-done | bytes 557088 | tf_op jit(solution)/shard_map/all_to_all | solution.py:233
  147.5 0.1 convert_reduce_fusion
  147.7 0.1 maximum_maximum_fusion
  147.8 3.3 %collective-permute-start.2 = (f16[272,128]{1,0:T(8,128)(2,1)S(1)}, f16[272,128]{1,0:T(8,128)(2,1)S(1)}, u32[]{:S(2)}, u32[]{:S(2)}) collective-permute-start(f16[272,128]{1,0:T(8,128)(2,1)S(1)} %maximum_maximum_fusion), channel_id=1, source_target_pairs={{0,1},{1,0},{2,3},{3,2},{4,5},{5,4},{6,7},{7,6},{8,9},{9,8},{10,11... | collective-permute-start | bytes 208904 | tf_op jit(solution)/shard_map/ppermute | solution.py:241
  151.2 11.6 %collective-permute-done.2 = f16[272,128]{1,0:T(8,128)(2,1)S(1)} collective-permute-done((f16[272,128]{1,0:T(8,128)(2,1)S(1)}, f16[272,128]{1,0:T(8,128)(2,1)S(1)}, u32[]{:S(2)}, u32[]{:S(2)}) %collective-permute-start.2) | collective-permute-done | bytes 69664 | tf_op jit(solution)/shard_map/ppermute | solution.py:241
  162.8 1.5 bitcast_add_fusion
  (11 shorter events, 0.2 us)
Async XLA Ops:
  18.5 13.2 %all-to-all-start.1 = ((bf16[8,8,16,256]{3,2,1,0:T(8,128)(2,1)}), bf16[8,8,16,256]{3,2,1,0:T(8,128)(2,1)S(1)}, u32[]{:S(2)}, u32[]{:S(2)}) async-start(bf16[8,8,16,256]{3,2,1,0:T(8,128)(2,1)} %bitcast.40), calls=%async_computation.1 | async-start | bytes 1048576 | tf_op jit(solution)/shard_map/all_to_all | solution.py:219
  22.0 33.9 %collective-permute-start.1 = (bf16[8,8,16,256]{3,2,1,0:T(8,128)(2,1)S(1)}, bf16[8,8,16,256]{3,2,1,0:T(8,128)(2,1)S(1)}, u32[]{:S(2)}, u32[]{:S(2)}) collective-permute-start(bf16[8,8,16,256]{3,2,1,0:T(8,128)(2,1)S(1)} %bitcast.39), channel_id=1, source_target_pairs={{0,0},{1,64},{2,144},{3,208},{4,288},{5,352},{6,432},{7,496},{8,72... | collective-permute-start | bytes 1572872 | tf_op jit(solution)/shard_map/ppermute | solution.py:213
  38.8 72.6 %collective-permute-start = (bf16[8,8,16,256]{3,2,1,0:T(8,128)(2,1)S(1)}, bf16[8,8,16,256]{3,2,1,0:T(8,128)(2,1)}, u32[]{:S(2)}, u32[]{:S(2)}) collective-permute-start(bf16[8,8,16,256]{3,2,1,0:T(8,128)(2,1)S(1)} %bitcast.41), channel_id=1, source_target_pairs={{0,16},{1,80},{2,128},{3,192},{4,304},{5,368},{6,416},{7,480},{8,8... | collective-permute-start | bytes 1572872 | tf_op jit(solution)/shard_map/ppermute | solution.py:213
  111.3 13.8 %all-to-all-start.3 = ((bf16[8,8,16,256]{3,2,1,0:T(8,128)(2,1)}), bf16[8,8,16,256]{3,2,1,0:T(8,128)(2,1)S(1)}, u32[]{:S(2)}, u32[]{:S(2)}) async-start(bf16[8,8,16,256]{3,2,1,0:T(8,128)(2,1)} %collective-permute-done), calls=%async_computation.3 | async-start | bytes 1048576 | tf_op jit(solution)/shard_map/all_to_all | solution.py:230
  125.1 0.8 copy-start
  134.2 13.3 %all-to-all-start.4 = ((f16[4,272,256]{2,1,0:T(8,128)(2,1)}), f16[4,272,256]{2,1,0:T(8,128)(2,1)S(1)}, u32[]{:S(2)}, u32[]{:S(2)}) async-start(f16[4,272,256]{2,1,0:T(8,128)(2,1)} %convert_element_type.14), calls=%async_computation.4 | async-start | bytes 1114112 | tf_op jit(solution)/shard_map/all_to_all | solution.py:233
  147.8 14.9 %collective-permute-start.2 = (f16[272,128]{1,0:T(8,128)(2,1)S(1)}, f16[272,128]{1,0:T(8,128)(2,1)S(1)}, u32[]{:S(2)}, u32[]{:S(2)}) collective-permute-start(f16[272,128]{1,0:T(8,128)(2,1)S(1)} %maximum_maximum_fusion), channel_id=1, source_target_pairs={{0,1},{1,0},{2,3},{3,2},{4,5},{5,4},{6,7},{7,6},{8,9},{9,8},{10,11... | collective-permute-start | bytes 208904 | tf_op jit(solution)/shard_map/ppermute | solution.py:241

commit v7 on v3

--- a/solution.py
+++ b/solution.py
@@ -90,7 +90,7 @@
             jax.ShapeDtypeStruct((8, 1024), F32),
         ],
         cost_estimate=pl.CostEstimate(flops=1100000000, bytes_accessed=10000000, transcendentals=0),
-        compiler_params=pltpu.CompilerParams(vmem_limit_bytes=40 * 1024 * 1024),
+        compiler_params=pltpu.CompilerParams(vmem_limit_bytes=24 * 1024 * 1024),
         name="prepare",
     )(first, image, system)
 
@@ -147,8 +147,11 @@
                 part_ref[q, 0:256, :] = add
             else:
                 part_ref[q, 0:256, :] += add
+    row = lax.broadcasted_iota(jnp.int32, (16, 256), 0)
     for q in range(4):
-        part_ref[q, 256:264, :] = col_ref[:, q * 256 : (q + 1) * 256]
+        cols = col_ref[0:1, q * 256 : (q + 1) * 256]
+        high = cols.astype(BF16).astype(F32)
+        part_ref[q, 256:272, :] = jnp.where(row == 0, high, jnp.where(row == 1, cols - high, 0.0))
 
 
 def finish(where, near, far, a, fwd, rinv, col):
@@ -159,11 +162,11 @@
         out_specs=[vmem, vmem],
         out_shape=[
             jax.ShapeDtypeStruct((8, 256, 256), BF16),
-            jax.ShapeDtypeStruct((4, 264, 256), F32),
+            jax.ShapeDtypeStruct((4, 272, 256), F32),
         ],
         scratch_shapes=[pltpu.VMEM((256, 512), BF16)],
         cost_estimate=pl.CostEstimate(flops=1100000000, bytes_accessed=10000000, transcendentals=0),
-        compiler_params=pltpu.CompilerParams(vmem_limit_bytes=40 * 1024 * 1024),
+        compiler_params=pltpu.CompilerParams(vmem_limit_bytes=24 * 1024 * 1024),
         name="finish",
     )(where, near, *far, a, fwd, rinv, col)
 
@@ -190,14 +193,17 @@
     a, fwd, rinv, col = prepare(first_tile, image, system)
     where = jnp.stack([dh, dl, y]).astype(jnp.int32)
     residual, part = finish(where, near, far, a, fwd, rinv, col)
-    part = lax.all_to_all(part, "y", 0, 0, tiled=True).sum(0)
+    part = lax.all_to_all(part.astype(jnp.float16), "y", 0, 0, tiled=True).astype(F32).sum(0)
     halves = jnp.stack([part[:, :128], part[:, 128:]])
     mine = lax.dynamic_index_in_dim(halves, zh, 0, keepdims=False)
     other = lax.dynamic_index_in_dim(halves, 1 - zh, 0, keepdims=False)
+    cols = other[256:257] + other[257:258]
+    high = lax.reduce_precision(cols, 8, 7)
+    other = jnp.concatenate([other[:256], high, cols - high, jnp.zeros((14, 128), F32)]).astype(jnp.float16)
     swap = pairs(lambda x, zl, core, y, zh: (x, zl, core, y, 1 - zh))
-    total = mine + lax.ppermute(other, AXES, swap)
+    total = mine + lax.ppermute(other, AXES, swap).astype(F32)
     local = lax.dynamic_slice_in_dim(start_image, (y * 2 + zh) * 128, 128, 1).astype(F32)
-    new_image = local + total[:256] / total[256:257]
+    new_image = local + total[:256] / (total[256:257] + total[257:258])
     return new_image, residual
 
 

time: 165 us -> 157 us (0.952)
  waiting for transfers between devices: 60.7 us -> 53.6 us
    all_to_all x1, waiting for transfers between devices: 15.9 us -> 10.2 us  [on_device(): lax.all_to_all(part.astype(jnp.float16), 'y', 0, 0, tiled=True).astype(F32)]
    unnamed x14 -> x12, local copies, waits for them, and re-layouts: 9.02 us -> 7.99 us
  transfers between devices with their start and end apart: 12 -> 12, of which waited for: 5 -> 5; matrix products, arithmetic and copies ran while one was open for 0% -> 1% of each run, Pallas kernels for 3% -> 3%
where the time goes in v7:
time: 157 us; the launch traced here: 156 us
  starting transfers between devices  80.3 us (51%)
  waiting for transfers between devices  53.6 us (34%)
  local copies, waits for them, and re-layouts  8.84 us (6%)
  Pallas kernels  8.79 us (6%)
  other arithmetic  3.71 us (2%)
    ppermute x8, starting transfers between devices, send(): return lax.ppermute(block, AXES, pairs(dest))  65.6 us
    ppermute x8, waiting for transfers between devices, send(): return lax.ppermute(block, AXES, pairs(dest))  30.4 us
    ppermute x1, waiting for transfers between devices, on_device(): total = mine + lax.ppermute(other, AXES, swap).astype(F32)  13 us
    all_to_all x1, waiting for transfers between devices, on_device(): lax.all_to_all(part.astype(jnp.float16), 'y', 0, 0, tiled=True).astype(F32)  10.2 us
    unnamed x12, local copies, waits for them, and re-layouts  7.99 us
    all_to_all x1, starting transfers between devices, on_device(): near = lax.all_to_all(near, ('x', 'core'), 0, 0, tiled=True)  4.8 us
    pallas_call x1, Pallas kernels, prepare(): pl.pallas_call(prepare_kernel, grid=(4,), in_specs=[pl.BlockSpec(memory_s...  4.78 us
    all_to_all x1, starting transfers between devices, on_device(): lax.all_to_all(far.reshape(8, 4, 32, 256), ('core', 'y'), 0, 0, tiled=True)  4.48 us
  transfers between devices with their start and end apart: 12, of which 5 were waited for; matrix products, arithmetic and copies ran while one was open for 1% of the time, Pallas kernels for 3%

profile of v7, /device:TPU:4, one launch (start us, length us, event | category | flops | bytes accessed | tf_op | source)
XLA Modules:
  0.0 156.1 jit_solution(4960366575827746087)
XLA Ops:
  0.6 0.1 pad_add_fusion.1.where_ref
  0.7 0.0 copy-start.2
  0.7 1.2 copy-done.2
  1.9 2.1 %pack.1 = (bf16[4,2,32,256]{3,2,1,0:T(8,128)(2,1)S(1)}, bf16[4,2,32,256]{3,2,1,0:T(8,128)(2,1)S(1)}, bf16[4,2,32,256]{3,2,1,0:T(8,128)(2,1)S(1)}, bf16[4,2,32,25...) custom-call(s32[3]{0:T(128)S(1)} %pad_add_fusion.1.where_ref, bf16[4,8,2,32,256]{4,3,2,1,0:T(8,128)(2,1)S(1)} %bitcast.41), custom_call_target="tpu_custom_call" | custom-call | bytes 2097152 | tf_op jit(solution)/shard_map/pack/pallas_call | solution.py:116
  4.0 0.0 copy-start.5
  4.0 4.5 %all-to-all-start = ((bf16[8,4,32,256]{3,2,1,0:T(8,128)(2,1)}), bf16[8,4,32,256]{3,2,1,0:T(8,128)(2,1)S(1)}, u32[]{:S(2)}, u32[]{:S(2)}) async-start(bf16[8,4,32,256]{3,2,1,0:T(8,128)(2,1)} %bitcast.10), calls=%async_computation | async-start | bytes 1048576 | tf_op jit(solution)/shard_map/all_to_all | solution.py:187
  8.5 5.4 %collective-permute-start = (bf16[8,32,256]{2,1,0:T(8,128)(2,1)S(1)}, bf16[8,32,256]{2,1,0:T(8,128)(2,1)S(1)}, u32[]{:S(2)}, u32[]{:S(2)}) collective-permute-start(bf16[8,32,256]{2,1,0:T(8,128)(2,1)S(1)} %bitcast.45), channel_id=1, source_target_pairs={{0,0},{1,64},{2,128},{3,192},{4,256},{5,320},{6,384},{7,448},{8,8}... | collective-permute-start | bytes 393224 | tf_op jit(solution)/shard_map/ppermute | solution.py:182
  14.0 17.9 %collective-permute-start.1 = (bf16[8,32,256]{2,1,0:T(8,128)(2,1)S(1)}, bf16[8,32,256]{2,1,0:T(8,128)(2,1)S(1)}, u32[]{:S(2)}, u32[]{:S(2)}) collective-permute-start(bf16[8,32,256]{2,1,0:T(8,128)(2,1)S(1)} %bitcast.44), channel_id=1, source_target_pairs={{0,80},{1,16},{2,208},{3,144},{4,336},{5,272},{6,464},{7,400},{8,8... | collective-permute-start | bytes 393224 | tf_op jit(solution)/shard_map/ppermute | solution.py:182
  31.9 5.3 %collective-permute-start.2 = (bf16[8,32,256]{2,1,0:T(8,128)(2,1)S(1)}, bf16[8,32,256]{2,1,0:T(8,128)(2,1)S(1)}, u32[]{:S(2)}, u32[]{:S(2)}) collective-permute-start(bf16[8,32,256]{2,1,0:T(8,128)(2,1)S(1)} %bitcast.43), channel_id=1, source_target_pairs={{0,32},{1,96},{2,160},{3,224},{4,288},{5,352},{6,416},{7,480},{8,4... | collective-permute-start | bytes 393224 | tf_op jit(solution)/shard_map/ppermute | solution.py:182
  37.2 5.0 %collective-permute-start.3 = (bf16[8,32,256]{2,1,0:T(8,128)(2,1)S(1)}, bf16[8,32,256]{2,1,0:T(8,128)(2,1)S(1)}, u32[]{:S(2)}, u32[]{:S(2)}) collective-permute-start(bf16[8,32,256]{2,1,0:T(8,128)(2,1)S(1)} %bitcast.42), channel_id=1, source_target_pairs={{0,112},{1,48},{2,240},{3,176},{4,368},{5,304},{6,496},{7,432},{8,... | collective-permute-start | bytes 393224 | tf_op jit(solution)/shard_map/ppermute | solution.py:182
  42.2 0.0 collective-permute-done
  42.2 0.0 collective-permute-done.1
  42.2 5.5 %collective-permute-done.2 = bf16[8,32,256]{2,1,0:T(8,128)(2,1)S(1)} collective-permute-done((bf16[8,32,256]{2,1,0:T(8,128)(2,1)S(1)}, bf16[8,32,256]{2,1,0:T(8,128)(2,1)S(1)}, u32[]{:S(2)}, u32[]{:S(2)}) %collective-permute-start.2) | collective-permute-done | bytes 131104 | tf_op jit(solution)/shard_map/ppermute | solution.py:182
  47.7 6.6 %collective-permute-done.3 = bf16[8,32,256]{2,1,0:T(8,128)(2,1)S(1)} collective-permute-done((bf16[8,32,256]{2,1,0:T(8,128)(2,1)S(1)}, bf16[8,32,256]{2,1,0:T(8,128)(2,1)S(1)}, u32[]{:S(2)}, u32[]{:S(2)}) %collective-permute-start.3) | collective-permute-done | bytes 131104 | tf_op jit(solution)/shard_map/ppermute | solution.py:182
  54.3 0.0 all-to-all-done
  54.3 0.9 pad_maximum_fusion
  55.1 4.8 %all-to-all-start.1 = ((bf16[8,4,32,256]{3,2,1,0:T(8,128)(2,1)}), bf16[8,4,32,256]{3,2,1,0:T(8,128)(2,1)S(1)}, u32[]{:S(2)}, u32[]{:S(2)}) async-start(bf16[8,4,32,256]{3,2,1,0:T(8,128)(2,1)} %pad_maximum_fusion), calls=%async_computation.1 | async-start | bytes 1048576 | tf_op jit(solution)/shard_map/all_to_all | solution.py:192
  59.9 0.7 dynamic-slice_bitcast_fusion
  60.7 10.9 %collective-permute-start.4 = (bf16[8,32,256]{2,1,0:T(8,128)(2,1)}, bf16[8,32,256]{2,1,0:T(8,128)(2,1)S(1)}, u32[]{:S(2)}, u32[]{:S(2)}) collective-permute-start(bf16[8,32,256]{2,1,0:T(8,128)(2,1)} %get-tuple-element.43), channel_id=1, source_target_pairs={{0,64},{1,0},{2,192},{3,128},{4,320},{5,256},{6,448},{7,384},{8,72... | collective-permute-start | bytes 393224 | tf_op jit(solution)/shard_map/ppermute | solution.py:182
  71.5 3.5 %collective-permute-start.5 = (bf16[8,32,256]{2,1,0:T(8,128)(2,1)}, bf16[8,32,256]{2,1,0:T(8,128)(2,1)S(1)}, u32[]{:S(2)}, u32[]{:S(2)}) collective-permute-start(bf16[8,32,256]{2,1,0:T(8,128)(2,1)} %get-tuple-element.42), channel_id=1, source_target_pairs={{0,16},{1,80},{2,144},{3,208},{4,272},{5,336},{6,400},{7,464},{8,2... | collective-permute-start | bytes 393224 | tf_op jit(solution)/shard_map/ppermute | solution.py:182
  75.0 15.7 %collective-permute-start.6 = (bf16[8,32,256]{2,1,0:T(8,128)(2,1)S(1)}, bf16[8,32,256]{2,1,0:T(8,128)(2,1)S(1)}, u32[]{:S(2)}, u32[]{:S(2)}) collective-permute-start(bf16[8,32,256]{2,1,0:T(8,128)(2,1)S(1)} %get-tuple-element.41), channel_id=1, source_target_pairs={{0,96},{1,32},{2,224},{3,160},{4,352},{5,288},{6,480},{7,416},{8,1... | collective-permute-start | bytes 393224 | tf_op jit(solution)/shard_map/ppermute | solution.py:182
  90.8 1.9 %collective-permute-start.7 = (bf16[8,32,256]{2,1,0:T(8,128)(2,1)S(1)}, bf16[8,32,256]{2,1,0:T(8,128)(2,1)S(1)}, u32[]{:S(2)}, u32[]{:S(2)}) collective-permute-start(bf16[8,32,256]{2,1,0:T(8,128)(2,1)S(1)} %get-tuple-element.40), channel_id=1, source_target_pairs={{0,48},{1,112},{2,176},{3,240},{4,304},{5,368},{6,432},{7,496},{8,... | collective-permute-start | bytes 393224 | tf_op jit(solution)/shard_map/ppermute | solution.py:182
  92.7 0.0 copy-done.5
  92.7 0.0 copy-start.3
  92.7 1.0 copy-done.3
  93.8 0.0 copy-start.4
  93.8 1.6 %copy-done.4 = bf16[4,16,2,64,128]{4,3,2,1,0:T(8,128)(2,1)S(1)} copy-done((bf16[4,16,2,64,128]{4,3,2,1,0:T(8,128)(2,1)S(1)}, bf16[4,16,2,64,128]{4,3,2,1,0:T(8,128)(2,1)}, u32[]{:S(2)}) %copy-start.4) | copy-done | bytes 2097176
  95.3 4.8 %prepare.1 = (bf16[4,1024,512]{2,1,0:T(8,128)(2,1)S(1)}, f32[4,256,512]{2,1,0:T(8,128)S(1)}, f32[4,8,512]{2,1,0:T(8,128)S(1)}, f32[8,1024]{1,0:T(8,128)S(1)}) custom-call(s32[4,16]{1,0:T(4,128)S(1)} %copy-done.5, bf16[256,1024]{1,0:T(8,128)(2,1)S(1)} %copy-done.3, bf16[4,16,2,64,128]{4,3,2,1,0:T(8,128)(2,1)S(1)} %copy-done.4), custom_call_target="tpu_custom_call" | custom-call | flops 1100000000 | bytes 10000000 | tf_op jit(solution)/shard_map/prepare/pallas_call | solution.py:72
  100.1 0.0 copy-start
  100.2 2.0 %copy-done = bf16[4,1024,512]{2,1,0:T(8,128)(2,1)} copy-done((bf16[4,1024,512]{2,1,0:T(8,128)(2,1)}, bf16[4,1024,512]{2,1,0:T(8,128)(2,1)S(1)}, u32[]{:S(2)}) %copy-start) | copy-done | bytes 4194328
  102.1 0.1 pad_add_fusion.where_ref
  102.2 18.3 %collective-permute-done.4.refs_1_ = bf16[8,32,256]{2,1,0:T(8,128)(2,1)S(1)} collective-permute-done((bf16[8,32,256]{2,1,0:T(8,128)(2,1)}, bf16[8,32,256]{2,1,0:T(8,128)(2,1)S(1)}, u32[]{:S(2)}, u32[]{:S(2)}) %collective-permute-start.4) | collective-permute-done | bytes 131104 | tf_op jit(solution)/shard_map/ppermute | solution.py:182
  120.5 0.0 collective-permute-done.5.refs_2_
  120.5 0.0 collective-permute-done.6.refs_3_
  120.5 0.0 collective-permute-done.7.refs_4_
  120.5 0.0 all-to-all-done.1.refs_0_
  120.5 0.0 copy-start.1
  120.5 2.2 %copy-done.1 = bf16[4,1024,512]{2,1,0:T(8,128)(2,1)S(1)} copy-done((bf16[4,1024,512]{2,1,0:T(8,128)(2,1)S(1)}, bf16[4,1024,512]{2,1,0:T(8,128)(2,1)}, u32[]{:S(2)}) %copy-start.1) | copy-done | bytes 4194328
  122.7 1.9 %finish.1 = (bf16[8,256,256]{2,1,0:T(8,128)(2,1)}, f32[4,272,256]{2,1,0:T(8,128)S(1)}) custom-call(s32[3]{0:T(128)S(1)} %pad_add_fusion.where_ref, bf16[8,4,32,256]{3,2,1,0:T(8,128)(2,1)S(1)} %all-to-all-done.1.refs_0_, bf16[8,32,256]{2,1,0:T(8,128)(2,1)S(1)} %collective-permute-done.4.refs_1_, bf16[8,32,256]{2,1,0:T(8,128)(2,1)S(1)} %collective-permute-done.5.refs_2_, ...), custom_call_target="tpu_custom_call" | custom-call | flops 1100000000 | bytes 10000000 | tf_op jit(solution)/shard_map/finish/pallas_call | solution.py:159
  124.6 0.9 convert_element_type.14
  125.5 3.5 %all-to-all-start.2 = ((f16[4,272,256]{2,1,0:T(8,128)(2,1)}), f16[4,272,256]{2,1,0:T(8,128)(2,1)S(1)}, u32[]{:S(2)}, u32[]{:S(2)}) async-start(f16[4,272,256]{2,1,0:T(8,128)(2,1)} %convert_element_type.14), calls=%async_computation.2 | async-start | bytes 1114112 | tf_op jit(solution)/shard_map/all_to_all | solution.py:196
  129.0 0.1 pad.3.clone
  129.1 10.2 %all-to-all-done.2 = f16[4,272,256]{2,1,0:T(8,128)(2,1)S(1)} async-done(((f16[4,272,256]{2,1,0:T(8,128)(2,1)}), f16[4,272,256]{2,1,0:T(8,128)(2,1)S(1)}, u32[]{:S(2)}, u32[]{:S(2)}) %all-to-all-start.2) | async-done | bytes 557088 | tf_op jit(solution)/shard_map/all_to_all | solution.py:196
  139.3 0.1 convert_reduce_fusion
  139.5 0.1 maximum_maximum_fusion
  139.6 1.9 %collective-permute-start.8 = (f16[272,128]{1,0:T(8,128)(2,1)S(1)}, f16[272,128]{1,0:T(8,128)(2,1)S(1)}, u32[]{:S(2)}, u32[]{:S(2)}) collective-permute-start(f16[272,128]{1,0:T(8,128)(2,1)S(1)} %maximum_maximum_fusion), channel_id=1, source_target_pairs={{0,1},{1,0},{2,3},{3,2},{4,5},{5,4},{6,7},{7,6},{8,9},{9,8},{10,11... | collective-permute-start | bytes 208904 | tf_op jit(solution)/shard_map/ppermute | solution.py:204
  141.5 13.0 %collective-permute-done.8 = f16[272,128]{1,0:T(8,128)(2,1)S(1)} collective-permute-done((f16[272,128]{1,0:T(8,128)(2,1)S(1)}, f16[272,128]{1,0:T(8,128)(2,1)S(1)}, u32[]{:S(2)}, u32[]{:S(2)}) %collective-permute-start.8) | collective-permute-done | bytes 69664 | tf_op jit(solution)/shard_map/ppermute | solution.py:204
  154.6 1.5 fusion.4
  (7 shorter events, 0.1 us)
Async XLA Ops:
  0.7 1.2 copy-start.2
  4.0 88.7 %copy-start.5 = (s32[4,16]{1,0:T(4,128)S(1)}, s32[4,16]{1,0:T(4,128)}, u32[]{:S(2)}) copy-start(s32[4,16]{1,0:T(4,128)} %first_ref) | copy-start | bytes 772
  4.0 50.2 %all-to-all-start = ((bf16[8,4,32,256]{3,2,1,0:T(8,128)(2,1)}), bf16[8,4,32,256]{3,2,1,0:T(8,128)(2,1)S(1)}, u32[]{:S(2)}, u32[]{:S(2)}) async-start(bf16[8,4,32,256]{3,2,1,0:T(8,128)(2,1)} %bitcast.10), calls=%async_computation | async-start | bytes 1048576 | tf_op jit(solution)/shard_map/all_to_all | solution.py:187
  8.5 33.6 %collective-permute-start = (bf16[8,32,256]{2,1,0:T(8,128)(2,1)S(1)}, bf16[8,32,256]{2,1,0:T(8,128)(2,1)S(1)}, u32[]{:S(2)}, u32[]{:S(2)}) collective-permute-start(bf16[8,32,256]{2,1,0:T(8,128)(2,1)S(1)} %bitcast.45), channel_id=1, source_target_pairs={{0,0},{1,64},{2,128},{3,192},{4,256},{5,320},{6,384},{7,448},{8,8}... | collective-permute-start | bytes 393224 | tf_op jit(solution)/shard_map/ppermute | solution.py:182
  14.0 28.2 %collective-permute-start.1 = (bf16[8,32,256]{2,1,0:T(8,128)(2,1)S(1)}, bf16[8,32,256]{2,1,0:T(8,128)(2,1)S(1)}, u32[]{:S(2)}, u32[]{:S(2)}) collective-permute-start(bf16[8,32,256]{2,1,0:T(8,128)(2,1)S(1)} %bitcast.44), channel_id=1, source_target_pairs={{0,80},{1,16},{2,208},{3,144},{4,336},{5,272},{6,464},{7,400},{8,8... | collective-permute-start | bytes 393224 | tf_op jit(solution)/shard_map/ppermute | solution.py:182
  31.9 15.8 %collective-permute-start.2 = (bf16[8,32,256]{2,1,0:T(8,128)(2,1)S(1)}, bf16[8,32,256]{2,1,0:T(8,128)(2,1)S(1)}, u32[]{:S(2)}, u32[]{:S(2)}) collective-permute-start(bf16[8,32,256]{2,1,0:T(8,128)(2,1)S(1)} %bitcast.43), channel_id=1, source_target_pairs={{0,32},{1,96},{2,160},{3,224},{4,288},{5,352},{6,416},{7,480},{8,4... | collective-permute-start | bytes 393224 | tf_op jit(solution)/shard_map/ppermute | solution.py:182
  37.2 17.1 %collective-permute-start.3 = (bf16[8,32,256]{2,1,0:T(8,128)(2,1)S(1)}, bf16[8,32,256]{2,1,0:T(8,128)(2,1)S(1)}, u32[]{:S(2)}, u32[]{:S(2)}) collective-permute-start(bf16[8,32,256]{2,1,0:T(8,128)(2,1)S(1)} %bitcast.42), channel_id=1, source_target_pairs={{0,112},{1,48},{2,240},{3,176},{4,368},{5,304},{6,496},{7,432},{8,... | collective-permute-start | bytes 393224 | tf_op jit(solution)/shard_map/ppermute | solution.py:182
  55.1 65.4 %all-to-all-start.1 = ((bf16[8,4,32,256]{3,2,1,0:T(8,128)(2,1)}), bf16[8,4,32,256]{3,2,1,0:T(8,128)(2,1)S(1)}, u32[]{:S(2)}, u32[]{:S(2)}) async-start(bf16[8,4,32,256]{3,2,1,0:T(8,128)(2,1)} %pad_maximum_fusion), calls=%async_computation.1 | async-start | bytes 1048576 | tf_op jit(solution)/shard_map/all_to_all | solution.py:192
  60.7 59.8 %collective-permute-start.4 = (bf16[8,32,256]{2,1,0:T(8,128)(2,1)}, bf16[8,32,256]{2,1,0:T(8,128)(2,1)S(1)}, u32[]{:S(2)}, u32[]{:S(2)}) collective-permute-start(bf16[8,32,256]{2,1,0:T(8,128)(2,1)} %get-tuple-element.43), channel_id=1, source_target_pairs={{0,64},{1,0},{2,192},{3,128},{4,320},{5,256},{6,448},{7,384},{8,72... | collective-permute-start | bytes 393224 | tf_op jit(solution)/shard_map/ppermute | solution.py:182
  71.5 48.9 %collective-permute-start.5 = (bf16[8,32,256]{2,1,0:T(8,128)(2,1)}, bf16[8,32,256]{2,1,0:T(8,128)(2,1)S(1)}, u32[]{:S(2)}, u32[]{:S(2)}) collective-permute-start(bf16[8,32,256]{2,1,0:T(8,128)(2,1)} %get-tuple-element.42), channel_id=1, source_target_pairs={{0,16},{1,80},{2,144},{3,208},{4,272},{5,336},{6,400},{7,464},{8,2... | collective-permute-start | bytes 393224 | tf_op jit(solution)/shard_map/ppermute | solution.py:182
  75.0 45.5 %collective-permute-start.6 = (bf16[8,32,256]{2,1,0:T(8,128)(2,1)S(1)}, bf16[8,32,256]{2,1,0:T(8,128)(2,1)S(1)}, u32[]{:S(2)}, u32[]{:S(2)}) collective-permute-start(bf16[8,32,256]{2,1,0:T(8,128)(2,1)S(1)} %get-tuple-element.41), channel_id=1, source_target_pairs={{0,96},{1,32},{2,224},{3,160},{4,352},{5,288},{6,480},{7,416},{8,1... | collective-permute-start | bytes 393224 | tf_op jit(solution)/shard_map/ppermute | solution.py:182
  90.8 29.7 %collective-permute-start.7 = (bf16[8,32,256]{2,1,0:T(8,128)(2,1)S(1)}, bf16[8,32,256]{2,1,0:T(8,128)(2,1)S(1)}, u32[]{:S(2)}, u32[]{:S(2)}) collective-permute-start(bf16[8,32,256]{2,1,0:T(8,128)(2,1)S(1)} %get-tuple-element.40), channel_id=1, source_target_pairs={{0,48},{1,112},{2,176},{3,240},{4,304},{5,368},{6,432},{7,496},{8,... | collective-permute-start | bytes 393224 | tf_op jit(solution)/shard_map/ppermute | solution.py:182
  92.7 1.0 copy-start.3
  93.8 1.6 %copy-start.4 = (bf16[4,16,2,64,128]{4,3,2,1,0:T(8,128)(2,1)S(1)}, bf16[4,16,2,64,128]{4,3,2,1,0:T(8,128)(2,1)}, u32[]{:S(2)}) copy-start(bf16[4,16,2,64,128]{4,3,2,1,0:T(8,128)(2,1)} %system_ref) | copy-start | bytes 6291460
  100.1 2.0 %copy-start = (bf16[4,1024,512]{2,1,0:T(8,128)(2,1)}, bf16[4,1024,512]{2,1,0:T(8,128)(2,1)S(1)}, u32[]{:S(2)}) copy-start(bf16[4,1024,512]{2,1,0:T(8,128)(2,1)S(1)} %get-tuple-element.34.refs_5_) | copy-start | bytes 12582916
  120.5 2.2 %copy-start.1 = (bf16[4,1024,512]{2,1,0:T(8,128)(2,1)S(1)}, bf16[4,1024,512]{2,1,0:T(8,128)(2,1)}, u32[]{:S(2)}) copy-start(bf16[4,1024,512]{2,1,0:T(8,128)(2,1)} %copy-done) | copy-start | bytes 12582916
  125.5 13.8 %all-to-all-start.2 = ((f16[4,272,256]{2,1,0:T(8,128)(2,1)}), f16[4,272,256]{2,1,0:T(8,128)(2,1)S(1)}, u32[]{:S(2)}, u32[]{:S(2)}) async-start(f16[4,272,256]{2,1,0:T(8,128)(2,1)} %convert_element_type.14), calls=%async_computation.2 | async-start | bytes 1114112 | tf_op jit(solution)/shard_map/all_to_all | solution.py:196
  139.6 14.9 %collective-permute-start.8 = (f16[272,128]{1,0:T(8,128)(2,1)S(1)}, f16[272,128]{1,0:T(8,128)(2,1)S(1)}, u32[]{:S(2)}, u32[]{:S(2)}) collective-permute-start(f16[272,128]{1,0:T(8,128)(2,1)S(1)} %maximum_maximum_fusion), channel_id=1, source_target_pairs={{0,1},{1,0},{2,3},{3,2},{4,5},{5,4},{6,7},{7,6},{8,9},{9,8},{10,11... | collective-permute-start | bytes 208904 | tf_op jit(solution)/shard_map/ppermute | solution.py:204

commit v8 on v7

--- a/solution.py
+++ b/solution.py
@@ -10,12 +10,18 @@
 
 AXES = ("x", "zl", "core", "y", "zh")
 SIZES = (4, 8, 2, 4, 2)
+NEAR = (0, 1, 2, 3)
+FAR = (5, 4, 7, 6)
 F32 = jnp.float32
 BF16 = jnp.bfloat16
 
 
 def index_of(x, zl, core, y, zh):
     return (((x * 8 + zl) * 2 + core) * 4 + y) * 2 + zh
+
+
+def mixed(place):
+    return place ^ ((place & 1) * 4)
 
 
 def pairs(dest):
@@ -95,49 +101,55 @@
     )(first, image, system)
 
 
-def pack_kernel(where_ref, p_ref, n0_ref, n1_ref, n2_ref, n3_ref, far_ref, sems):
-    x, dl, zh = where_ref[0], where_ref[1], where_ref[2]
+def pack_kernel(p_ref, *refs):
+    far_ref, sems = refs[-2:]
+    x, place = lax.axis_index("x"), lax.axis_index("zh") * 4 + lax.rem(lax.axis_index("zl"), 4)
     copies = []
-    for b, near_ref in enumerate((n0_ref, n1_ref, n2_ref, n3_ref)):
-        low = dl ^ b
-        copies.append(pltpu.make_async_copy(p_ref.at[:, (zh ^ (low & 1)) * 4 + low], near_ref, sems.at[b]))
-    for m in range(4):
-        for low in range(4):
-            src = p_ref.at[x ^ m, (zh ^ (low & 1) ^ 1) * 4 + low]
-            copies.append(pltpu.make_async_copy(src, far_ref.at[:, m, low], sems.at[4 + m * 4 + low]))
+    for n, k in enumerate(NEAR):
+        copies.append(pltpu.make_async_copy(p_ref.at[:, mixed(place ^ k)], refs[n], sems.at[n]))
+    for n, k in enumerate(FAR):
+        for m in range(4):
+            sem = sems.at[len(NEAR) + n * 4 + m]
+            copies.append(pltpu.make_async_copy(p_ref.at[x ^ m, mixed(place ^ k)], far_ref.at[:, m, n], sem))
     for copy in copies:
         copy.start()
     for copy in copies:
         copy.wait()
 
 
-def pack(where, projections):
+def pack(projections):
     vmem = pl.BlockSpec(memory_space=pltpu.VMEM)
     return pl.pallas_call(
         pack_kernel,
-        in_specs=[pl.BlockSpec(memory_space=pltpu.SMEM), pl.BlockSpec(memory_space=pl.ANY)],
-        out_specs=[vmem] * 5,
-        out_shape=[jax.ShapeDtypeStruct((4, 2, 32, 256), BF16)] * 4 + [jax.ShapeDtypeStruct((2, 4, 4, 32, 256), BF16)],
-        scratch_shapes=[pltpu.SemaphoreType.DMA((20,))],
+        in_specs=[pl.BlockSpec(memory_space=pl.ANY)],
+        out_specs=[vmem] * (len(NEAR) + 1),
+        out_shape=[jax.ShapeDtypeStruct((4, 2, 32, 256), BF16)] * len(NEAR)
+        + [jax.ShapeDtypeStruct((2, 4, len(FAR), 32, 256), BF16)],
+        scratch_shapes=[pltpu.SemaphoreType.DMA((len(NEAR) + 4 * len(FAR),))],
         cost_estimate=pl.CostEstimate(flops=0, bytes_accessed=2097152, transcendentals=0),
-        compiler_params=pltpu.CompilerParams(vmem_limit_bytes=8 * 1024 * 1024),
+        compiler_params=pltpu.CompilerParams(vmem_limit_bytes=60 * 1024 * 1024),
         name="pack",
-    )(where.astype(jnp.int32), projections.reshape(4, 8, 2, 32, 256))
+    )(projections.reshape(4, 8, 2, 32, 256))
 
 
 def finish_kernel(where_ref, *refs):
-    near_ref, far_refs, (a_ref, fwd_ref, rinv_ref, col_ref, res_ref, part_ref, held_ref) = refs[0], refs[1:5], refs[5:]
+    near_ref, far_refs = refs[0], refs[1 : 1 + len(FAR)]
+    a_ref, fwd_ref, rinv_ref, col_ref, res_ref, part_ref, held_ref = refs[1 + len(FAR) :]
     dh, dl, own_y = where_ref[0], where_ref[1], where_ref[2]
     for b in range(4):
         g = dl ^ b
         for a in range(2):
             zh = dh ^ (dl & 1) ^ a
+            k = a * 4 + b
             for t in range(2):
                 rinv = rinv_ref[g, 0:1, t * 256 : (t + 1) * 256]
                 for y in range(4):
                     rows = pl.ds(pl.multiple_of((y * 2 + zh) * 32, 32), 32)
                     lanes = slice(t * 256, (t + 1) * 256)
-                    block = near_ref[(y ^ own_y) * 2 + t, b] if a == 0 else far_refs[b][t * 4 + y]
+                    if k in NEAR:
+                        block = near_ref[(y ^ own_y) * 2 + t, NEAR.index(k)]
+                    else:
+                        block = far_refs[FAR.index(k)][t * 4 + y]
                     res = ((block.astype(F32) - fwd_ref[g, rows, lanes]) * rinv).astype(BF16)
                     res_ref[g * 2 + t, rows, :] = res
                     held_ref[rows, lanes] = res
@@ -158,7 +170,7 @@
     vmem = pl.BlockSpec(memory_space=pltpu.VMEM)
     return pl.pallas_call(
         finish_kernel,
-        in_specs=[pl.BlockSpec(memory_space=pltpu.SMEM)] + [vmem] * 9,
+        in_specs=[pl.BlockSpec(memory_space=pltpu.SMEM)] + [vmem] * (5 + len(FAR)),
         out_specs=[vmem, vmem],
         out_shape=[
             jax.ShapeDtypeStruct((8, 256, 256), BF16),
@@ -172,25 +184,25 @@
 
 
 def on_device(projections, start_image, system, first_tile):
-    x, zl, y, zh = (lax.axis_index(name) for name in ("x", "zl", "y", "zh"))
+    zl, y, zh = (lax.axis_index(name) for name in ("zl", "y", "zh"))
     dh, dl = zl // 4, zl % 4
-    def send(block, half, b):
+    def send(block, k):
         def dest(x, zl, core, y, zh):
-            low = (zl % 4) ^ b
-            return (x ^ y, (zh ^ (low & 1) ^ half) * 4 + low, core, x, zl // 4)
+            return (x ^ y, mixed((zh * 4 + zl % 4) ^ k), core, x, zl // 4)
 
         return lax.ppermute(block, AXES, pairs(dest))
 
-    *near, far = pack(jnp.stack([x, dl, zh]), projections)
-    first_tile, image, system, far = lax.optimization_barrier((first_tile, start_image, system, far))
-    near = [send(block.reshape(8, 32, 256), 0, b) for b, block in enumerate(near)]
-    far = lax.all_to_all(far.reshape(8, 4, 32, 256), ("core", "y"), 0, 0, tiled=True)
+    *near, far = pack(projections)
+    near = [send(block.reshape(8, 32, 256), k) for k, block in zip(NEAR, near)]
+    far = lax.all_to_all(far.reshape(8, len(FAR), 32, 256), ("core", "y"), 0, 0, tiled=True)
     near, _ = lax.optimization_barrier((near, far))
-    far = [lax.dynamic_index_in_dim(far, dl ^ b, 1, keepdims=False) for b in range(4)]
     near = jnp.stack(near, 1)
-    far = [send(block, 1, b) for b, block in enumerate(far)]
+    far = [send(far[:, n], k) for n, k in enumerate(FAR)]
     near = lax.all_to_all(near, ("x", "core"), 0, 0, tiled=True)
+    first_tile, image, system, near = lax.optimization_barrier((first_tile, start_image, system, near))
+    local = lax.dynamic_slice_in_dim(image, (y * 2 + zh) * 128, 128, 1).astype(F32)
     a, fwd, rinv, col = prepare(first_tile, image, system)
+    col, local = lax.optimization_barrier((col, local))
     where = jnp.stack([dh, dl, y]).astype(jnp.int32)
     residual, part = finish(where, near, far, a, fwd, rinv, col)
     part = lax.all_to_all(part.astype(jnp.float16), "y", 0, 0, tiled=True).astype(F32).sum(0)
@@ -202,7 +214,6 @@
     other = jnp.concatenate([other[:256], high, cols - high, jnp.zeros((14, 128), F32)]).astype(jnp.float16)
     swap = pairs(lambda x, zl, core, y, zh: (x, zl, core, y, 1 - zh))
     total = mine + lax.ppermute(other, AXES, swap).astype(F32)
-    local = lax.dynamic_slice_in_dim(start_image, (y * 2 + zh) * 128, 128, 1).astype(F32)
     new_image = local + total[:256] / (total[256:257] + total[257:258])
     return new_image, residual
 

time: 157 us -> 151 us (0.962)
  starting transfers between devices: 80.3 us -> 88.6 us
  local copies, waits for them, and re-layouts: 8.84 us -> 1.74 us
  waiting for transfers between devices: 53.6 us -> 47.4 us
    ppermute x8, starting transfers between devices: 65.6 us -> 73.8 us  [send(): return lax.ppermute(block, AXES, pairs(dest))]
    unnamed x12 -> x6, local copies, waits for them, and re-layouts: 7.99 us -> 1.6 us
    ppermute x8, waiting for transfers between devices: 30.4 us -> 24.3 us  [send(): return lax.ppermute(block, AXES, pairs(dest))]
  transfers between devices with their start and end apart: 12 -> 12, of which waited for: 5 -> 5; matrix products, arithmetic and copies ran while one was open for 1% -> 0% of each run, Pallas kernels for 3% -> 3%
where the time goes in v8:
time: 151 us
  starting transfers between devices  88.6 us (59%)
  waiting for transfers between devices  47.4 us (31%)
  Pallas kernels  9.16 us (6%)
  other arithmetic  2.85 us (2%)
  local copies, waits for them, and re-layouts  1.74 us (1%)
    ppermute x8, starting transfers between devices, send(): return lax.ppermute(block, AXES, pairs(dest))  73.8 us
    ppermute x8, waiting for transfers between devices, send(): return lax.ppermute(block, AXES, pairs(dest))  24.3 us
    ppermute x1, waiting for transfers between devices, on_device(): total = mine + lax.ppermute(other, AXES, swap).astype(F32)  13 us
    all_to_all x1, waiting for transfers between devices, on_device(): lax.all_to_all(part.astype(jnp.float16), 'y', 0, 0, tiled=True).astype(F32)  10.2 us
    pallas_call x1, Pallas kernels, prepare(): pl.pallas_call(prepare_kernel, grid=(4,), in_specs=[pl.BlockSpec(memory_s...  4.87 us
    all_to_all x1, starting transfers between devices, on_device(): near = lax.all_to_all(near, ('x', 'core'), 0, 0, tiled=True)  4.8 us
    all_to_all x1, starting transfers between devices, on_device(): lax.all_to_all(far.reshape(8, len(FAR), 32, 256), ('core', 'y'), 0, 0, ti...  4.61 us
    all_to_all x1, starting transfers between devices, on_device(): lax.all_to_all(part.astype(jnp.float16), 'y', 0, 0, tiled=True).astype(F32)  3.47 us
  transfers between devices with their start and end apart: 12, of which 5 were waited for; matrix products, arithmetic and copies ran while one was open for 0% of the time, Pallas kernels for 3%

profile of v8, /device:TPU:4, one launch (start us, length us, event | category | flops | bytes accessed | tf_op | source)
XLA Modules:
  0.0 150.7 jit_solution(5280935631439031190)
XLA Ops:
  0.6 2.3 %pack.1 = (bf16[4,2,32,256]{3,2,1,0:T(8,128)(2,1)}, bf16[4,2,32,256]{3,2,1,0:T(8,128)(2,1)}, bf16[4,2,32,256]{3,2,1,0:T(8,128)(2,1)}, bf16[4,2,32,256]{3,2,1,0:T(8,128)(2,1)}, bf16[2,4,4,32,256]{4,3,2,1,0:T(8,128)(2,1)}) custom-call(bf16[4,8,2,32,256]{4,3,2,1,0:T(8,128)(2,1)} %bitcast.47), custom_call_target="tpu_custom_call" | custom-call | bytes 2097152 | tf_op jit(solution)/shard_map/pack/pallas_call | solution.py:122
  3.0 0.0 copy-start
  3.0 0.0 copy-start.2
  3.0 4.6 %all-to-all-start = ((bf16[8,4,32,256]{3,2,1,0:T(8,128)(2,1)}), bf16[8,4,32,256]{3,2,1,0:T(8,128)(2,1)S(1)}, u32[]{:S(2)}, u32[]{:S(2)}) async-start(bf16[8,4,32,256]{3,2,1,0:T(8,128)(2,1)} %bitcast.48), calls=%async_computation | async-start | bytes 1048576 | tf_op jit(solution)/shard_map/all_to_all | solution.py:197
  7.6 5.4 %collective-permute-start = (bf16[8,32,256]{2,1,0:T(8,128)(2,1)}, bf16[8,32,256]{2,1,0:T(8,128)(2,1)S(1)}, u32[]{:S(2)}, u32[]{:S(2)}) collective-permute-start(bf16[8,32,256]{2,1,0:T(8,128)(2,1)} %bitcast.56), channel_id=1, source_target_pairs={{0,0},{1,64},{2,128},{3,192},{4,256},{5,320},{6,384},{7,448},{8,8}... | collective-permute-start | bytes 393224 | tf_op jit(solution)/shard_map/ppermute | solution.py:193
  13.0 17.9 %collective-permute-start.1 = (bf16[8,32,256]{2,1,0:T(8,128)(2,1)}, bf16[8,32,256]{2,1,0:T(8,128)(2,1)S(1)}, u32[]{:S(2)}, u32[]{:S(2)}) collective-permute-start(bf16[8,32,256]{2,1,0:T(8,128)(2,1)} %bitcast.55), channel_id=1, source_target_pairs={{0,80},{1,16},{2,208},{3,144},{4,336},{5,272},{6,464},{7,400},{8,8... | collective-permute-start | bytes 393224 | tf_op jit(solution)/shard_map/ppermute | solution.py:193
  31.0 5.3 %collective-permute-start.2 = (bf16[8,32,256]{2,1,0:T(8,128)(2,1)}, bf16[8,32,256]{2,1,0:T(8,128)(2,1)S(1)}, u32[]{:S(2)}, u32[]{:S(2)}) collective-permute-start(bf16[8,32,256]{2,1,0:T(8,128)(2,1)} %bitcast.54), channel_id=1, source_target_pairs={{0,32},{1,96},{2,160},{3,224},{4,288},{5,352},{6,416},{7,480},{8,4... | collective-permute-start | bytes 393224 | tf_op jit(solution)/shard_map/ppermute | solution.py:193
  36.3 5.0 %collective-permute-start.3 = (bf16[8,32,256]{2,1,0:T(8,128)(2,1)}, bf16[8,32,256]{2,1,0:T(8,128)(2,1)S(1)}, u32[]{:S(2)}, u32[]{:S(2)}) collective-permute-start(bf16[8,32,256]{2,1,0:T(8,128)(2,1)} %bitcast.53), channel_id=1, source_target_pairs={{0,112},{1,48},{2,240},{3,176},{4,368},{5,304},{6,496},{7,432},{8,... | collective-permute-start | bytes 393224 | tf_op jit(solution)/shard_map/ppermute | solution.py:193
  41.3 0.0 collective-permute-done
  41.3 0.0 collective-permute-done.1
  41.3 5.7 %collective-permute-done.2 = bf16[8,32,256]{2,1,0:T(8,128)(2,1)S(1)} collective-permute-done((bf16[8,32,256]{2,1,0:T(8,128)(2,1)}, bf16[8,32,256]{2,1,0:T(8,128)(2,1)S(1)}, u32[]{:S(2)}, u32[]{:S(2)}) %collective-permute-start.2) | collective-permute-done | bytes 131104 | tf_op jit(solution)/shard_map/ppermute | solution.py:193
  47.0 6.6 %collective-permute-done.3 = bf16[8,32,256]{2,1,0:T(8,128)(2,1)S(1)} collective-permute-done((bf16[8,32,256]{2,1,0:T(8,128)(2,1)}, bf16[8,32,256]{2,1,0:T(8,128)(2,1)S(1)}, u32[]{:S(2)}, u32[]{:S(2)}) %collective-permute-start.3) | collective-permute-done | bytes 131104 | tf_op jit(solution)/shard_map/ppermute | solution.py:193
  53.6 0.0 all-to-all-done
  53.6 0.9 pad_maximum_fusion
  54.4 4.8 %all-to-all-start.1 = ((bf16[8,4,32,256]{3,2,1,0:T(8,128)(2,1)}), bf16[8,4,32,256]{3,2,1,0:T(8,128)(2,1)S(1)}, u32[]{:S(2)}, u32[]{:S(2)}) async-start(bf16[8,4,32,256]{3,2,1,0:T(8,128)(2,1)} %pad_maximum_fusion), calls=%async_computation.1 | async-start | bytes 1048576 | tf_op jit(solution)/shard_map/all_to_all | solution.py:201
  59.2 0.1 pad_add_fusion.where_ref
  59.4 12.3 %collective-permute-start.4 = (bf16[8,32,256]{2,1,0:T(8,128)(2,1)S(1)}, bf16[8,32,256]{2,1,0:T(8,128)(2,1)S(1)}, u32[]{:S(2)}, u32[]{:S(2)}) collective-permute-start(bf16[8,32,256]{2,1,0:T(8,128)(2,1)S(1)} %get-tuple-element.47), channel_id=1, source_target_pairs={{0,16},{1,80},{2,144},{3,208},{4,272},{5,336},{6,400},{7,464},{8,2... | collective-permute-start | bytes 393224 | tf_op jit(solution)/shard_map/ppermute | solution.py:193
  71.7 1.9 %collective-permute-start.5 = (bf16[8,32,256]{2,1,0:T(8,128)(2,1)S(1)}, bf16[8,32,256]{2,1,0:T(8,128)(2,1)S(1)}, u32[]{:S(2)}, u32[]{:S(2)}) collective-permute-start(bf16[8,32,256]{2,1,0:T(8,128)(2,1)S(1)} %get-tuple-element.46), channel_id=1, source_target_pairs={{0,64},{1,0},{2,192},{3,128},{4,320},{5,256},{6,448},{7,384},{8,72... | collective-permute-start | bytes 393224 | tf_op jit(solution)/shard_map/ppermute | solution.py:193
  73.6 9.2 %collective-permute-start.6 = (bf16[8,32,256]{2,1,0:T(8,128)(2,1)S(1)}, bf16[8,32,256]{2,1,0:T(8,128)(2,1)S(1)}, u32[]{:S(2)}, u32[]{:S(2)}) collective-permute-start(bf16[8,32,256]{2,1,0:T(8,128)(2,1)S(1)} %get-tuple-element.45), channel_id=1, source_target_pairs={{0,48},{1,112},{2,176},{3,240},{4,304},{5,368},{6,432},{7,496},{8,... | collective-permute-start | bytes 393224 | tf_op jit(solution)/shard_map/ppermute | solution.py:193
  82.8 16.8 %collective-permute-start.7 = (bf16[8,32,256]{2,1,0:T(8,128)(2,1)S(1)}, bf16[8,32,256]{2,1,0:T(8,128)(2,1)S(1)}, u32[]{:S(2)}, u32[]{:S(2)}) collective-permute-start(bf16[8,32,256]{2,1,0:T(8,128)(2,1)S(1)} %get-tuple-element.44), channel_id=1, source_target_pairs={{0,96},{1,32},{2,224},{3,160},{4,352},{5,288},{6,480},{7,416},{8,1... | collective-permute-start | bytes 393224 | tf_op jit(solution)/shard_map/ppermute | solution.py:193
  99.6 0.0 all-to-all-done.1.refs_0_
  99.6 0.0 copy-done
  99.6 0.0 copy-done.2
  99.6 0.0 copy-start.1
  99.7 1.6 %copy-done.1 = bf16[4,16,2,64,128]{4,3,2,1,0:T(8,128)(2,1)S(1)} copy-done((bf16[4,16,2,64,128]{4,3,2,1,0:T(8,128)(2,1)S(1)}, bf16[4,16,2,64,128]{4,3,2,1,0:T(8,128)(2,1)}, u32[]{:S(2)}) %copy-start.1) | copy-done | bytes 2097176
  101.2 4.9 %prepare.1 = (bf16[4,1024,512]{2,1,0:T(8,128)(2,1)S(1)}, f32[4,256,512]{2,1,0:T(8,128)S(1)}, f32[4,8,512]{2,1,0:T(8,128)S(1)}, f32[8,1024]{1,0:T(8,128)S(1)}) custom-call(s32[4,16]{1,0:T(4,128)S(1)} %copy-done.2, bf16[256,1024]{1,0:T(8,128)(2,1)S(1)} %copy-done, bf16[4,16,2,64,128]{4,3,2,1,0:T(8,128)(2,1)S(1)} %copy-done.1), custom_call_target="tpu_custom_call" | custom-call | flops 1100000000 | bytes 10000000 | tf_op jit(solution)/shard_map/prepare/pallas_call | solution.py:78
  106.2 0.0 collective-permute-done.4.refs_1_
  106.2 11.9 %collective-permute-done.5.refs_2_ = bf16[8,32,256]{2,1,0:T(8,128)(2,1)S(1)} collective-permute-done((bf16[8,32,256]{2,1,0:T(8,128)(2,1)S(1)}, bf16[8,32,256]{2,1,0:T(8,128)(2,1)S(1)}, u32[]{:S(2)}, u32[]{:S(2)}) %collective-permute-start.5) | collective-permute-done | bytes 131104 | tf_op jit(solution)/shard_map/ppermute | solution.py:193
  118.1 0.0 collective-permute-done.6.refs_3_
  118.1 0.0 collective-permute-done.7.refs_4_
  118.1 2.0 %finish.1 = (bf16[8,256,256]{2,1,0:T(8,128)(2,1)}, f32[4,272,256]{2,1,0:T(8,128)S(1)}) custom-call(s32[3]{0:T(128)S(1)} %pad_add_fusion.where_ref, bf16[8,4,32,256]{3,2,1,0:T(8,128)(2,1)S(1)} %all-to-all-done.1.refs_0_, bf16[8,32,256]{2,1,0:T(8,128)(2,1)S(1)} %collective-permute-done.4.refs_1_, bf16[8,32,256]{2,1,0:T(8,128)(2,1)S(1)} %collective-permute-done.5.refs_2_, ...), custom_call_target="tpu_custom_call" | custom-call | flops 1100000000 | bytes 10000000 | tf_op jit(solution)/shard_map/finish/pallas_call | solution.py:171
  120.1 0.9 convert_element_type.14
  121.0 3.5 %all-to-all-start.2 = ((f16[4,272,256]{2,1,0:T(8,128)(2,1)}), f16[4,272,256]{2,1,0:T(8,128)(2,1)S(1)}, u32[]{:S(2)}, u32[]{:S(2)}) async-start(f16[4,272,256]{2,1,0:T(8,128)(2,1)} %convert_element_type.14), calls=%async_computation.2 | async-start | bytes 1114112 | tf_op jit(solution)/shard_map/all_to_all | solution.py:208
  124.5 0.1 pad.3.clone
  124.6 10.2 %all-to-all-done.2 = f16[4,272,256]{2,1,0:T(8,128)(2,1)S(1)} async-done(((f16[4,272,256]{2,1,0:T(8,128)(2,1)}), f16[4,272,256]{2,1,0:T(8,128)(2,1)S(1)}, u32[]{:S(2)}, u32[]{:S(2)}) %all-to-all-start.2) | async-done | bytes 557088 | tf_op jit(solution)/shard_map/all_to_all | solution.py:208
  134.7 0.1 convert_reduce_fusion
  134.9 0.1 maximum_maximum_fusion
  135.0 1.9 %collective-permute-start.8 = (f16[272,128]{1,0:T(8,128)(2,1)S(1)}, f16[272,128]{1,0:T(8,128)(2,1)S(1)}, u32[]{:S(2)}, u32[]{:S(2)}) collective-permute-start(f16[272,128]{1,0:T(8,128)(2,1)S(1)} %maximum_maximum_fusion), channel_id=1, source_target_pairs={{0,1},{1,0},{2,3},{3,2},{4,5},{5,4},{6,7},{7,6},{8,9},{9,8},{10,11... | collective-permute-start | bytes 208904 | tf_op jit(solution)/shard_map/ppermute | solution.py:216
  137.0 13.0 %collective-permute-done.8 = f16[272,128]{1,0:T(8,128)(2,1)S(1)} collective-permute-done((f16[272,128]{1,0:T(8,128)(2,1)S(1)}, f16[272,128]{1,0:T(8,128)(2,1)S(1)}, u32[]{:S(2)}, u32[]{:S(2)}) %collective-permute-start.8) | collective-permute-done | bytes 69664 | tf_op jit(solution)/shard_map/ppermute | solution.py:216
  150.0 0.7 fusion.4
  (9 shorter events, 0.2 us)
Async XLA Ops:
  3.0 96.7 %copy-start = (bf16[256,1024]{1,0:T(8,128)(2,1)S(1)}, bf16[256,1024]{1,0:T(8,128)(2,1)}, u32[]{:S(2)}) copy-start(bf16[256,1024]{1,0:T(8,128)(2,1)} %image_ref) | copy-start | bytes 1572868
  3.0 96.6 %copy-start.2 = (s32[4,16]{1,0:T(4,128)S(1)}, s32[4,16]{1,0:T(4,128)}, u32[]{:S(2)}) copy-start(s32[4,16]{1,0:T(4,128)} %first_ref) | copy-start | bytes 772
  3.0 50.6 %all-to-all-start = ((bf16[8,4,32,256]{3,2,1,0:T(8,128)(2,1)}), bf16[8,4,32,256]{3,2,1,0:T(8,128)(2,1)S(1)}, u32[]{:S(2)}, u32[]{:S(2)}) async-start(bf16[8,4,32,256]{3,2,1,0:T(8,128)(2,1)} %bitcast.48), calls=%async_computation | async-start | bytes 1048576 | tf_op jit(solution)/shard_map/all_to_all | solution.py:197
  7.6 33.6 %collective-permute-start = (bf16[8,32,256]{2,1,0:T(8,128)(2,1)}, bf16[8,32,256]{2,1,0:T(8,128)(2,1)S(1)}, u32[]{:S(2)}, u32[]{:S(2)}) collective-permute-start(bf16[8,32,256]{2,1,0:T(8,128)(2,1)} %bitcast.56), channel_id=1, source_target_pairs={{0,0},{1,64},{2,128},{3,192},{4,256},{5,320},{6,384},{7,448},{8,8}... | collective-permute-start | bytes 393224 | tf_op jit(solution)/shard_map/ppermute | solution.py:193
  13.0 28.2 %collective-permute-start.1 = (bf16[8,32,256]{2,1,0:T(8,128)(2,1)}, bf16[8,32,256]{2,1,0:T(8,128)(2,1)S(1)}, u32[]{:S(2)}, u32[]{:S(2)}) collective-permute-start(bf16[8,32,256]{2,1,0:T(8,128)(2,1)} %bitcast.55), channel_id=1, source_target_pairs={{0,80},{1,16},{2,208},{3,144},{4,336},{5,272},{6,464},{7,400},{8,8... | collective-permute-start | bytes 393224 | tf_op jit(solution)/shard_map/ppermute | solution.py:193
  31.0 16.0 %collective-permute-start.2 = (bf16[8,32,256]{2,1,0:T(8,128)(2,1)}, bf16[8,32,256]{2,1,0:T(8,128)(2,1)S(1)}, u32[]{:S(2)}, u32[]{:S(2)}) collective-permute-start(bf16[8,32,256]{2,1,0:T(8,128)(2,1)} %bitcast.54), channel_id=1, source_target_pairs={{0,32},{1,96},{2,160},{3,224},{4,288},{5,352},{6,416},{7,480},{8,4... | collective-permute-start | bytes 393224 | tf_op jit(solution)/shard_map/ppermute | solution.py:193
  36.3 17.3 %collective-permute-start.3 = (bf16[8,32,256]{2,1,0:T(8,128)(2,1)}, bf16[8,32,256]{2,1,0:T(8,128)(2,1)S(1)}, u32[]{:S(2)}, u32[]{:S(2)}) collective-permute-start(bf16[8,32,256]{2,1,0:T(8,128)(2,1)} %bitcast.53), channel_id=1, source_target_pairs={{0,112},{1,48},{2,240},{3,176},{4,368},{5,304},{6,496},{7,432},{8,... | collective-permute-start | bytes 393224 | tf_op jit(solution)/shard_map/ppermute | solution.py:193
  54.4 45.2 %all-to-all-start.1 = ((bf16[8,4,32,256]{3,2,1,0:T(8,128)(2,1)}), bf16[8,4,32,256]{3,2,1,0:T(8,128)(2,1)S(1)}, u32[]{:S(2)}, u32[]{:S(2)}) async-start(bf16[8,4,32,256]{3,2,1,0:T(8,128)(2,1)} %pad_maximum_fusion), calls=%async_computation.1 | async-start | bytes 1048576 | tf_op jit(solution)/shard_map/all_to_all | solution.py:201
  59.4 46.8 %collective-permute-start.4 = (bf16[8,32,256]{2,1,0:T(8,128)(2,1)S(1)}, bf16[8,32,256]{2,1,0:T(8,128)(2,1)S(1)}, u32[]{:S(2)}, u32[]{:S(2)}) collective-permute-start(bf16[8,32,256]{2,1,0:T(8,128)(2,1)S(1)} %get-tuple-element.47), channel_id=1, source_target_pairs={{0,16},{1,80},{2,144},{3,208},{4,272},{5,336},{6,400},{7,464},{8,2... | collective-permute-start | bytes 393224 | tf_op jit(solution)/shard_map/ppermute | solution.py:193
  71.7 46.4 %collective-permute-start.5 = (bf16[8,32,256]{2,1,0:T(8,128)(2,1)S(1)}, bf16[8,32,256]{2,1,0:T(8,128)(2,1)S(1)}, u32[]{:S(2)}, u32[]{:S(2)}) collective-permute-start(bf16[8,32,256]{2,1,0:T(8,128)(2,1)S(1)} %get-tuple-element.46), channel_id=1, source_target_pairs={{0,64},{1,0},{2,192},{3,128},{4,320},{5,256},{6,448},{7,384},{8,72... | collective-permute-start | bytes 393224 | tf_op jit(solution)/shard_map/ppermute | solution.py:193
  73.6 44.5 %collective-permute-start.6 = (bf16[8,32,256]{2,1,0:T(8,128)(2,1)S(1)}, bf16[8,32,256]{2,1,0:T(8,128)(2,1)S(1)}, u32[]{:S(2)}, u32[]{:S(2)}) collective-permute-start(bf16[8,32,256]{2,1,0:T(8,128)(2,1)S(1)} %get-tuple-element.45), channel_id=1, source_target_pairs={{0,48},{1,112},{2,176},{3,240},{4,304},{5,368},{6,432},{7,496},{8,... | collective-permute-start | bytes 393224 | tf_op jit(solution)/shard_map/ppermute | solution.py:193
  82.8 35.3 %collective-permute-start.7 = (bf16[8,32,256]{2,1,0:T(8,128)(2,1)S(1)}, bf16[8,32,256]{2,1,0:T(8,128)(2,1)S(1)}, u32[]{:S(2)}, u32[]{:S(2)}) collective-permute-start(bf16[8,32,256]{2,1,0:T(8,128)(2,1)S(1)} %get-tuple-element.44), channel_id=1, source_target_pairs={{0,96},{1,32},{2,224},{3,160},{4,352},{5,288},{6,480},{7,416},{8,1... | collective-permute-start | bytes 393224 | tf_op jit(solution)/shard_map/ppermute | solution.py:193
  99.6 1.6 %copy-start.1 = (bf16[4,16,2,64,128]{4,3,2,1,0:T(8,128)(2,1)S(1)}, bf16[4,16,2,64,128]{4,3,2,1,0:T(8,128)(2,1)}, u32[]{:S(2)}) copy-start(bf16[4,16,2,64,128]{4,3,2,1,0:T(8,128)(2,1)} %system_ref) | copy-start | bytes 6291460
  121.0 13.7 %all-to-all-start.2 = ((f16[4,272,256]{2,1,0:T(8,128)(2,1)}), f16[4,272,256]{2,1,0:T(8,128)(2,1)S(1)}, u32[]{:S(2)}, u32[]{:S(2)}) async-start(f16[4,272,256]{2,1,0:T(8,128)(2,1)} %convert_element_type.14), calls=%async_computation.2 | async-start | bytes 1114112 | tf_op jit(solution)/shard_map/all_to_all | solution.py:208
  135.0 14.9 %collective-permute-start.8 = (f16[272,128]{1,0:T(8,128)(2,1)S(1)}, f16[272,128]{1,0:T(8,128)(2,1)S(1)}, u32[]{:S(2)}, u32[]{:S(2)}) collective-permute-start(f16[272,128]{1,0:T(8,128)(2,1)S(1)} %maximum_maximum_fusion), channel_id=1, source_target_pairs={{0,1},{1,0},{2,3},{3,2},{4,5},{5,4},{6,7},{7,6},{8,9},{9,8},{10,11... | collective-permute-start | bytes 208904 | tf_op jit(solution)/shard_map/ppermute | solution.py:216

commit v9 on v8

--- a/solution.py
+++ b/solution.py
@@ -10,8 +10,8 @@
 
 AXES = ("x", "zl", "core", "y", "zh")
 SIZES = (4, 8, 2, 4, 2)
-NEAR = (0, 1, 2, 3)
-FAR = (5, 4, 7, 6)
+NEAR = (4, 5, 6, 7)
+FAR = (0, 1, 2, 3)
 F32 = jnp.float32
 BF16 = jnp.bfloat16
 

time: 151 us -> 144 us (0.954)
  the two profiles are of different devices: /device:TPU:4 before, /device:TPU:486 now
where the time goes in v9:
time: 144 us
  starting transfers between devices  70.6 us (49%)
  waiting for transfers between devices  57.8 us (40%)
  Pallas kernels  9.67 us (7%)
  other arithmetic  2.84 us (2%)
  local copies, waits for them, and re-layouts  1.74 us (1%)
    ppermute x8, starting transfers between devices, send(): return lax.ppermute(block, AXES, pairs(dest))  55.3 us
    ppermute x8, waiting for transfers between devices, send(): return lax.ppermute(block, AXES, pairs(dest))  34.6 us
    ppermute x1, waiting for transfers between devices, on_device(): total = mine + lax.ppermute(other, AXES, swap).astype(F32)  13 us
    all_to_all x1, waiting for transfers between devices, on_device(): lax.all_to_all(part.astype(jnp.float16), 'y', 0, 0, tiled=True).astype(F32)  10.2 us
    all_to_all x1, starting transfers between devices, on_device(): near = lax.all_to_all(near, ('x', 'core'), 0, 0, tiled=True)  5.25 us
    pallas_call x1, Pallas kernels, prepare(): pl.pallas_call(prepare_kernel, grid=(4,), in_specs=[pl.BlockSpec(memory_s...  4.87 us
    all_to_all x1, starting transfers between devices, on_device(): lax.all_to_all(far.reshape(8, len(FAR), 32, 256), ('core', 'y'), 0, 0, ti...  4.61 us
    all_to_all x1, starting transfers between devices, on_device(): lax.all_to_all(part.astype(jnp.float16), 'y', 0, 0, tiled=True).astype(F32)  3.47 us
  transfers between devices with their start and end apart: 12, of which 5 were waited for; matrix products, arithmetic and copies ran while one was open for 0% of the time, Pallas kernels for 3%

profile of v9, /device:TPU:486, one launch (start us, length us, event | category | flops | bytes accessed | tf_op | source)
XLA Modules:
  0.0 143.5 jit_solution(4948869557269684916)
XLA Ops:
  0.6 2.3 %pack.1 = (bf16[4,2,32,256]{3,2,1,0:T(8,128)(2,1)}, bf16[4,2,32,256]{3,2,1,0:T(8,128)(2,1)}, bf16[4,2,32,256]{3,2,1,0:T(8,128)(2,1)}, bf16[4,2,32,256]{3,2,1,0:T(8,128)(2,1)}, bf16[2,4,4,32,256]{4,3,2,1,0:T(8,128)(2,1)}) custom-call(bf16[4,8,2,32,256]{4,3,2,1,0:T(8,128)(2,1)} %bitcast.47), custom_call_target="tpu_custom_call" | custom-call | bytes 2097152 | tf_op jit(solution)/shard_map/pack/pallas_call | solution.py:122
  3.0 0.0 copy-start
  3.0 0.0 copy-start.2
  3.0 4.6 %all-to-all-start = ((bf16[8,4,32,256]{3,2,1,0:T(8,128)(2,1)}), bf16[8,4,32,256]{3,2,1,0:T(8,128)(2,1)S(1)}, u32[]{:S(2)}, u32[]{:S(2)}) async-start(bf16[8,4,32,256]{3,2,1,0:T(8,128)(2,1)} %bitcast.48), calls=%async_computation | async-start | bytes 1048576 | tf_op jit(solution)/shard_map/all_to_all | solution.py:197
  7.6 5.1 %collective-permute-start = (bf16[8,32,256]{2,1,0:T(8,128)(2,1)}, bf16[8,32,256]{2,1,0:T(8,128)(2,1)S(1)}, u32[]{:S(2)}, u32[]{:S(2)}) collective-permute-start(bf16[8,32,256]{2,1,0:T(8,128)(2,1)} %bitcast.56), channel_id=1, source_target_pairs={{0,64},{1,0},{2,192},{3,128},{4,320},{5,256},{6,448},{7,384},{8,72... | collective-permute-start | bytes 393224 | tf_op jit(solution)/shard_map/ppermute | solution.py:193
  12.8 5.4 %collective-permute-start.1 = (bf16[8,32,256]{2,1,0:T(8,128)(2,1)}, bf16[8,32,256]{2,1,0:T(8,128)(2,1)S(1)}, u32[]{:S(2)}, u32[]{:S(2)}) collective-permute-start(bf16[8,32,256]{2,1,0:T(8,128)(2,1)} %bitcast.55), channel_id=1, source_target_pairs={{0,16},{1,80},{2,144},{3,208},{4,272},{5,336},{6,400},{7,464},{8,2... | collective-permute-start | bytes 393224 | tf_op jit(solution)/shard_map/ppermute | solution.py:193
  18.1 3.3 %collective-permute-start.2 = (bf16[8,32,256]{2,1,0:T(8,128)(2,1)}, bf16[8,32,256]{2,1,0:T(8,128)(2,1)S(1)}, u32[]{:S(2)}, u32[]{:S(2)}) collective-permute-start(bf16[8,32,256]{2,1,0:T(8,128)(2,1)} %bitcast.54), channel_id=1, source_target_pairs={{0,96},{1,32},{2,224},{3,160},{4,352},{5,288},{6,480},{7,416},{8,1... | collective-permute-start | bytes 393224 | tf_op jit(solution)/shard_map/ppermute | solution.py:193
  21.4 8.5 %collective-permute-start.3 = (bf16[8,32,256]{2,1,0:T(8,128)(2,1)}, bf16[8,32,256]{2,1,0:T(8,128)(2,1)S(1)}, u32[]{:S(2)}, u32[]{:S(2)}) collective-permute-start(bf16[8,32,256]{2,1,0:T(8,128)(2,1)} %bitcast.53), channel_id=1, source_target_pairs={{0,48},{1,112},{2,176},{3,240},{4,304},{5,368},{6,432},{7,496},{8,... | collective-permute-start | bytes 393224 | tf_op jit(solution)/shard_map/ppermute | solution.py:193
  29.9 0.0 collective-permute-done
  29.9 0.0 collective-permute-done.1
  29.9 2.6 %collective-permute-done.2 = bf16[8,32,256]{2,1,0:T(8,128)(2,1)S(1)} collective-permute-done((bf16[8,32,256]{2,1,0:T(8,128)(2,1)}, bf16[8,32,256]{2,1,0:T(8,128)(2,1)S(1)}, u32[]{:S(2)}, u32[]{:S(2)}) %collective-permute-start.2) | collective-permute-done | bytes 131104 | tf_op jit(solution)/shard_map/ppermute | solution.py:193
  32.5 9.7 %collective-permute-done.3 = bf16[8,32,256]{2,1,0:T(8,128)(2,1)S(1)} collective-permute-done((bf16[8,32,256]{2,1,0:T(8,128)(2,1)}, bf16[8,32,256]{2,1,0:T(8,128)(2,1)S(1)}, u32[]{:S(2)}, u32[]{:S(2)}) %collective-permute-start.3) | collective-permute-done | bytes 131104 | tf_op jit(solution)/shard_map/ppermute | solution.py:193
  42.2 0.0 all-to-all-done
  42.2 0.9 pad_maximum_fusion
  43.1 5.3 %all-to-all-start.1 = ((bf16[8,4,32,256]{3,2,1,0:T(8,128)(2,1)}), bf16[8,4,32,256]{3,2,1,0:T(8,128)(2,1)S(1)}, u32[]{:S(2)}, u32[]{:S(2)}) async-start(bf16[8,4,32,256]{3,2,1,0:T(8,128)(2,1)} %pad_maximum_fusion), calls=%async_computation.1 | async-start | bytes 1048576 | tf_op jit(solution)/shard_map/all_to_all | solution.py:201
  48.3 0.1 pad_add_fusion.where_ref
  48.4 16.9 %collective-permute-start.4 = (bf16[8,32,256]{2,1,0:T(8,128)(2,1)S(1)}, bf16[8,32,256]{2,1,0:T(8,128)(2,1)S(1)}, u32[]{:S(2)}, u32[]{:S(2)}) collective-permute-start(bf16[8,32,256]{2,1,0:T(8,128)(2,1)S(1)} %get-tuple-element.47), channel_id=1, source_target_pairs={{0,0},{1,64},{2,128},{3,192},{4,256},{5,320},{6,384},{7,448},{8,8}... | collective-permute-start | bytes 393224 | tf_op jit(solution)/shard_map/ppermute | solution.py:193
  65.4 4.7 %collective-permute-start.5 = (bf16[8,32,256]{2,1,0:T(8,128)(2,1)S(1)}, bf16[8,32,256]{2,1,0:T(8,128)(2,1)S(1)}, u32[]{:S(2)}, u32[]{:S(2)}) collective-permute-start(bf16[8,32,256]{2,1,0:T(8,128)(2,1)S(1)} %get-tuple-element.46), channel_id=1, source_target_pairs={{0,80},{1,16},{2,208},{3,144},{4,336},{5,272},{6,464},{7,400},{8,8... | collective-permute-start | bytes 393224 | tf_op jit(solution)/shard_map/ppermute | solution.py:193
  70.1 4.7 %collective-permute-start.6 = (bf16[8,32,256]{2,1,0:T(8,128)(2,1)S(1)}, bf16[8,32,256]{2,1,0:T(8,128)(2,1)S(1)}, u32[]{:S(2)}, u32[]{:S(2)}) collective-permute-start(bf16[8,32,256]{2,1,0:T(8,128)(2,1)S(1)} %get-tuple-element.45), channel_id=1, source_target_pairs={{0,32},{1,96},{2,160},{3,224},{4,288},{5,352},{6,416},{7,480},{8,4... | collective-permute-start | bytes 393224 | tf_op jit(solution)/shard_map/ppermute | solution.py:193
  74.9 6.7 %collective-permute-start.7 = (bf16[8,32,256]{2,1,0:T(8,128)(2,1)S(1)}, bf16[8,32,256]{2,1,0:T(8,128)(2,1)S(1)}, u32[]{:S(2)}, u32[]{:S(2)}) collective-permute-start(bf16[8,32,256]{2,1,0:T(8,128)(2,1)S(1)} %get-tuple-element.44), channel_id=1, source_target_pairs={{0,112},{1,48},{2,240},{3,176},{4,368},{5,304},{6,496},{7,432},{8,... | collective-permute-start | bytes 393224 | tf_op jit(solution)/shard_map/ppermute | solution.py:193
  81.6 0.0 all-to-all-done.1.refs_0_
  81.6 0.0 copy-done
  81.6 0.0 copy-done.2
  81.6 0.0 copy-start.1
  81.6 1.6 %copy-done.1 = bf16[4,16,2,64,128]{4,3,2,1,0:T(8,128)(2,1)S(1)} copy-done((bf16[4,16,2,64,128]{4,3,2,1,0:T(8,128)(2,1)S(1)}, bf16[4,16,2,64,128]{4,3,2,1,0:T(8,128)(2,1)}, u32[]{:S(2)}) %copy-start.1) | copy-done | bytes 2097176
  83.2 4.9 %prepare.1 = (bf16[4,1024,512]{2,1,0:T(8,128)(2,1)S(1)}, f32[4,256,512]{2,1,0:T(8,128)S(1)}, f32[4,8,512]{2,1,0:T(8,128)S(1)}, f32[8,1024]{1,0:T(8,128)S(1)}) custom-call(s32[4,16]{1,0:T(4,128)S(1)} %copy-done.2, bf16[256,1024]{1,0:T(8,128)(2,1)S(1)} %copy-done, bf16[4,16,2,64,128]{4,3,2,1,0:T(8,128)(2,1)S(1)} %copy-done.1), custom_call_target="tpu_custom_call" | custom-call | flops 1100000000 | bytes 10000000 | tf_op jit(solution)/shard_map/prepare/pallas_call | solution.py:78
  88.1 22.3 %collective-permute-done.4.refs_1_ = bf16[8,32,256]{2,1,0:T(8,128)(2,1)S(1)} collective-permute-done((bf16[8,32,256]{2,1,0:T(8,128)(2,1)S(1)}, bf16[8,32,256]{2,1,0:T(8,128)(2,1)S(1)}, u32[]{:S(2)}, u32[]{:S(2)}) %collective-permute-start.4) | collective-permute-done | bytes 131104 | tf_op jit(solution)/shard_map/ppermute | solution.py:193
  110.4 0.0 collective-permute-done.5.refs_2_
  110.4 0.0 collective-permute-done.6.refs_3_
  110.4 0.0 collective-permute-done.7.refs_4_
  110.4 2.5 %finish.1 = (bf16[8,256,256]{2,1,0:T(8,128)(2,1)}, f32[4,272,256]{2,1,0:T(8,128)S(1)}) custom-call(s32[3]{0:T(128)S(1)} %pad_add_fusion.where_ref, bf16[8,4,32,256]{3,2,1,0:T(8,128)(2,1)S(1)} %all-to-all-done.1.refs_0_, bf16[8,32,256]{2,1,0:T(8,128)(2,1)S(1)} %collective-permute-done.4.refs_1_, bf16[8,32,256]{2,1,0:T(8,128)(2,1)S(1)} %collective-permute-done.5.refs_2_, ...), custom_call_target="tpu_custom_call" | custom-call | flops 1100000000 | bytes 10000000 | tf_op jit(solution)/shard_map/finish/pallas_call | solution.py:171
  112.8 0.9 convert_element_type.14
  113.7 3.5 %all-to-all-start.2 = ((f16[4,272,256]{2,1,0:T(8,128)(2,1)}), f16[4,272,256]{2,1,0:T(8,128)(2,1)S(1)}, u32[]{:S(2)}, u32[]{:S(2)}) async-start(f16[4,272,256]{2,1,0:T(8,128)(2,1)} %convert_element_type.14), calls=%async_computation.2 | async-start | bytes 1114112 | tf_op jit(solution)/shard_map/all_to_all | solution.py:208
  117.2 0.1 pad.3.clone
  117.3 10.2 %all-to-all-done.2 = f16[4,272,256]{2,1,0:T(8,128)(2,1)S(1)} async-done(((f16[4,272,256]{2,1,0:T(8,128)(2,1)}), f16[4,272,256]{2,1,0:T(8,128)(2,1)S(1)}, u32[]{:S(2)}, u32[]{:S(2)}) %all-to-all-start.2) | async-done | bytes 557088 | tf_op jit(solution)/shard_map/all_to_all | solution.py:208
  127.6 0.1 convert_reduce_fusion
  127.7 0.1 maximum_maximum_fusion
  127.9 1.9 %collective-permute-start.8 = (f16[272,128]{1,0:T(8,128)(2,1)S(1)}, f16[272,128]{1,0:T(8,128)(2,1)S(1)}, u32[]{:S(2)}, u32[]{:S(2)}) collective-permute-start(f16[272,128]{1,0:T(8,128)(2,1)S(1)} %maximum_maximum_fusion), channel_id=1, source_target_pairs={{0,1},{1,0},{2,3},{3,2},{4,5},{5,4},{6,7},{7,6},{8,9},{9,8},{10,11... | collective-permute-start | bytes 208904 | tf_op jit(solution)/shard_map/ppermute | solution.py:216
  129.8 13.0 %collective-permute-done.8 = f16[272,128]{1,0:T(8,128)(2,1)S(1)} collective-permute-done((f16[272,128]{1,0:T(8,128)(2,1)S(1)}, f16[272,128]{1,0:T(8,128)(2,1)S(1)}, u32[]{:S(2)}, u32[]{:S(2)}) %collective-permute-start.8) | collective-permute-done | bytes 69664 | tf_op jit(solution)/shard_map/ppermute | solution.py:216
  142.8 0.7 fusion.4
  (9 shorter events, 0.2 us)
Async XLA Ops:
  3.0 78.6 %copy-start = (bf16[256,1024]{1,0:T(8,128)(2,1)S(1)}, bf16[256,1024]{1,0:T(8,128)(2,1)}, u32[]{:S(2)}) copy-start(bf16[256,1024]{1,0:T(8,128)(2,1)} %image_ref) | copy-start | bytes 1572868
  3.0 78.6 %copy-start.2 = (s32[4,16]{1,0:T(4,128)S(1)}, s32[4,16]{1,0:T(4,128)}, u32[]{:S(2)}) copy-start(s32[4,16]{1,0:T(4,128)} %first_ref) | copy-start | bytes 772
  3.0 39.2 %all-to-all-start = ((bf16[8,4,32,256]{3,2,1,0:T(8,128)(2,1)}), bf16[8,4,32,256]{3,2,1,0:T(8,128)(2,1)S(1)}, u32[]{:S(2)}, u32[]{:S(2)}) async-start(bf16[8,4,32,256]{3,2,1,0:T(8,128)(2,1)} %bitcast.48), calls=%async_computation | async-start | bytes 1048576 | tf_op jit(solution)/shard_map/all_to_all | solution.py:197
  7.6 22.3 %collective-permute-start = (bf16[8,32,256]{2,1,0:T(8,128)(2,1)}, bf16[8,32,256]{2,1,0:T(8,128)(2,1)S(1)}, u32[]{:S(2)}, u32[]{:S(2)}) collective-permute-start(bf16[8,32,256]{2,1,0:T(8,128)(2,1)} %bitcast.56), channel_id=1, source_target_pairs={{0,64},{1,0},{2,192},{3,128},{4,320},{5,256},{6,448},{7,384},{8,72... | collective-permute-start | bytes 393224 | tf_op jit(solution)/shard_map/ppermute | solution.py:193
  12.8 17.1 %collective-permute-start.1 = (bf16[8,32,256]{2,1,0:T(8,128)(2,1)}, bf16[8,32,256]{2,1,0:T(8,128)(2,1)S(1)}, u32[]{:S(2)}, u32[]{:S(2)}) collective-permute-start(bf16[8,32,256]{2,1,0:T(8,128)(2,1)} %bitcast.55), channel_id=1, source_target_pairs={{0,16},{1,80},{2,144},{3,208},{4,272},{5,336},{6,400},{7,464},{8,2... | collective-permute-start | bytes 393224 | tf_op jit(solution)/shard_map/ppermute | solution.py:193
  18.1 14.4 %collective-permute-start.2 = (bf16[8,32,256]{2,1,0:T(8,128)(2,1)}, bf16[8,32,256]{2,1,0:T(8,128)(2,1)S(1)}, u32[]{:S(2)}, u32[]{:S(2)}) collective-permute-start(bf16[8,32,256]{2,1,0:T(8,128)(2,1)} %bitcast.54), channel_id=1, source_target_pairs={{0,96},{1,32},{2,224},{3,160},{4,352},{5,288},{6,480},{7,416},{8,1... | collective-permute-start | bytes 393224 | tf_op jit(solution)/shard_map/ppermute | solution.py:193
  21.4 20.8 %collective-permute-start.3 = (bf16[8,32,256]{2,1,0:T(8,128)(2,1)}, bf16[8,32,256]{2,1,0:T(8,128)(2,1)S(1)}, u32[]{:S(2)}, u32[]{:S(2)}) collective-permute-start(bf16[8,32,256]{2,1,0:T(8,128)(2,1)} %bitcast.53), channel_id=1, source_target_pairs={{0,48},{1,112},{2,176},{3,240},{4,304},{5,368},{6,432},{7,496},{8,... | collective-permute-start | bytes 393224 | tf_op jit(solution)/shard_map/ppermute | solution.py:193
  43.1 38.5 %all-to-all-start.1 = ((bf16[8,4,32,256]{3,2,1,0:T(8,128)(2,1)}), bf16[8,4,32,256]{3,2,1,0:T(8,128)(2,1)S(1)}, u32[]{:S(2)}, u32[]{:S(2)}) async-start(bf16[8,4,32,256]{3,2,1,0:T(8,128)(2,1)} %pad_maximum_fusion), calls=%async_computation.1 | async-start | bytes 1048576 | tf_op jit(solution)/shard_map/all_to_all | solution.py:201
  48.4 61.9 %collective-permute-start.4 = (bf16[8,32,256]{2,1,0:T(8,128)(2,1)S(1)}, bf16[8,32,256]{2,1,0:T(8,128)(2,1)S(1)}, u32[]{:S(2)}, u32[]{:S(2)}) collective-permute-start(bf16[8,32,256]{2,1,0:T(8,128)(2,1)S(1)} %get-tuple-element.47), channel_id=1, source_target_pairs={{0,0},{1,64},{2,128},{3,192},{4,256},{5,320},{6,384},{7,448},{8,8}... | collective-permute-start | bytes 393224 | tf_op jit(solution)/shard_map/ppermute | solution.py:193
  65.4 45.0 %collective-permute-start.5 = (bf16[8,32,256]{2,1,0:T(8,128)(2,1)S(1)}, bf16[8,32,256]{2,1,0:T(8,128)(2,1)S(1)}, u32[]{:S(2)}, u32[]{:S(2)}) collective-permute-start(bf16[8,32,256]{2,1,0:T(8,128)(2,1)S(1)} %get-tuple-element.46), channel_id=1, source_target_pairs={{0,80},{1,16},{2,208},{3,144},{4,336},{5,272},{6,464},{7,400},{8,8... | collective-permute-start | bytes 393224 | tf_op jit(solution)/shard_map/ppermute | solution.py:193
  70.1 40.2 %collective-permute-start.6 = (bf16[8,32,256]{2,1,0:T(8,128)(2,1)S(1)}, bf16[8,32,256]{2,1,0:T(8,128)(2,1)S(1)}, u32[]{:S(2)}, u32[]{:S(2)}) collective-permute-start(bf16[8,32,256]{2,1,0:T(8,128)(2,1)S(1)} %get-tuple-element.45), channel_id=1, source_target_pairs={{0,32},{1,96},{2,160},{3,224},{4,288},{5,352},{6,416},{7,480},{8,4... | collective-permute-start | bytes 393224 | tf_op jit(solution)/shard_map/ppermute | solution.py:193
  74.9 35.5 %collective-permute-start.7 = (bf16[8,32,256]{2,1,0:T(8,128)(2,1)S(1)}, bf16[8,32,256]{2,1,0:T(8,128)(2,1)S(1)}, u32[]{:S(2)}, u32[]{:S(2)}) collective-permute-start(bf16[8,32,256]{2,1,0:T(8,128)(2,1)S(1)} %get-tuple-element.44), channel_id=1, source_target_pairs={{0,112},{1,48},{2,240},{3,176},{4,368},{5,304},{6,496},{7,432},{8,... | collective-permute-start | bytes 393224 | tf_op jit(solution)/shard_map/ppermute | solution.py:193
  81.6 1.6 %copy-start.1 = (bf16[4,16,2,64,128]{4,3,2,1,0:T(8,128)(2,1)S(1)}, bf16[4,16,2,64,128]{4,3,2,1,0:T(8,128)(2,1)}, u32[]{:S(2)}) copy-start(bf16[4,16,2,64,128]{4,3,2,1,0:T(8,128)(2,1)} %system_ref) | copy-start | bytes 6291460
  113.7 13.8 %all-to-all-start.2 = ((f16[4,272,256]{2,1,0:T(8,128)(2,1)}), f16[4,272,256]{2,1,0:T(8,128)(2,1)S(1)}, u32[]{:S(2)}, u32[]{:S(2)}) async-start(f16[4,272,256]{2,1,0:T(8,128)(2,1)} %convert_element_type.14), calls=%async_computation.2 | async-start | bytes 1114112 | tf_op jit(solution)/shard_map/all_to_all | solution.py:208
  127.9 14.9 %collective-permute-start.8 = (f16[272,128]{1,0:T(8,128)(2,1)S(1)}, f16[272,128]{1,0:T(8,128)(2,1)S(1)}, u32[]{:S(2)}, u32[]{:S(2)}) collective-permute-start(f16[272,128]{1,0:T(8,128)(2,1)S(1)} %maximum_maximum_fusion), channel_id=1, source_target_pairs={{0,1},{1,0},{2,3},{3,2},{4,5},{5,4},{6,7},{7,6},{8,9},{9,8},{10,11... | collective-permute-start | bytes 208904 | tf_op jit(solution)/shard_map/ppermute | solution.py:216
